TPU v7x, 256 devices: a whole 4x4x8 slice. The times are simulated.
256 devices in a mesh: seq: 32 (over x, y, core), tp: 8 (over z).
Axes of the slice: x: 4, y: 4, z: 8, core: 2. Of those that a mesh axis runs over, the one named last changes fastest.
Arguments:
- x_in: bfloat16 [16384, 8192], P('seq', 'tp'), may hold values from -6 to 6
- b_in: bfloat16 [16384, 1024], P('seq', 'tp'), may hold values from -6 to 6
- c_in: bfloat16 [16384, 1024], P('seq', 'tp'), may hold values from -6 to 6
- z_in: bfloat16 [16384, 8192], P('seq', 'tp'), may hold values from -6 to 6
- step_size: float32 [16384, 128], P('seq', 'tp'), may hold values from 0 to 0.4
- log_decay: float32 [16384, 128], P('seq', 'tp'), may hold values from -0.7 to 0
- conv_x: float32 [4, 8192], P(None, 'tp'), may hold values from -3 to 3
- conv_b: float32 [4, 1024], P(None, 'tp'), may hold values from -3 to 3
- conv_c: float32 [4, 1024], P(None, 'tp'), may hold values from -3 to 3
- d_skip: float32 [128], P('tp'), may hold values from 0.5 to 2
- norm_gain: float32 [8192], P('tp'), may hold values from 0.1 to 1.9
- out_weight: bfloat16 [8192, 4096], P('tp'), may hold values from -127 to 127, as said below
- out_exponent: int32 [4096], replicated, may hold values from -14 to -12
- out_sign: int32 [4096], replicated, may hold values from -1 to 1, as said below
Outputs:
- layer_out: bfloat16 [16384, 4096], P(('seq', 'tp'))
Inputs may be any that keep to these rules, and one draw needn't show every extreme that they name: `out_weight`: every entry is an integer. `out_sign`: every entry is -1 or 1.
All inputs are finite; a program needn't handle non-finite values.
Results may differ from a plain program's by a relative error of at most 0.0053.
Values may be sent and summed in bfloat16 or wider, within the bound.
No kernel may reach another device: no remote copies, remote signals or barrier semaphores. Data moves between devices by JAX's collectives and lax.ppermute only.
A program may use at most 128 MiB of HBM per device.

v0:
```python
import math

import jax
import jax.numpy as jnp
from jax import lax
from jax.sharding import PartitionSpec as P

HEAD_DIM = 64
STATE = 128
GROUPS = 8
CONV = 4
SPAN = 256
HAD_BLOCK = 128
INNER = 8192


HIGHEST = lax.Precision.HIGHEST


def shifted(value, axis, steps):
    count = lax.axis_size(axis)
    initial, last = (max(0, -steps), min(count, count - steps))
    return lax.ppermute(value, axis, [(source, source + steps) for source in range(initial, last)])


def entering_2(part, axis, combine, identity):
    place = lax.axis_index(axis)
    gathered = jax.tree.map(lambda a: lax.all_gather(a, axis), part)
    state = jax.tree.map(lambda a, e: jnp.zeros_like(a) + jnp.asarray(e, a.dtype), part, identity)

    def one(turn, state):
        return combine(
            state, jax.tree.map(lambda a: lax.dynamic_index_in_dim(a, turn, 0, False), gathered)
        )

    return lax.fori_loop(0, place, one, state)


def sylvester(order):
    index = jnp.arange(order)
    matrix = jnp.ones((order, order), jnp.float32)
    bit = 1
    while bit < order:
        upper = index // bit % 2
        matrix = matrix * (1.0 - 2.0 * (upper[:, None] * upper[None, :]).astype(jnp.float32))
        bit = bit * 2
    return matrix


def causal_conv(values, kernel, rim):
    padded = jnp.concatenate([rim, values], 0).astype(jnp.float32)
    length = values.shape[0]
    total = kernel[0][None, :] * padded[0:length]
    for offset in range(1, kernel.shape[0]):
        total = total + kernel[offset][None, :] * padded[offset : offset + length]
    return jax.nn.silu(total).astype(jnp.bfloat16)


def span_local(inputs, keys_b, reads_c, steps, decays, skip, start_state):
    length, heads, width = inputs.shape
    groups = keys_b.shape[1]
    per_group = heads // groups
    blocks_count = length // SPAN
    order = jnp.arange(SPAN)
    lower = (order[:, None] >= order[None, :])[:, :, None]

    def advance(state, block):
        values, enter, leave, step_block, decay_block = block
        running = jnp.cumsum(decay_block, axis=0)
        spread = running[:, None, :] - running[None, :, :]
        mixing = jnp.where(lower, jnp.exp(jnp.where(lower, spread, 0.0)), 0.0)
        scores = jnp.einsum("tgn,sgn->tsg", leave, enter, preferred_element_type=jnp.float32)
        scores = jnp.repeat(scores, per_group, axis=2)
        weights = (mixing * scores * step_block[None, :, :]).astype(jnp.bfloat16)
        inside = jnp.einsum("tsh,shp->thp", weights, values, preferred_element_type=jnp.float32)
        enter_heads = jnp.repeat(enter, per_group, axis=1)
        output = inside + skip[None, :, None] * values.astype(jnp.float32)
        toward_end = jnp.exp(running[-1][None, :] - running) * step_block
        feed = (values.astype(jnp.float32) * toward_end[:, :, None]).astype(jnp.bfloat16)
        new_state = jnp.exp(running[-1])[:, None, None] * state + jnp.einsum(
            "shp,shn->hpn", feed, enter_heads, preferred_element_type=jnp.float32
        )
        return (new_state, (output, state))

    blocks = tuple(
        (
            item.reshape((blocks_count, SPAN) + item.shape[1:])
            for item in (inputs, keys_b, reads_c, steps, decays)
        )
    )
    end_state, (outputs, starts) = lax.scan(advance, start_state, blocks)
    return (outputs, starts, end_state)


def chain_combine(earlier, later):
    return (earlier[0] * later[0], later[0][:, None, None] * earlier[1] + later[1])


def local(
    x_in,
    b_in,
    c_in,
    z_in,
    step_size,
    log_decay,
    conv_x,
    conv_b,
    conv_c,
    d_skip,
    norm_gain,
    out_weight,
    out_exponent,
    out_sign,
):
    length = x_in.shape[0]
    inner_local = x_in.shape[1]
    heads_local = d_skip.shape[0]
    band = b_in.shape[1]
    groups_local = band // STATE
    per_group = heads_local // groups_local
    blocks_count = length // SPAN
    joined = jnp.concatenate([x_in, b_in, c_in], 1)
    kernel = jnp.concatenate([conv_x, conv_b, conv_c], 1)
    rim = shifted(joined[length - (CONV - 1) :], "seq", 1)
    mixed = causal_conv(joined, kernel, rim)
    inputs = mixed[:, :inner_local].reshape(length, heads_local, HEAD_DIM)
    keys_b = mixed[:, inner_local : inner_local + band].reshape(length, groups_local, STATE)
    reads_c = mixed[:, inner_local + band :].reshape(length, groups_local, STATE)
    empty_state = jnp.zeros((heads_local, HEAD_DIM, STATE), jnp.float32)
    local_out, starts, end_state = span_local(
        inputs, keys_b, reads_c, step_size, log_decay, d_skip, empty_state
    )
    running = jnp.cumsum(log_decay.reshape(blocks_count, SPAN, heads_local), axis=1)
    block_sums = running[:, -1]
    before = jnp.cumsum(block_sums, axis=0) - block_sums
    total = jnp.exp(jnp.sum(block_sums, axis=0))
    identity = (jnp.ones((heads_local,), jnp.float32), empty_state)
    earlier_decay, incoming = entering_2((total, end_state), "seq", chain_combine, identity)
    entering = starts + jnp.exp(before)[:, :, None, None] * incoming[None]
    start_read = entering.astype(jnp.bfloat16)
    reads_heads = jnp.repeat(
        reads_c.reshape(blocks_count, SPAN, groups_local, STATE), per_group, axis=2
    )
    carried = jnp.exp(running)[:, :, :, None] * jnp.einsum(
        "kthn,khpn->kthp", reads_heads, start_read, preferred_element_type=jnp.float32
    )
    flat = (local_out + carried).reshape(length, inner_local)
    gated = flat * jax.nn.silu(z_in.astype(jnp.float32))
    grouped = gated.reshape(length, -1, INNER // GROUPS)
    meansq = jnp.mean(grouped * grouped, axis=2, keepdims=True)
    normed = (
        (grouped * lax.rsqrt(meansq + 1e-05)).reshape(length, inner_local) * norm_gain[None, :]
    ).astype(jnp.bfloat16)
    share = length // lax.axis_size("tp")
    summed = lax.psum_scatter(
        jnp.dot(normed, out_weight, preferred_element_type=jnp.float32),
        "tp",
        scatter_dimension=0,
        tiled=True,
    )
    column_scale = jnp.exp2(out_exponent.astype(jnp.float32)) * out_sign.astype(jnp.float32)
    table = sylvester(HAD_BLOCK) / jnp.float32(math.sqrt(HAD_BLOCK))
    scaled = (summed * column_scale[None, :]).reshape(share, -1, HAD_BLOCK)
    rotated = jnp.einsum("rbk,kj->rbj", scaled, table, precision=HIGHEST)
    return rotated.reshape(share, -1).astype(jnp.bfloat16)


def solution(mesh):
    return jax.shard_map(
        local,
        mesh=mesh,
        in_specs=(
            P("seq", "tp"),
            P("seq", "tp"),
            P("seq", "tp"),
            P("seq", "tp"),
            P("seq", "tp"),
            P("seq", "tp"),
            P(None, "tp"),
            P(None, "tp"),
            P(None, "tp"),
            P("tp"),
            P("tp"),
            P("tp", None),
            P(),
            P(),
        ),
        out_specs=P(("seq", "tp"), None),
        check_vma=False,
    )
```

profile of v0, /device:TPU:2, one launch (start us, length us, event | category | flops | bytes accessed | tf_op | source)
XLA Modules:
  0.0 266.5 jit_solution(5695789485072662048)
XLA Ops:
  6.6 1.4 constant_dynamic-update-slice_fusion.5
  8.2 1.9 collective-permute-start
  10.3 4.9 %collective-permute-done = bf16[3,1280]{1,0:T(4,128)(2,1)S(1)} collective-permute-done((bf16[3,1280]{1,0:T(4,128)(2,1)S(1)}, bf16[3,1280]{1,0:T(4,128)(2,1)S(1)}, u32[]{:S(2)}, u32[]{:S(2)}) %collective-permute-start) | collective-permute-done | bytes 7712 | tf_op jit(solution)/shard_map/ppermute | solution.py:23
  15.5 1.6 multiply_convert_fusion.10
  17.3 2.4 reshape.439
  19.7 2.8 %copy.53 = bf16[2,256,16,64]{1,3,2,0:T(8,128)(2,1)S(1)} copy(bf16[2,256,16,64]{3,2,1,0:T(8,128)(2,1)} %reshape.439) | data formatting | bytes 2097152
  22.5 8.9 %while.29 = (s32[]{:T(128)}, f32[16,64,128]{2,1,0:T(8,128)S(1)}, f32[2,256,16,64]{1,3,2,0:T(8,128)}, f32[2,16,64,128]{3,2,1,0:T(8,128)S(1)}, f32[2,256,16]{1,0,2...) while((s32[]{:T(128)}, f32[16,64,128]{2,1,0:T(8,128)S(1)}, ...), condition=%wide.region_3.4_spmd.clone.clone, body=%wide.region_0.3_spmd.clone.clone.sunk | while | flops 227094576 | bytes 6541864 | solution.py:91
  24.5 2.5 fusion.120
  28.9 2.5 fusion.120
  35.2 53.8 %all-reduce = f32[512]{0:T(512)S(1)} all-reduce(f32[512]{0:T(512)S(1)} %exponential_dynamic-update-slice_fusion), channel_id=2, replica_groups=mesh['seq'=32,'tp'=8] {'seq'}, use_global_device_ids=true, to_apply=%add | all-reduce | flops 512 | bytes 4096
  89.1 1.5 copy.60
  90.8 20.2 %all-gather.4.cloned.1.call-done = f32[512,64,128]{2,1,0:T(8,128)} async-done(((f32[16,64,128]{2,1,0:T(8,128)}), f32[512,64,128]{2,1,0:T(8,128)}) %all-gather.4.cloned.1.call-update) | async-done | bytes 16777232 | tf_op jit(solution)/shard_map/all_gather | solution.py:28
  111.0 10.0 %while.28 = (s32[]{:T(128)}, f32[16,64,128]{2,1,0:T(8,128)S(1)}, s32[]{:T(128)}, f32[32,16]{1,0:T(8,128)S(1)}, f32[32,16,64,128]{3,2,1,0:T(8,128)}, /*index=5*/s32[]{:T(128)}, s32[]{:T(128)}, s32[]{:T(128)}) while((s32[]{:T(128)}, f32[16,64,128]{2,1,0:T(8,128)S(1)}, s32[]{:T(128)}, f32[32,16]{1,0:T(8,128)S(1)}, ...), condition=%wide.region_9.10_spmd, body=%wide.region_8.9_spmd.sunk | while | flops 262149 | bytes 1573191 | solution.py:36
  111.1 1.2 bitcast_add_fusion.2
  112.3 1.2 bitcast_add_fusion.2
  113.6 1.2 bitcast_add_fusion.2
  114.8 1.2 bitcast_add_fusion.2
  116.0 1.2 bitcast_add_fusion.2
  117.2 1.2 bitcast_add_fusion.2
  121.1 2.6 fusion.35
  123.8 1.6 copy.59
  126.4 7.4 %fusion.36 = f32[512,4096]{1,0:T(8,128)} fusion(bf16[1024,4096]{1,0:T(8,128)(2,1)S(1)} %bitcast.169, f32[1024]{0:T(1024)S(1)} %copy-done.10, f32[512]{0:T(512)S(1)} %add_rsqrt_fusion, f32[512,1024]{0,1:T(8,128)S(1)} %bitcast.158, bf16[512,1024]{0,1:T(8,128)(2,1)S(1)} %copy.60), kind=kOutput, calls=%fused_computation.66 | convolution fusion | flops 4299685888 | bytes 19929088 | tf_op jit(solution)/shard_map/dot_general | solution.py:156
  134.6 121.4 %reduce-scatter.2.cloned.1.call-done = f32[64,4096]{1,0:T(8,128)} async-done(((f32[512,4096]{1,0:T(8,128)}), f32[64,4096]{1,0:T(8,128)}) %reduce-scatter.2.cloned.1.call-update) | async-done | bytes 1048592 | tf_op jit(solution)/shard_map/reduce_scatter | solution.py:155
  256.0 1.3 multiply_bitcast_fusion
  (121 shorter events, 14.4 us)
Async XLA Ops:
  6.5 1.5 copy-start.1
  6.5 1.6 copy-start.2
  6.5 3.5 %copy-start.7 = (f32[4,1024]{1,0:T(4,128)S(1)}, f32[4,1024]{1,0:T(4,128)}, u32[]{:S(2)}) copy-start(f32[4,1024]{1,0:T(4,128)} %param.24) | copy-start | bytes 49156
  6.5 3.6 %copy-start.8 = (f32[4,128]{1,0:T(4,128)S(1)}, f32[4,128]{1,0:T(4,128)}, u32[]{:S(2)}) copy-start(f32[4,128]{1,0:T(4,128)} %param.25) | copy-start | bytes 6148
  6.5 3.6 %copy-start.9 = (f32[4,128]{1,0:T(4,128)S(1)}, f32[4,128]{1,0:T(4,128)}, u32[]{:S(2)}) copy-start(f32[4,128]{1,0:T(4,128)} %param.26) | copy-start | bytes 6148
  6.5 3.7 %copy-start.3 = (f32[512,16]{0,1:T(8,128)S(1)}, f32[512,16]{0,1:T(8,128)}, u32[]{:S(2)}) copy-start(f32[512,16]{0,1:T(8,128)} %param.23) | copy-start | bytes 98308
  6.6 3.7 %copy-start.4 = (f32[512,16]{0,1:T(8,128)S(1)}, f32[512,16]{0,1:T(8,128)}, u32[]{:S(2)}) copy-start(f32[512,16]{0,1:T(8,128)} %param.22) | copy-start | bytes 98308
  6.6 104.4 %all-gather.4.cloned.1.call-start = ((), (), s32[]{:S(2)}) async-start(), calls=%async_computation.2 | async-start | bytes 17301504 | tf_op jit(solution)/shard_map/all_gather | solution.py:28
  8.2 7.1 %collective-permute-start = (bf16[3,1280]{1,0:T(4,128)(2,1)S(1)}, bf16[3,1280]{1,0:T(4,128)(2,1)S(1)}, u32[]{:S(2)}, u32[]{:S(2)}) collective-permute-start(bf16[3,1280]{1,0:T(4,128)(2,1)S(1)} %slice.79), channel_id=1, source_target_pairs={{0,8},{8,16},{16,24},{24,32},{32,40},{40,48},{48,56},{56,64},{64,7... | collective-permute-start | bytes 23048 | tf_op jit(solution)/shard_map/ppermute | solution.py:23
  19.6 2.8 %copy-start.11 = (f32[16]{0:T(128)S(1)}, f32[16]{0:T(128)}, u32[]{:S(2)}) copy-start(f32[16]{0:T(128)} %param.27) | copy-start | bytes 196
  22.5 11.3 %copy-start.12 = (u32[256]{0:T(256)S(1)}, u32[256]{0:T(256)}, u32[]{:S(2)}) copy-start(u32[256]{0:T(256)} %constant.236) | copy-start | bytes 3076
  31.4 0.8 copy-start
  32.2 223.7 %reduce-scatter.2.cloned.1.call-start = ((), (), s32[]{:S(2)}) async-start(), calls=%async_computation.1 | async-start | bytes 9437184 | tf_op jit(solution)/shard_map/reduce_scatter | solution.py:155
  121.1 5.2 %slice-start = ((s8[8388608]{0:T(1024)(128)(4,1)}), s8[4194304]{0:T(1024)(128)(4,1)S(1)}, s32[]{:S(2)}) async-start(s8[8388608]{0:T(1024)(128)(4,1)} %bitcast.168), calls=%async_computation.3 | async-start | bytes 8388608
  123.7 2.5 slice-start.1
  125.6 0.8 copy-start.10
  133.8 0.7 copy-start.5
  133.8 0.7 copy-start.6
Sparse Core Ops, SparseCore 0:
  32.4 78.6 all-gather.3
  134.0 121.9 reduce-scatter.1
where the time goes:
time: 269 us; the launch traced here: 266 us
  waiting for transfers between devices  147 us (55%)
  blocking collectives  53.8 us (20%)
  matrix products  17.2 us (6%)
  other arithmetic  16.7 us (6%)
  local copies, waits for them, and re-layouts  15.1 us (6%)
  between operations  14.4 us (5%)
    reduce_scatter x1, waiting for transfers between devices, local(): lax.psum_scatter(jnp.dot(normed, out_weight, preferred_element_type=jnp.f...  121 us
    unnamed x1, blocking collectives  53.8 us
    all_gather x1, waiting for transfers between devices, entering_2(): gathered = jax.tree.map(lambda a: lax.all_gather(a, axis), part)  20.2 us
    add x8, other arithmetic, chain_combine(): later[0][:, None, None] * earlier[1] + later[1]  9.5 us
    unnamed x42, local copies, waits for them, and re-layouts  9.35 us
    dot_general x1, matrix products, local(): jnp.dot(normed, out_weight, preferred_element_type=jnp.float32)  7.44 us
  transfers between devices with their start and end apart: 3, of which 3 were waited for; matrix products, arithmetic and copies ran while one was open for 2% of the time, Pallas kernels for 0%

commit v1 on v0

v1 whole, which is shorter than its diff:
```python
import math

import jax
import jax.numpy as jnp
from jax import lax
from jax.experimental import pallas as pl
from jax.experimental.pallas import tpu as pltpu
from jax.sharding import PartitionSpec as P

HEAD_DIM = 64
STATE = 128
SPAN = 256
HAD_BLOCK = 128
HEADS_LOCAL = 16
TOK = 512
CH = 1024
PARTS = 32
PIECE = 32
PAY = 48
TILE = 256
MIB = 1024 * 1024

F32 = jnp.float32
BF16 = jnp.bfloat16
HIGHEST = lax.Precision.HIGHEST


def dot(a, b, dims=((1,), (0,)), precision=None):
    return lax.dot_general(a, b, (dims, ((), ())), precision=precision, preferred_element_type=F32)


def conv_silu(pad, rim, values, taps):
    width = values.shape[1]
    pad[0:8, 0:width] = rim[8:16].astype(F32)
    pad[8 : TOK + 8, 0:width] = values.astype(F32)
    total = taps[0:1] * pad[5 : 5 + TOK, 0:width]
    for k in range(1, 4):
        total = total + taps[k : k + 1] * pad[5 + k : 5 + k + TOK, 0:width]
    return jax.nn.silu(total).astype(BF16)


def head_rows(first, channels):
    head = lax.broadcasted_iota(jnp.int32, (HEADS_LOCAL, channels), 0)
    channel = lax.broadcasted_iota(jnp.int32, (HEADS_LOCAL, channels), 1)
    return (channel // HEAD_DIM + first == head).astype(F32)


def head_columns(first, channels, row):
    channel = lax.broadcasted_iota(jnp.int32, (channels, HEADS_LOCAL), 0)
    head = lax.broadcasted_iota(jnp.int32, (channels, HEADS_LOCAL), 1)
    return jnp.sum(jnp.where(channel // HEAD_DIM + first == head, row, 0.0), axis=1, keepdims=True)


def scan_in(rim_x, rim_b, rim_c, x, b, c, step, decay, tap_x, tap_b, tap_c,
            xs_o, bs_o, cs_o, run_o, pay_o, first_o, pad, toward):
    tile = pl.program_id(0)

    @pl.when(tile == 0)
    def _():
        bs_o[...] = conv_silu(pad, rim_b[...], b[...], tap_b[...])
        cs_o[...] = conv_silu(pad, rim_c[...], c[...], tap_c[...])
        later = lax.broadcasted_iota(jnp.int32, (SPAN, SPAN), 0)
        earlier = lax.broadcasted_iota(jnp.int32, (SPAN, SPAN), 1)
        lower = (later >= earlier).astype(F32)
        for k in range(2):
            rows = slice(k * SPAN, (k + 1) * SPAN)
            running = dot(lower, decay[rows], precision=HIGHEST)
            run_o[rows] = running
            toward[rows] = jnp.exp(running[SPAN - 1 :] - running) * step[rows]

    xs = conv_silu(pad, rim_x[...], x[...], tap_x[...])
    xs_o[...] = xs
    first = tile * (TILE // HEAD_DIM)
    wide = dot(toward[...], head_rows(first, TILE), precision=HIGHEST)
    feed = (xs.astype(F32) * wide).astype(BF16)
    one = dot(feed[:SPAN], bs_o[:SPAN], ((0,), (0,)))
    two = dot(feed[SPAN:], bs_o[SPAN:], ((0,), (0,)))
    first_o[...] = one
    end0 = run_o[SPAN - 1 : SPAN]
    end1 = run_o[TOK - 1 : TOK]
    state = jnp.exp(head_columns(first, TILE, end1)) * one + two
    pay_o[:, 0:PIECE, :] = state.astype(BF16).reshape(TILE // PIECE, PIECE, STATE)
    total = jnp.broadcast_to(head_columns(first, TILE, end0 + end1), (TILE, STATE))
    high = total.astype(BF16)
    rest = total - high.astype(F32)
    middle = rest.astype(BF16)
    low = (rest - middle.astype(F32)).astype(BF16)
    row = lax.broadcasted_iota(jnp.int32, (TILE, STATE), 0) % PIECE
    parts = jnp.where(row == 0, high.astype(F32), jnp.where(row == 1, middle.astype(F32), low.astype(F32)))
    pay_o[:, PIECE:PAY, :] = parts.astype(BF16).reshape(TILE // PIECE, PIECE, STATE)[:, 0 : PAY - PIECE, :]


def prefix(got, out):
    state = jnp.zeros((PIECE, STATE), F32)
    for k in range(PARTS):
        out[k] = state.astype(BF16)
        if k < PARTS - 1:
            piece = got[k].astype(F32)
            total = piece[PIECE : PIECE + 1] + piece[PIECE + 1 : PIECE + 2] + piece[PIECE + 2 : PIECE + 3]
            state = jnp.exp(total) * state + piece[:PIECE]


def inside(xs, bs, cs, run, decay, step, skip, out, scores, run_t, step_t):
    tile = pl.program_id(0)

    @pl.when(tile == 0)
    def _():
        later = lax.broadcasted_iota(jnp.int32, (SPAN, SPAN), 0)
        earlier = lax.broadcasted_iota(jnp.int32, (SPAN, SPAN), 1)
        upper = (later <= earlier).astype(F32)
        same = (later == earlier).astype(F32)
        for k in range(2):
            rows = slice(k * SPAN, (k + 1) * SPAN)
            raw = dot(cs[rows], bs[rows], ((1,), (1,)))
            scores[rows] = jnp.where(later >= earlier, raw, 0.0)
            run_t[:, rows] = dot(decay[rows], upper, ((0,), (0,)), precision=HIGHEST)
            step_t[:, rows] = dot(step[rows], same, ((0,), (0,)), precision=HIGHEST)

    per_tile = TILE // HEAD_DIM
    head_lane = lax.broadcasted_iota(jnp.int32, (HEADS_LOCAL, 1), 0)
    lane_head = lax.broadcasted_iota(jnp.int32, (TOK, HEADS_LOCAL), 1)
    for q in range(per_tile):
        head = tile * per_tile + q
        column = jnp.sum(jnp.where(lane_head == head, run[...], 0.0), axis=1, keepdims=True)
        r_row = jnp.sum(jnp.where(head_lane == head, run_t[...], 0.0), axis=0, keepdims=True)
        s_row = jnp.sum(jnp.where(head_lane == head, step_t[...], 0.0), axis=0, keepdims=True)
        lanes = slice(q * HEAD_DIM, (q + 1) * HEAD_DIM)
        for k in range(2):
            rows = slice(k * SPAN, (k + 1) * SPAN)
            spread = jnp.minimum(column[rows] - r_row[:, rows], 0.0)
            weights = (jnp.exp(spread) * scores[rows] * s_row[:, rows]).astype(BF16)
            out[rows, lanes] = dot(weights, xs[rows, lanes])
    out[...] = out[...] + skip[...] * xs[...].astype(F32)


def norm_project(y, cs, run, first, incoming, z, gain, weight, normed_o, part_o):
    @pl.when(pl.program_id(0) == 0)
    def _():
        end0 = run[SPAN - 1 : SPAN]
        expand = head_rows(0, CH)
        for k in range(2):
            rows = slice(k * SPAN, (k + 1) * SPAN)
            if k == 0:
                start = incoming[...]
            else:
                start = (jnp.exp(head_columns(0, CH, end0)) * incoming[...].astype(F32) + first[...]).astype(BF16)
            grown = dot(jnp.exp(run[rows]), expand, precision=HIGHEST)
            carried = grown * dot(cs[rows], start, ((1,), (1,)))
            gated = (y[rows] + carried) * jax.nn.silu(z[rows].astype(F32))
            meansq = jnp.sum(gated * gated, axis=1, keepdims=True) * (1.0 / CH)
            normed_o[rows] = (gated * lax.rsqrt(meansq + 1e-05) * gain[...]).astype(BF16)

    part_o[...] = dot(normed_o[...], weight[...])


def project(normed, weight, part_o):
    part_o[...] = dot(normed[...], weight[...])


def finish(own, up, down, scale, out):
    total = (own[...] + up[...].astype(F32) + down[...].astype(F32)) * scale[...]
    high = total.astype(BF16)
    rest = total - high.astype(F32)
    middle = rest.astype(BF16)
    low = (rest - middle.astype(F32)).astype(BF16)
    row = lax.broadcasted_iota(jnp.int32, (HAD_BLOCK, HAD_BLOCK), 0)
    column = lax.broadcasted_iota(jnp.int32, (HAD_BLOCK, HAD_BLOCK), 1)
    ones = row & column
    parity = jnp.zeros_like(ones)
    for bit in range(7):
        parity = parity ^ ((ones >> bit) & 1)
    table = (1 - 2 * parity).astype(F32).astype(BF16)
    for k in range(total.shape[1] // HAD_BLOCK):
        lanes = slice(k * HAD_BLOCK, (k + 1) * HAD_BLOCK)
        rotated = dot(high[:, lanes], table) + dot(middle[:, lanes], table) + dot(low[:, lanes], table)
        out[:, lanes] = (rotated * (1.0 / math.sqrt(HAD_BLOCK))).astype(BF16)


def whole(shape):
    return pl.BlockSpec(shape, lambda i: (0,) * len(shape))


def tiled(shape, axis):
    return pl.BlockSpec(shape, lambda i: tuple(i if d == axis else 0 for d in range(len(shape))))


def params(mib):
    return pltpu.CompilerParams(vmem_limit_bytes=mib * MIB)


def ring(value, step):
    count = lax.axis_size("tp")
    return lax.ppermute(value, "tp", [(k, (k + step) % count) for k in range(count)])


def local(x_in, b_in, c_in, z_in, step_size, log_decay, conv_x, conv_b, conv_c, d_skip, norm_gain,
          out_weight, out_exponent, out_sign):
    seq = lax.axis_size("seq")
    tail = jnp.concatenate([x_in[TOK - 16 :], b_in[TOK - 16 :], c_in[TOK - 16 :]], 1)
    rim = lax.ppermute(tail, "seq", [(k, k + 1) for k in range(seq - 1)])
    tiles = CH // TILE
    xs, bs, cs, run, pay, first = pl.pallas_call(
        scan_in,
        grid=(tiles,),
        in_specs=[
            tiled((16, TILE), 1),
            pl.BlockSpec((16, STATE), lambda i: (0, CH // STATE)),
            pl.BlockSpec((16, STATE), lambda i: (0, CH // STATE + 1)),
            tiled((TOK, TILE), 1),
            whole((TOK, STATE)),
            whole((TOK, STATE)),
            whole((TOK, HEADS_LOCAL)),
            whole((TOK, HEADS_LOCAL)),
            tiled((4, TILE), 1),
            whole((4, STATE)),
            whole((4, STATE)),
        ],
        out_specs=[
            tiled((TOK, TILE), 1),
            whole((TOK, STATE)),
            whole((TOK, STATE)),
            whole((TOK, HEADS_LOCAL)),
            tiled((TILE // PIECE, PAY, STATE), 0),
            tiled((TILE, STATE), 0),
        ],
        out_shape=[
            jax.ShapeDtypeStruct((TOK, CH), BF16),
            jax.ShapeDtypeStruct((TOK, STATE), BF16),
            jax.ShapeDtypeStruct((TOK, STATE), BF16),
            jax.ShapeDtypeStruct((TOK, HEADS_LOCAL), F32),
            jax.ShapeDtypeStruct((PARTS, PAY, STATE), BF16),
            jax.ShapeDtypeStruct((CH, STATE), F32),
        ],
        scratch_shapes=[pltpu.VMEM((TOK + 8, TILE), F32), pltpu.VMEM((TOK, HEADS_LOCAL), F32)],
        compiler_params=params(32),
        cost_estimate=pl.CostEstimate(flops=10**9, bytes_accessed=4 * 10**6, transcendentals=10**6),
        name="scan_in",
    )(rim, rim, rim, x_in, b_in, c_in, step_size, log_decay, conv_x, conv_b, conv_c)

    got = lax.all_to_all(pay, "seq", 0, 0, tiled=True)
    y = pl.pallas_call(
        inside,
        grid=(tiles,),
        in_specs=[
            tiled((TOK, TILE), 1),
            whole((TOK, STATE)),
            whole((TOK, STATE)),
            whole((TOK, HEADS_LOCAL)),
            whole((TOK, HEADS_LOCAL)),
            whole((TOK, HEADS_LOCAL)),
            tiled((1, TILE), 1),
        ],
        out_specs=tiled((TOK, TILE), 1),
        out_shape=jax.ShapeDtypeStruct((TOK, CH), F32),
        scratch_shapes=[
            pltpu.VMEM((TOK, SPAN), F32),
            pltpu.VMEM((HEADS_LOCAL, TOK), F32),
            pltpu.VMEM((HEADS_LOCAL, TOK), F32),
        ],
        compiler_params=params(32),
        cost_estimate=pl.CostEstimate(flops=4 * 10**9, bytes_accessed=6 * 10**6, transcendentals=2 * 10**6),
        name="inside",
    )(xs, bs, cs, run, log_decay, step_size, jnp.repeat(d_skip, HEAD_DIM)[None, :])

    before = pl.pallas_call(
        prefix,
        out_shape=jax.ShapeDtypeStruct((PARTS, PIECE, STATE), BF16),
        name="prefix",
    )(got)
    incoming = lax.all_to_all(before, "seq", 0, 0, tiled=True).reshape(CH, STATE)

    model = out_weight.shape[1]
    half = model // 2
    step_cols = 512
    normed, part_a = pl.pallas_call(
        norm_project,
        grid=(half // step_cols,),
        in_specs=[
            whole((TOK, CH)),
            whole((TOK, STATE)),
            whole((TOK, HEADS_LOCAL)),
            whole((CH, STATE)),
            whole((CH, STATE)),
            whole((TOK, CH)),
            whole((1, CH)),
            tiled((CH, step_cols), 1),
        ],
        out_specs=[whole((TOK, CH)), tiled((TOK, step_cols), 1)],
        out_shape=[jax.ShapeDtypeStruct((TOK, CH), BF16), jax.ShapeDtypeStruct((TOK, half), F32)],
        compiler_params=params(40),
        name="norm_project",
    )(y, cs, run, first, incoming, z_in, norm_gain[None, :], out_weight)
    part_b = pl.pallas_call(
        project,
        grid=(half // step_cols,),
        in_specs=[
            whole((TOK, CH)),
            pl.BlockSpec((CH, step_cols), lambda i: (0, i + half // step_cols)),
        ],
        out_specs=tiled((TOK, step_cols), 1),
        out_shape=jax.ShapeDtypeStruct((TOK, half), F32),
        compiler_params=params(32),
        cost_estimate=pl.CostEstimate(flops=2 * 10**9, bytes_accessed=8 * 10**6, transcendentals=0),
        name="project",
    )(normed, out_weight)

    place = lax.axis_index("tp")
    count = lax.axis_size("tp")
    share = TOK // count
    scale = jnp.exp2(out_exponent.astype(F32)) * out_sign.astype(F32)
    results = []
    for group, part in enumerate((part_a, part_b)):

        def mine(distance, part=part):
            row = lax.rem(place + distance + count, count) * share
            return lax.dynamic_slice_in_dim(part, row, share, 0)

        ends = []
        up = count // 2 if group == 0 else count // 2 - 1
        for sign, hops in ((1, up), (-1, count - 1 - up)):
            value = mine(sign * hops).astype(BF16)
            for k in range(hops - 1, -1, -1):
                value = ring(value, sign)
                if k > 0:
                    value = (value.astype(F32) + mine(sign * k)).astype(BF16)
            ends.append(value)
        results.append(
            pl.pallas_call(
                finish,
                out_shape=jax.ShapeDtypeStruct((share, half), BF16),
                name="finish",
            )(mine(0), ends[0], ends[1], scale[None, group * half : (group + 1) * half])
        )
    return jnp.concatenate(results, 1)


def solution(mesh):
    return jax.shard_map(
        local,
        mesh=mesh,
        in_specs=(
            P("seq", "tp"),
            P("seq", "tp"),
            P("seq", "tp"),
            P("seq", "tp"),
            P("seq", "tp"),
            P("seq", "tp"),
            P(None, "tp"),
            P(None, "tp"),
            P(None, "tp"),
            P("tp"),
            P("tp"),
            P("tp", None),
            P(),
            P(),
        ),
        out_specs=P(("seq", "tp"), None),
        check_vma=False,
    )
```

time: 269 us -> 128 us (0.48)
  waiting for transfers between devices: 147 us -> 30.5 us
  blocking collectives: 53.8 us -> 0 us
  starting transfers between devices: 2 us -> 35.8 us
  Pallas kernels: 0 us -> 29.9 us
  matrix products: 17.2 us -> 0 us
  between operations: 14.4 us -> 0.32 us
  other arithmetic: 16.7 us -> 4.12 us
  local copies, waits for them, and re-layouts: 15.1 us -> 25.8 us
    reduce_scatter x1 -> x0, waiting for transfers between devices: 121 us -> none  [local(): lax.psum_scatter(jnp.dot(normed, out_weight, preferred_element_type=jnp.f...]
    unnamed x1 -> x0, blocking collectives: 53.8 us -> none
    pallas_call x0 -> x7, Pallas kernels: none -> 29.9 us  [the longest x1 7.42 us: local(): pl.pallas_call(norm_project, grid=(half // step_cols,), in_specs=[whole((...]
    ppermute x1 -> x15, starting transfers between devices: 1.92 us -> 25.1 us  [the longest x14 23.2 us: ring(): lax.ppermute(value, 'tp', [(k, (k + step) % count) for k in range(count)])]
    all_gather x1 -> x0, waiting for transfers between devices: 20.2 us -> none  [entering_2(): gathered = jax.tree.map(lambda a: lax.all_gather(a, axis), part)]
    dot_general x9 -> x0, matrix products: 17.2 us -> none  [the longest x1 7.44 us: local(): jnp.dot(normed, out_weight, preferred_element_type=jnp.float32)]
    ppermute x1 -> x15, waiting for transfers between devices: 4.93 us -> 22 us  [the longest x14 18.3 us: ring(): lax.ppermute(value, 'tp', [(k, (k + step) % count) for k in range(count)])]
    unnamed x42 -> x62, local copies, waits for them, and re-layouts: 9.35 us -> 22.8 us
  transfers between devices with their start and end apart: 3 -> 17, of which waited for: 3 -> 8; matrix products, arithmetic and copies ran while one was open for 2% -> 4% of each run, Pallas kernels for 0% -> 9%
where the time goes in v1:
time: 128 us; the launch traced here: 126 us
  starting transfers between devices  35.8 us (28%)
  waiting for transfers between devices  30.5 us (24%)
  Pallas kernels  29.9 us (23%)
  local copies, waits for them, and re-layouts  25.8 us (20%)
  other arithmetic  4.12 us (3%)
    ppermute x14, starting transfers between devices, ring(): lax.ppermute(value, 'tp', [(k, (k + step) % count) for k in range(count)])  23.2 us
    unnamed x62, local copies, waits for them, and re-layouts  22.8 us
    ppermute x14, waiting for transfers between devices, ring(): lax.ppermute(value, 'tp', [(k, (k + step) % count) for k in range(count)])  18.3 us
    all_to_all x1, waiting for transfers between devices, local(): got = lax.all_to_all(pay, 'seq', 0, 0, tiled=True)  8.51 us
    pallas_call x1, Pallas kernels, local(): pl.pallas_call(norm_project, grid=(half // step_cols,), in_specs=[whole((...  7.42 us
    pallas_call x1, Pallas kernels, local(): pl.pallas_call(scan_in, grid=(tiles,), in_specs=[tiled((16, TILE), 1), pl...  6.97 us
    all_to_all x1, starting transfers between devices, local(): got = lax.all_to_all(pay, 'seq', 0, 0, tiled=True)  5.5 us
    pallas_call x1, Pallas kernels, local(): pl.pallas_call(inside, grid=(tiles,), in_specs=[tiled((TOK, TILE), 1), wh...  5.34 us
  transfers between devices with their start and end apart: 17, of which 8 were waited for; matrix products, arithmetic and copies ran while one was open for 4% of the time, Pallas kernels for 9%

profile of v1, /device:TPU:2, one launch (start us, length us, event | category | flops | bytes accessed | tf_op | source)
XLA Modules:
  0.0 126.4 jit_solution(15481327604231764144)
XLA Ops:
  2.2 1.9 %collective-permute-start = (bf16[16,1280]{1,0:T(8,128)(2,1)S(1)}, bf16[16,1280]{1,0:T(8,128)(2,1)S(1)}, u32[]{:S(2)}, u32[]{:S(2)}) collective-permute-start(bf16[16,1280]{1,0:T(8,128)(2,1)S(1)} %pad_maximum_fusion.1), channel_id=1, source_target_pairs={{0,8},{8,16},{16,24},{24,32},{32,40},{40,48},{48,56},{56,64},{64,7... | collective-permute-start | bytes 122888 | tf_op jit(solution)/shard_map/ppermute | solution.py:200
  5.9 3.7 %collective-permute-done.rim_x.rim_b.rim_c = bf16[16,1280]{1,0:T(8,128)(2,1)S(1)} collective-permute-done((bf16[16,1280]{1,0:T(8,128)(2,1)S(1)}, bf16[16,1280]{1,0:T(8,128)(2,1)S(1)}, u32[]{:S(2)}, u32[]{:S(2)}) %collective-permute-start) | collective-permute-done | bytes 40992 | tf_op jit(solution)/shard_map/ppermute | solution.py:200
  14.7 7.0 %scan_in.1 = (bf16[512,1024]{1,0:T(8,128)(2,1)S(1)}, bf16[512,128]{1,0:T(8,128)(2,1)S(1)}, bf16[512,128]{1,0:T(8,128)(2,1)S(1)}, f32[512,16]{1,0:T(8,128)S(1)}, ...) custom-call(bf16[16,1280]{1,0:T(8,128)(2,1)S(1)} %collective-permute-done.rim_x.rim_b.rim_c, ...), custom_call_target="tpu_custom_call" | custom-call | flops 1000000000 | bytes 4000000 | tf_op jit(solution)/shard_map/scan_in/pallas_call | solution.py:202
  24.8 5.5 %all-to-all-start = ((bf16[32,48,128]{2,1,0:T(8,128)(2,1)}), bf16[32,48,128]{2,1,0:T(8,128)(2,1)S(1)}, u32[]{:S(2)}, u32[]{:S(2)}) async-start(bf16[32,48,128]{2,1,0:T(8,128)(2,1)} %get-tuple-element.18), calls=%async_computation | async-start | bytes 786432 | tf_op jit(solution)/shard_map/all_to_all | solution.py:240
  30.6 8.5 %all-to-all-done.got = bf16[32,48,128]{2,1,0:T(8,128)(2,1)S(1)} async-done(((bf16[32,48,128]{2,1,0:T(8,128)(2,1)}), bf16[32,48,128]{2,1,0:T(8,128)(2,1)S(1)}, u32[]{:S(2)}, u32[]{:S(2)}) %all-to-all-start) | async-done | bytes 393248 | tf_op jit(solution)/shard_map/all_to_all | solution.py:240
  41.6 5.1 %all-to-all-start.1 = ((bf16[32,32,128]{2,1,0:T(8,128)(2,1)}), bf16[32,32,128]{2,1,0:T(8,128)(2,1)S(1)}, u32[]{:S(2)}, u32[]{:S(2)}) async-start(bf16[32,32,128]{2,1,0:T(8,128)(2,1)} %prefix.1), calls=%async_computation.1 | async-start | bytes 524288 | tf_op jit(solution)/shard_map/all_to_all | solution.py:270
  51.8 5.3 %inside.1.y = f32[512,1024]{1,0:T(8,128)S(1)} custom-call(bf16[512,1024]{1,0:T(8,128)(2,1)S(1)} %copy-done.19, bf16[512,128]{1,0:T(8,128)(2,1)S(1)} %copy-done.21, bf16[512,128]{1,0:T(8,128)(2,1)S(1)} %get-tuple-element.15.cs, f32[512,16]{1,0:T(8,128)S(1)} %copy-done.5, f32[512,16]{1,0:T(8,128)S(1)} %copy-done.10, f32[512,16]{1,0:T(8,128)S(1)} %copy-done.8, ...), custom_call_target="tpu_custom_call" | custom-call | flops 4000000000 | bytes 6000000 | tf_op jit(solution)/shard_map/inside/pallas_call | solution.py:241
  59.2 7.4 %norm_project.1 = (bf16[512,1024]{1,0:T(8,128)(2,1)S(1)}, f32[512,2048]{1,0:T(8,128)S(1)}) custom-call(f32[512,1024]{1,0:T(8,128)S(1)} %inside.1.y, bf16[512,128]{1,0:T(8,128)(2,1)S(1)} %get-tuple-element.15.cs, f32[512,16]{1,0:T(8,128)S(1)} %copy-done.6, f32[1024,128]{1,0:T(8,128)S(1)} %copy-done.3, bf16[1024,128]{1,0:T(8,128)(2,1)S(1)} %bitcast.4, ...), custom_call_target="tpu_custom_call" | custom-call | tf_op jit(solution)/shard_map/norm_project/pallas_call | solution.py:275
  66.7 2.0 %collective-permute-start.1 = (bf16[64,2048]{1,0:T(8,128)(2,1)S(1)}, bf16[64,2048]{1,0:T(8,128)(2,1)S(1)}, u32[]{:S(2)}, u32[]{:S(2)}) collective-permute-start(bf16[64,2048]{1,0:T(8,128)(2,1)S(1)} %get-tuple-element.27), channel_id=1, source_target_pairs={{0,1},{1,2},{2,3},{3,4},{4,5},{5,6},{6,7},{7,0},{8,9},{9,10},{10,1... | collective-permute-start | bytes 786440 | tf_op jit(solution)/shard_map/ppermute | solution.py:193
  68.7 4.0 %collective-permute-start.5 = (bf16[64,2048]{1,0:T(8,128)(2,1)S(1)}, bf16[64,2048]{1,0:T(8,128)(2,1)S(1)}, u32[]{:S(2)}, u32[]{:S(2)}) collective-permute-start(bf16[64,2048]{1,0:T(8,128)(2,1)S(1)} %get-tuple-element.26), channel_id=1, source_target_pairs={{0,7},{1,0},{2,1},{3,2},{4,3},{5,4},{6,5},{7,6},{8,15},{9,8},{10,9... | collective-permute-start | bytes 786440 | tf_op jit(solution)/shard_map/ppermute | solution.py:193
  72.7 3.4 %copy-done = bf16[1024,4096]{1,0:T(8,128)(2,1)S(1)} copy-done((bf16[1024,4096]{1,0:T(8,128)(2,1)S(1)}, bf16[1024,4096]{1,0:T(8,128)(2,1)}, u32[]{:S(2)}) %copy-start) | copy-done | bytes 8388632
  76.1 3.5 %project.1 = f32[512,2048]{1,0:T(8,128)S(1)} custom-call(bf16[512,1024]{1,0:T(8,128)(2,1)S(1)} %get-tuple-element.20.normed, bf16[1024,4096]{1,0:T(8,128)(2,1)S(1)} %copy-done), custom_call_target="tpu_custom_call" | custom-call | flops 2000000000 | bytes 8000000 | tf_op jit(solution)/shard_map/project/pallas_call | solution.py:293
  79.6 2.0 %collective-permute-start.11 = (bf16[64,2048]{1,0:T(8,128)(2,1)S(1)}, bf16[64,2048]{1,0:T(8,128)(2,1)S(1)}, u32[]{:S(2)}, u32[]{:S(2)}) collective-permute-start(bf16[64,2048]{1,0:T(8,128)(2,1)S(1)} %get-tuple-element.33), channel_id=1, source_target_pairs={{0,7},{1,0},{2,1},{3,2},{4,3},{5,4},{6,5},{7,6},{8,15},{9,8},{10,9... | collective-permute-start | bytes 786440 | tf_op jit(solution)/shard_map/ppermute | solution.py:193
  82.1 5.7 %collective-permute-done.11 = bf16[64,2048]{1,0:T(8,128)(2,1)S(1)} collective-permute-done((bf16[64,2048]{1,0:T(8,128)(2,1)S(1)}, bf16[64,2048]{1,0:T(8,128)(2,1)S(1)}, u32[]{:S(2)}, u32[]{:S(2)}) %collective-permute-start.11) | collective-permute-done | bytes 262176 | tf_op jit(solution)/shard_map/ppermute | solution.py:193
  87.9 3.0 %collective-permute-start.12 = (bf16[64,2048]{1,0:T(8,128)(2,1)S(1)}, bf16[64,2048]{1,0:T(8,128)(2,1)S(1)}, u32[]{:S(2)}, u32[]{:S(2)}) collective-permute-start(bf16[64,2048]{1,0:T(8,128)(2,1)S(1)} %add_convert_fusion.2), channel_id=1, source_target_pairs={{0,7},{1,0},{2,1},{3,2},{4,3},{5,4},{6,5},{7,6},{8,15},{9,8},{10,9... | collective-permute-start | bytes 786440 | tf_op jit(solution)/shard_map/ppermute | solution.py:193
  90.8 5.2 %collective-permute-done.2 = bf16[64,2048]{1,0:T(8,128)(2,1)S(1)} collective-permute-done((bf16[64,2048]{1,0:T(8,128)(2,1)S(1)}, bf16[64,2048]{1,0:T(8,128)(2,1)S(1)}, u32[]{:S(2)}, u32[]{:S(2)}) %collective-permute-start.2) | collective-permute-done | bytes 262176 | tf_op jit(solution)/shard_map/ppermute | solution.py:193
  96.2 3.2 %collective-permute-start.6 = (bf16[64,2048]{1,0:T(8,128)(2,1)S(1)}, bf16[64,2048]{1,0:T(8,128)(2,1)S(1)}, u32[]{:S(2)}, u32[]{:S(2)}) collective-permute-start(bf16[64,2048]{1,0:T(8,128)(2,1)S(1)} %get-tuple-element.24), channel_id=1, source_target_pairs={{0,7},{1,0},{2,1},{3,2},{4,3},{5,4},{6,5},{7,6},{8,15},{9,8},{10,9... | collective-permute-start | bytes 786440 | tf_op jit(solution)/shard_map/ppermute | solution.py:193
  99.7 2.0 %collective-permute-start.9 = (bf16[64,2048]{1,0:T(8,128)(2,1)S(1)}, bf16[64,2048]{1,0:T(8,128)(2,1)S(1)}, u32[]{:S(2)}, u32[]{:S(2)}) collective-permute-start(bf16[64,2048]{1,0:T(8,128)(2,1)S(1)} %get-tuple-element.32), channel_id=1, source_target_pairs={{0,1},{1,2},{2,3},{3,4},{4,5},{5,6},{6,7},{7,0},{8,9},{9,10},{10,1... | collective-permute-start | bytes 786440 | tf_op jit(solution)/shard_map/ppermute | solution.py:193
  101.7 5.0 %collective-permute-done.3 = bf16[64,2048]{1,0:T(8,128)(2,1)S(1)} collective-permute-done((bf16[64,2048]{1,0:T(8,128)(2,1)S(1)}, bf16[64,2048]{1,0:T(8,128)(2,1)S(1)}, u32[]{:S(2)}, u32[]{:S(2)}) %collective-permute-start.3) | collective-permute-done | bytes 262176 | tf_op jit(solution)/shard_map/ppermute | solution.py:193
  107.6 3.2 %collective-permute-start.7 = (bf16[64,2048]{1,0:T(8,128)(2,1)S(1)}, bf16[64,2048]{1,0:T(8,128)(2,1)S(1)}, u32[]{:S(2)}, u32[]{:S(2)}) collective-permute-start(bf16[64,2048]{1,0:T(8,128)(2,1)S(1)} %get-tuple-element.21), channel_id=1, source_target_pairs={{0,7},{1,0},{2,1},{3,2},{4,3},{5,4},{6,5},{7,6},{8,15},{9,8},{10,9... | collective-permute-start | bytes 786440 | tf_op jit(solution)/shard_map/ppermute | solution.py:193
  113.2 3.2 %collective-permute-start.14 = (bf16[64,2048]{1,0:T(8,128)(2,1)S(1)}, bf16[64,2048]{1,0:T(8,128)(2,1)S(1)}, u32[]{:S(2)}, u32[]{:S(2)}) collective-permute-start(bf16[64,2048]{1,0:T(8,128)(2,1)S(1)} %get-tuple-element.28), channel_id=1, source_target_pairs={{0,7},{1,0},{2,1},{3,2},{4,3},{5,4},{6,5},{7,6},{8,15},{9,8},{10,9... | collective-permute-start | bytes 786440 | tf_op jit(solution)/shard_map/ppermute | solution.py:193
  118.8 2.5 %finish.2 = bf16[64,2048]{1,0:T(8,128)(2,1)} custom-call(f32[64,2048]{1,0:T(8,128)} %get-tuple-element.23.own, bf16[64,2048]{1,0:T(8,128)(2,1)} %copy-done.23, bf16[64,2048]{1,0:T(8,128)(2,1)} %copy-done.24, f32[1,2048]{1,0:T(1,128)} %bitcast.7), custom_call_target="tpu_custom_call" | custom-call | tf_op jit(solution)/shard_map/finish/pallas_call | solution.py:328
  122.1 2.5 %finish.3 = bf16[64,2048]{1,0:T(8,128)(2,1)} custom-call(f32[64,2048]{1,0:T(8,128)} %get-tuple-element.30.own, bf16[64,2048]{1,0:T(8,128)(2,1)} %copy-done.25, bf16[64,2048]{1,0:T(8,128)(2,1)} %copy-done.26, f32[1,2048]{1,0:T(1,128)} %bitcast.6), custom_call_target="tpu_custom_call" | custom-call | tf_op jit(solution)/shard_map/finish/pallas_call | solution.py:328
  124.6 1.9 %pad_maximum_fusion = bf16[64,4096]{1,0:T(8,128)(2,1)} fusion(bf16[64,2048]{1,0:T(8,128)(2,1)} %finish.3, bf16[64,2048]{1,0:T(8,128)(2,1)} %finish.2), kind=kLoop, calls=%fused_computation | loop fusion | flops 1048576 | bytes 1048576 | tf_op jit(solution)/shard_map/concatenate | solution.py:334
  (96 shorter events, 29.5 us)
Async XLA Ops:
  0.0 30.4 %copy-start.29 = (f32[16]{0:T(128)S(1)}, f32[16]{0:T(128)}, u32[]{:S(2)}) copy-start(f32[16]{0:T(128)} %param.23) | copy-start | bytes 196
  2.2 7.4 %collective-permute-start = (bf16[16,1280]{1,0:T(8,128)(2,1)S(1)}, bf16[16,1280]{1,0:T(8,128)(2,1)S(1)}, u32[]{:S(2)}, u32[]{:S(2)}) collective-permute-start(bf16[16,1280]{1,0:T(8,128)(2,1)S(1)} %pad_maximum_fusion.1), channel_id=1, source_target_pairs={{0,8},{8,16},{16,24},{24,32},{32,40},{40,48},{48,56},{56,64},{64,7... | collective-permute-start | bytes 122888 | tf_op jit(solution)/shard_map/ppermute | solution.py:200
  5.0 41.8 %copy-start.7 = (f32[512,16]{1,0:T(8,128)}, f32[512,16]{1,0:T(8,128)S(1)}, u32[]{:S(2)}) copy-start(f32[512,16]{1,0:T(8,128)S(1)} %copy.15.step) | copy-start | bytes 98308
  5.9 40.9 %copy-start.9 = (f32[512,16]{1,0:T(8,128)}, f32[512,16]{1,0:T(8,128)S(1)}, u32[]{:S(2)}) copy-start(f32[512,16]{1,0:T(8,128)S(1)} %copy.16.decay) | copy-start | bytes 98308
  24.8 14.2 %all-to-all-start = ((bf16[32,48,128]{2,1,0:T(8,128)(2,1)}), bf16[32,48,128]{2,1,0:T(8,128)(2,1)S(1)}, u32[]{:S(2)}, u32[]{:S(2)}) async-start(bf16[32,48,128]{2,1,0:T(8,128)(2,1)} %get-tuple-element.18), calls=%async_computation | async-start | bytes 786432 | tf_op jit(solution)/shard_map/all_to_all | solution.py:240
  41.6 15.5 %all-to-all-start.1 = ((bf16[32,32,128]{2,1,0:T(8,128)(2,1)}), bf16[32,32,128]{2,1,0:T(8,128)(2,1)S(1)}, u32[]{:S(2)}, u32[]{:S(2)}) async-start(bf16[32,32,128]{2,1,0:T(8,128)(2,1)} %prefix.1), calls=%async_computation.1 | async-start | bytes 524288 | tf_op jit(solution)/shard_map/all_to_all | solution.py:270
  51.8 5.4 %copy-start.1 = (bf16[512,1024]{1,0:T(8,128)(2,1)S(1)}, bf16[512,1024]{1,0:T(8,128)(2,1)}, u32[]{:S(2)}) copy-start(bf16[512,1024]{1,0:T(8,128)(2,1)} %z.1) | copy-start | bytes 3145732
  51.8 5.4 %copy-start.11 = (f32[1024]{0:T(1024)S(1)}, f32[1024]{0:T(1024)}, u32[]{:S(2)}) copy-start(f32[1024]{0:T(1024)} %param.24) | copy-start | bytes 12292
  66.7 15.1 %collective-permute-start.1 = (bf16[64,2048]{1,0:T(8,128)(2,1)S(1)}, bf16[64,2048]{1,0:T(8,128)(2,1)S(1)}, u32[]{:S(2)}, u32[]{:S(2)}) collective-permute-start(bf16[64,2048]{1,0:T(8,128)(2,1)S(1)} %get-tuple-element.27), channel_id=1, source_target_pairs={{0,1},{1,2},{2,3},{3,4},{4,5},{5,6},{6,7},{7,0},{8,9},{9,10},{10,1... | collective-permute-start | bytes 786440 | tf_op jit(solution)/shard_map/ppermute | solution.py:193
  68.7 22.1 %collective-permute-start.5 = (bf16[64,2048]{1,0:T(8,128)(2,1)S(1)}, bf16[64,2048]{1,0:T(8,128)(2,1)S(1)}, u32[]{:S(2)}, u32[]{:S(2)}) collective-permute-start(bf16[64,2048]{1,0:T(8,128)(2,1)S(1)} %get-tuple-element.26), channel_id=1, source_target_pairs={{0,7},{1,0},{2,1},{3,2},{4,3},{5,4},{6,5},{7,6},{8,15},{9,8},{10,9... | collective-permute-start | bytes 786440 | tf_op jit(solution)/shard_map/ppermute | solution.py:193
  79.6 8.2 %collective-permute-start.11 = (bf16[64,2048]{1,0:T(8,128)(2,1)S(1)}, bf16[64,2048]{1,0:T(8,128)(2,1)S(1)}, u32[]{:S(2)}, u32[]{:S(2)}) collective-permute-start(bf16[64,2048]{1,0:T(8,128)(2,1)S(1)} %get-tuple-element.33), channel_id=1, source_target_pairs={{0,7},{1,0},{2,1},{3,2},{4,3},{5,4},{6,5},{7,6},{8,15},{9,8},{10,9... | collective-permute-start | bytes 786440 | tf_op jit(solution)/shard_map/ppermute | solution.py:193
  81.7 17.8 %collective-permute-start.8 = (bf16[64,2048]{1,0:T(8,128)(2,1)S(1)}, bf16[64,2048]{1,0:T(8,128)(2,1)S(1)}, u32[]{:S(2)}, u32[]{:S(2)}) collective-permute-start(bf16[64,2048]{1,0:T(8,128)(2,1)S(1)} %get-tuple-element.34), channel_id=1, source_target_pairs={{0,1},{1,2},{2,3},{3,4},{4,5},{5,6},{6,7},{7,0},{8,9},{9,10},{10,1... | collective-permute-start | bytes 786440 | tf_op jit(solution)/shard_map/ppermute | solution.py:193
  81.8 14.2 %collective-permute-start.2 = (bf16[64,2048]{1,0:T(8,128)(2,1)S(1)}, bf16[64,2048]{1,0:T(8,128)(2,1)S(1)}, u32[]{:S(2)}, u32[]{:S(2)}) collective-permute-start(bf16[64,2048]{1,0:T(8,128)(2,1)S(1)} %add_convert_fusion.9), channel_id=1, source_target_pairs={{0,1},{1,2},{2,3},{3,4},{4,5},{5,6},{6,7},{7,0},{8,9},{9,10},{10,1... | collective-permute-start | bytes 786440 | tf_op jit(solution)/shard_map/ppermute | solution.py:193
  87.9 11.6 %collective-permute-start.12 = (bf16[64,2048]{1,0:T(8,128)(2,1)S(1)}, bf16[64,2048]{1,0:T(8,128)(2,1)S(1)}, u32[]{:S(2)}, u32[]{:S(2)}) collective-permute-start(bf16[64,2048]{1,0:T(8,128)(2,1)S(1)} %add_convert_fusion.2), channel_id=1, source_target_pairs={{0,7},{1,0},{2,1},{3,2},{4,3},{5,4},{6,5},{7,6},{8,15},{9,8},{10,9... | collective-permute-start | bytes 786440 | tf_op jit(solution)/shard_map/ppermute | solution.py:193
  96.1 10.5 %collective-permute-start.3 = (bf16[64,2048]{1,0:T(8,128)(2,1)S(1)}, bf16[64,2048]{1,0:T(8,128)(2,1)S(1)}, u32[]{:S(2)}, u32[]{:S(2)}) collective-permute-start(bf16[64,2048]{1,0:T(8,128)(2,1)S(1)} %get-tuple-element.25), channel_id=1, source_target_pairs={{0,1},{1,2},{2,3},{3,4},{4,5},{5,6},{6,7},{7,0},{8,9},{9,10},{10,1... | collective-permute-start | bytes 786440 | tf_op jit(solution)/shard_map/ppermute | solution.py:193
  96.2 20.3 %copy-start.27 = (s32[4096]{0:T(1024)S(1)}, s32[4096]{0:T(1024)}, u32[]{:S(2)}) copy-start(s32[4096]{0:T(1024)} %param.27) | copy-start | bytes 49156
  96.2 20.3 %copy-start.28 = (s32[4096]{0:T(1024)S(1)}, s32[4096]{0:T(1024)}, u32[]{:S(2)}) copy-start(s32[4096]{0:T(1024)} %param.26) | copy-start | bytes 49156
  96.2 10.4 %collective-permute-start.6 = (bf16[64,2048]{1,0:T(8,128)(2,1)S(1)}, bf16[64,2048]{1,0:T(8,128)(2,1)S(1)}, u32[]{:S(2)}, u32[]{:S(2)}) collective-permute-start(bf16[64,2048]{1,0:T(8,128)(2,1)S(1)} %get-tuple-element.24), channel_id=1, source_target_pairs={{0,7},{1,0},{2,1},{3,2},{4,3},{5,4},{6,5},{7,6},{8,15},{9,8},{10,9... | collective-permute-start | bytes 786440 | tf_op jit(solution)/shard_map/ppermute | solution.py:193
  99.6 12.2 %collective-permute-start.13 = (bf16[64,2048]{1,0:T(8,128)(2,1)S(1)}, bf16[64,2048]{1,0:T(8,128)(2,1)S(1)}, u32[]{:S(2)}, u32[]{:S(2)}) collective-permute-start(bf16[64,2048]{1,0:T(8,128)(2,1)S(1)} %get-tuple-element.31), channel_id=1, source_target_pairs={{0,7},{1,0},{2,1},{3,2},{4,3},{5,4},{6,5},{7,6},{8,15},{9,8},{10,9... | collective-permute-start | bytes 786440 | tf_op jit(solution)/shard_map/ppermute | solution.py:193
  99.7 12.6 %collective-permute-start.9 = (bf16[64,2048]{1,0:T(8,128)(2,1)S(1)}, bf16[64,2048]{1,0:T(8,128)(2,1)S(1)}, u32[]{:S(2)}, u32[]{:S(2)}) collective-permute-start(bf16[64,2048]{1,0:T(8,128)(2,1)S(1)} %get-tuple-element.32), channel_id=1, source_target_pairs={{0,1},{1,2},{2,3},{3,4},{4,5},{5,6},{6,7},{7,0},{8,9},{9,10},{10,1... | collective-permute-start | bytes 786440 | tf_op jit(solution)/shard_map/ppermute | solution.py:193
  107.6 10.5 %collective-permute-start.4 = (bf16[64,2048]{1,0:T(8,128)(2,1)S(1)}, bf16[64,2048]{1,0:T(8,128)(2,1)S(1)}, u32[]{:S(2)}, u32[]{:S(2)}) collective-permute-start(bf16[64,2048]{1,0:T(8,128)(2,1)S(1)} %get-tuple-element.22), channel_id=1, source_target_pairs={{0,1},{1,2},{2,3},{3,4},{4,5},{5,6},{6,7},{7,0},{8,9},{9,10},{10,1... | collective-permute-start | bytes 786440 | tf_op jit(solution)/shard_map/ppermute | solution.py:193
  107.6 10.5 %collective-permute-start.7 = (bf16[64,2048]{1,0:T(8,128)(2,1)S(1)}, bf16[64,2048]{1,0:T(8,128)(2,1)S(1)}, u32[]{:S(2)}, u32[]{:S(2)}) collective-permute-start(bf16[64,2048]{1,0:T(8,128)(2,1)S(1)} %get-tuple-element.21), channel_id=1, source_target_pairs={{0,7},{1,0},{2,1},{3,2},{4,3},{5,4},{6,5},{7,6},{8,15},{9,8},{10,9... | collective-permute-start | bytes 786440 | tf_op jit(solution)/shard_map/ppermute | solution.py:193
  113.2 8.1 %collective-permute-start.10 = (bf16[64,2048]{1,0:T(8,128)(2,1)S(1)}, bf16[64,2048]{1,0:T(8,128)(2,1)S(1)}, u32[]{:S(2)}, u32[]{:S(2)}) collective-permute-start(bf16[64,2048]{1,0:T(8,128)(2,1)S(1)} %get-tuple-element.29), channel_id=1, source_target_pairs={{0,1},{1,2},{2,3},{3,4},{4,5},{5,6},{6,7},{7,0},{8,9},{9,10},{10,1... | collective-permute-start | bytes 786440 | tf_op jit(solution)/shard_map/ppermute | solution.py:193
  113.2 8.1 %collective-permute-start.14 = (bf16[64,2048]{1,0:T(8,128)(2,1)S(1)}, bf16[64,2048]{1,0:T(8,128)(2,1)S(1)}, u32[]{:S(2)}, u32[]{:S(2)}) collective-permute-start(bf16[64,2048]{1,0:T(8,128)(2,1)S(1)} %get-tuple-element.28), channel_id=1, source_target_pairs={{0,7},{1,0},{2,1},{3,2},{4,3},{5,4},{6,5},{7,6},{8,15},{9,8},{10,9... | collective-permute-start | bytes 786440 | tf_op jit(solution)/shard_map/ppermute | solution.py:193
  (23 other events, 22.4 us)

commit v2 on v1

v2 whole, which is shorter than its diff:
```python
import math

import jax
import jax.numpy as jnp
from jax import lax
from jax.experimental import pallas as pl
from jax.experimental.pallas import tpu as pltpu
from jax.sharding import PartitionSpec as P

HEAD_DIM = 64
STATE = 128
SPAN = 256
HAD_BLOCK = 128
HEADS_LOCAL = 16
TOK = 512
CH = 1024
PARTS = 32
PIECE = 32
PAY = 48
TILE = 256
ROWS = 128
SHARE = 64
MIB = 1024 * 1024
LIMIT = dict(tail_rows=58, scan_in=58, scan_edge=58, inside=58, prefix=16, norm_first=52, project=58, ring=50)

F32 = jnp.float32
BF16 = jnp.bfloat16
HIGHEST = lax.Precision.HIGHEST


def dot(a, b, dims=((1,), (0,)), precision=None):
    return lax.dot_general(a, b, (dims, ((), ())), precision=precision, preferred_element_type=F32)


def conv_silu(pad, rim, values, taps):
    width = values.shape[1]
    pad[0:8, 0:width] = rim[8:16].astype(F32)
    pad[8 : TOK + 8, 0:width] = values.astype(F32)
    total = taps[0:1] * pad[5 : 5 + TOK, 0:width]
    for k in range(1, 4):
        total = total + taps[k : k + 1] * pad[5 + k : 5 + k + TOK, 0:width]
    return jax.nn.silu(total).astype(BF16)


def head_rows(first, channels):
    head = lax.broadcasted_iota(jnp.int32, (HEADS_LOCAL, channels), 0)
    channel = lax.broadcasted_iota(jnp.int32, (HEADS_LOCAL, channels), 1)
    return (channel // HEAD_DIM + first == head).astype(F32)


def head_columns(first, channels, row):
    channel = lax.broadcasted_iota(jnp.int32, (channels, HEADS_LOCAL), 0)
    head = lax.broadcasted_iota(jnp.int32, (channels, HEADS_LOCAL), 1)
    return jnp.sum(jnp.where(channel // HEAD_DIM + first == head, row, 0.0), axis=1, keepdims=True)


def tail_rows(x, b, c, out):
    out[:, 0:CH] = x[...]
    out[:, CH : CH + STATE] = b[...]
    out[:, CH + STATE :] = c[...]


def scan_in(x, b, c, step_t, decay_t, tap_x, tap_b, tap_c, xs_o, bs_o, cs_o, run_o, toward_o, one_o, two_o, pad):
    tile = pl.program_id(0)

    @pl.when(tile == 0)
    def _():
        empty = jnp.zeros((16, STATE), BF16)
        bs_o[...] = conv_silu(pad, empty, b[...], tap_b[...])
        cs_o[...] = conv_silu(pad, empty, c[...], tap_c[...])
        later = lax.broadcasted_iota(jnp.int32, (SPAN, SPAN), 0)
        earlier = lax.broadcasted_iota(jnp.int32, (SPAN, SPAN), 1)
        lower = (later >= earlier).astype(F32)
        same = (later == earlier).astype(F32)
        for k in range(2):
            rows = slice(k * SPAN, (k + 1) * SPAN)
            running = dot(lower, decay_t[:, rows], ((1,), (1,)), precision=HIGHEST)
            step = dot(same, step_t[:, rows], ((1,), (1,)), precision=HIGHEST)
            run_o[rows] = running
            toward_o[rows] = jnp.exp(running[SPAN - 1 :] - running) * step

    xs = conv_silu(pad, jnp.zeros((16, TILE), BF16), x[...], tap_x[...])
    xs_o[...] = xs
    first = tile * (TILE // HEAD_DIM)
    wide = dot(toward_o[...], head_rows(first, TILE), precision=HIGHEST)
    row = lax.broadcasted_iota(jnp.int32, (TOK, 1), 0)
    feed = jnp.where(row < 8, 0.0, xs.astype(F32) * wide).astype(BF16)
    one_o[...] = dot(feed[:SPAN], bs_o[:SPAN], ((0,), (0,)))
    two_o[...] = dot(feed[SPAN:], bs_o[SPAN:], ((0,), (0,)))


def conv_head(rim, values, taps):
    padded = jnp.concatenate([rim.astype(F32), values.astype(F32)], 0)
    total = taps[0:1] * padded[13:29]
    for k in range(1, 4):
        total = total + taps[k : k + 1] * padded[13 + k : 29 + k]
    return jax.nn.silu(total).astype(BF16)


def scan_edge(rim, x, b, c, tap_x, tap_b, tap_c, toward, run0, run1, one, two, xs_in, bs_in, cs_in,
              xs_o, bs_o, cs_o, first_o, pay_o):
    xs = conv_head(rim[:, 0:CH], x[...], tap_x[...])
    bs = conv_head(rim[:, CH : CH + STATE], b[...], tap_b[...])
    xs_o[...] = xs
    bs_o[...] = bs
    cs_o[...] = conv_head(rim[:, CH + STATE :], c[...], tap_c[...])
    wide = dot(toward[...], head_rows(0, CH), precision=HIGHEST)
    row = lax.broadcasted_iota(jnp.int32, (16, 1), 0)
    feed = jnp.where(row < 8, xs.astype(F32) * wide, 0.0).astype(BF16)
    first = one[...] + dot(feed, bs, ((0,), (0,)))
    first_o[...] = first
    end0 = run0[7:8]
    end1 = run1[7:8]
    state = jnp.exp(head_columns(0, CH, end1)) * first + two[...]
    pay_o[:, 0:PIECE, :] = state.astype(BF16).reshape(PARTS, PIECE, STATE)
    total = head_columns(0, CH, end0 + end1).reshape(PARTS, PIECE, 1)[:, 0 : PAY - PIECE, :]
    total = jnp.broadcast_to(total, (PARTS, PAY - PIECE, STATE))
    high = total.astype(BF16).astype(F32)
    rest = total - high
    middle = rest.astype(BF16).astype(F32)
    low = rest - middle
    row = lax.broadcasted_iota(jnp.int32, total.shape, 1)
    pay_o[:, PIECE:PAY, :] = jnp.where(row == 0, high, jnp.where(row == 1, middle, low)).astype(BF16)


def prefix(got, out):
    log_total = got[:, PIECE : PIECE + 8, :].astype(F32)
    grow = jnp.exp(log_total[:, 0:1] + log_total[:, 1:2] + log_total[:, 2:3])
    state = jnp.zeros((PIECE, STATE), F32)
    for k in range(PARTS):
        out[k] = state.astype(BF16)
        if k < PARTS - 1:
            state = grow[k] * state + got[k, 0:PIECE, :].astype(F32)


def inside(xs, bs, cs, run, decay_t, step_t, skip, z, y_o, grow_o, scores, run_t):
    tile = pl.program_id(0)

    @pl.when(tile == 0)
    def _():
        later = lax.broadcasted_iota(jnp.int32, (SPAN, SPAN), 0)
        earlier = lax.broadcasted_iota(jnp.int32, (SPAN, SPAN), 1)
        upper = (later <= earlier).astype(F32)
        for k in range(2):
            rows = slice(k * SPAN, (k + 1) * SPAN)
            raw = dot(cs[rows], bs[rows], ((1,), (1,)))
            scores[rows] = jnp.where(later >= earlier, raw, 0.0)
            run_t[:, rows] = dot(decay_t[:, rows], upper, precision=HIGHEST)

    per_tile = TILE // HEAD_DIM
    head_lane = lax.broadcasted_iota(jnp.int32, (HEADS_LOCAL, 1), 0)
    lane_head = lax.broadcasted_iota(jnp.int32, (TOK, HEADS_LOCAL), 1)
    for q in range(per_tile):
        head = tile * per_tile + q
        column = jnp.sum(jnp.where(lane_head == head, run[...], 0.0), axis=1, keepdims=True)
        r_row = jnp.sum(jnp.where(head_lane == head, run_t[...], 0.0), axis=0, keepdims=True)
        s_row = jnp.sum(jnp.where(head_lane == head, step_t[...], 0.0), axis=0, keepdims=True)
        lanes = slice(q * HEAD_DIM, (q + 1) * HEAD_DIM)
        for k in range(2):
            rows = slice(k * SPAN, (k + 1) * SPAN)
            spread = jnp.minimum(column[rows] - r_row[:, rows], 0.0)
            weights = (jnp.exp(spread) * scores[rows] * s_row[:, rows]).astype(BF16)
            y_o[rows, lanes] = dot(weights, xs[rows, lanes])
    gate = jax.nn.silu(z[...].astype(F32))
    y_o[...] = (y_o[...] + skip[...] * xs[...].astype(F32)) * gate
    grow_o[...] = dot(jnp.exp(run[...]), head_rows(tile * per_tile, TILE), precision=HIGHEST) * gate


def norm_first(y, grow, cs, run, first, incoming, gain, weight, normed_o, up_o, down_o, start, held, picked, sem):
    step = pl.program_id(0)
    fetch = pltpu.make_async_copy(weight.at[:, 0 : held.shape[1]], held, sem)

    @pl.when(step == 0)
    def _():
        fetch.start()
        start[...] = incoming[...]

    @pl.when(step == SPAN // ROWS)
    def _():
        decay = jnp.exp(head_columns(0, CH, run[7:8]))
        start[...] = (decay * incoming[...].astype(F32) + first[...]).astype(BF16)

    carried = dot(cs[...], start[...], ((1,), (1,)))
    gated = y[...] + grow[...] * carried
    meansq = jnp.sum(gated * gated, axis=1, keepdims=True) * (1.0 / CH)
    rows = pl.ds(pl.multiple_of(step * ROWS, ROWS), ROWS)
    normed_o[rows] = (gated * lax.rsqrt(meansq + 1e-05) * gain[...]).astype(BF16)

    @pl.when(step == TOK // ROWS - 1)
    def _():
        place = lax.axis_index("tp")
        for k, distance in enumerate((4, 5)):
            at = pl.multiple_of(lax.rem(place + distance, 8) * SHARE, SHARE)
            picked[k * SHARE : (k + 1) * SHARE] = normed_o[pl.ds(at, SHARE)]
        fetch.wait()
        for k in range(held.shape[1] // 512):
            lanes = slice(k * 512, (k + 1) * 512)
            both = dot(picked[...], held[:, lanes]).astype(BF16)
            up_o[:, lanes] = both[:SHARE]
            down_o[:, lanes] = both[SHARE:]


def project(normed, weight, part_o):
    part_o[...] = dot(normed[...], weight[...])


def add_hop(place, came, part, out):
    out[...] = (came[...].astype(F32) + part[...]).astype(BF16)


def first_hop(place, part_up, part_down, up_o, down_o):
    up_o[...] = part_up[...].astype(BF16)
    down_o[...] = part_down[...].astype(BF16)


def finish(place, own, up_a, down_a, up_b, down_b, scale, out):
    row = lax.broadcasted_iota(jnp.int32, (HAD_BLOCK, HAD_BLOCK), 0)
    column = lax.broadcasted_iota(jnp.int32, (HAD_BLOCK, HAD_BLOCK), 1)
    ones = row & column
    ones = ones ^ (ones >> 4)
    ones = ones ^ (ones >> 2)
    ones = ones ^ (ones >> 1)
    table = (1 - 2 * (ones & 1)).astype(F32).astype(BF16)
    half = up_a.shape[1]
    for group, (up, down) in enumerate(((up_a, down_a), (up_b, down_b))):
        at = slice(group * half, (group + 1) * half)
        total = (own[:, at] + up[...].astype(F32) + down[...].astype(F32)) * scale[:, at]
        stacked = jnp.concatenate(
            [total[:, k * HAD_BLOCK : (k + 1) * HAD_BLOCK] for k in range(half // HAD_BLOCK)], 0
        )
        high = stacked.astype(BF16)
        rest = stacked - high.astype(F32)
        middle = rest.astype(BF16)
        low = (rest - middle.astype(F32)).astype(BF16)
        rotated = dot(high, table) + dot(middle, table) + dot(low, table)
        rotated = (rotated * (1.0 / math.sqrt(HAD_BLOCK))).astype(BF16)
        for k in range(half // HAD_BLOCK):
            lanes = slice(group * half + k * HAD_BLOCK, group * half + (k + 1) * HAD_BLOCK)
            out[:, lanes] = rotated[k * SHARE : (k + 1) * SHARE]


def whole(shape):
    return pl.BlockSpec(shape, lambda i: (0,) * len(shape))


def tiled(shape, axis):
    return pl.BlockSpec(shape, lambda i: tuple(i if d == axis else 0 for d in range(len(shape))))


def params(mib):
    return pltpu.CompilerParams(vmem_limit_bytes=mib * MIB)


def ring(value, step):
    count = lax.axis_size("tp")
    return lax.ppermute(value, "tp", [(k, (k + step) % count) for k in range(count)])


def shape(dims, dtype):
    return jax.ShapeDtypeStruct(dims, dtype)


def block(dims, *index):
    return pl.BlockSpec(dims, lambda i: index)


def local(x_in, b_in, c_in, z_in, step_size, log_decay, conv_x, conv_b, conv_c, d_skip, norm_gain,
          out_weight, out_exponent, out_sign):
    seq = lax.axis_size("seq")
    tiles = CH // TILE
    step_t = step_size.T
    decay_t = log_decay.T
    last = TOK // 16 - 1
    tail = pl.pallas_call(
        tail_rows,
        grid=(1,),
        in_specs=[block((16, CH), last, 0), block((16, STATE), last, 0), block((16, STATE), last, 0)],
        out_specs=whole((16, CH + 2 * STATE)),
        out_shape=shape((16, CH + 2 * STATE), BF16),
        compiler_params=params(LIMIT["tail_rows"]),
        name="tail_rows",
    )(x_in, b_in, c_in)
    rim = lax.ppermute(tail, "seq", [(k, k + 1) for k in range(seq - 1)])
    xs, bs, cs, run, toward, one, two = pl.pallas_call(
        scan_in,
        grid=(tiles,),
        in_specs=[
            tiled((TOK, TILE), 1),
            whole((TOK, STATE)),
            whole((TOK, STATE)),
            whole((HEADS_LOCAL, TOK)),
            whole((HEADS_LOCAL, TOK)),
            tiled((4, TILE), 1),
            whole((4, STATE)),
            whole((4, STATE)),
        ],
        out_specs=[
            tiled((TOK, TILE), 1),
            whole((TOK, STATE)),
            whole((TOK, STATE)),
            whole((TOK, HEADS_LOCAL)),
            whole((TOK, HEADS_LOCAL)),
            tiled((TILE, STATE), 0),
            tiled((TILE, STATE), 0),
        ],
        out_shape=[
            shape((TOK, CH), BF16),
            shape((TOK, STATE), BF16),
            shape((TOK, STATE), BF16),
            shape((TOK, HEADS_LOCAL), F32),
            shape((TOK, HEADS_LOCAL), F32),
            shape((CH, STATE), F32),
            shape((CH, STATE), F32),
        ],
        scratch_shapes=[pltpu.VMEM((TOK + 8, TILE), F32)],
        compiler_params=params(LIMIT["scan_in"]),
        cost_estimate=pl.CostEstimate(flops=10**9, bytes_accessed=4 * 10**6, transcendentals=10**6),
        name="scan_in",
    )(x_in, b_in, c_in, step_t, decay_t, conv_x, conv_b, conv_c)

    xs, bs, cs, first, pay = pl.pallas_call(
        scan_edge,
        grid=(1,),
        in_specs=[
            whole((16, CH + 2 * STATE)),
            whole((16, CH)),
            whole((16, STATE)),
            whole((16, STATE)),
            whole((4, CH)),
            whole((4, STATE)),
            whole((4, STATE)),
            whole((16, HEADS_LOCAL)),
            block((8, HEADS_LOCAL), SPAN // 8 - 1, 0),
            block((8, HEADS_LOCAL), TOK // 8 - 1, 0),
            whole((CH, STATE)),
            whole((CH, STATE)),
            pl.BlockSpec(memory_space=pl.ANY),
            pl.BlockSpec(memory_space=pl.ANY),
            pl.BlockSpec(memory_space=pl.ANY),
        ],
        out_specs=[
            whole((16, CH)),
            whole((16, STATE)),
            whole((16, STATE)),
            whole((CH, STATE)),
            whole((PARTS, PAY, STATE)),
        ],
        out_shape=[
            shape((TOK, CH), BF16),
            shape((TOK, STATE), BF16),
            shape((TOK, STATE), BF16),
            shape((CH, STATE), F32),
            shape((PARTS, PAY, STATE), BF16),
        ],
        input_output_aliases={12: 0, 13: 1, 14: 2},
        compiler_params=params(LIMIT["scan_edge"]),
        name="scan_edge",
    )(rim, x_in, b_in, c_in, conv_x, conv_b, conv_c, toward, run, run, one, two, xs, bs, cs)

    got = lax.all_to_all(pay, "seq", 0, 0, tiled=True)
    y, grow = pl.pallas_call(
        inside,
        grid=(tiles,),
        in_specs=[
            tiled((TOK, TILE), 1),
            whole((TOK, STATE)),
            whole((TOK, STATE)),
            whole((TOK, HEADS_LOCAL)),
            whole((HEADS_LOCAL, TOK)),
            whole((HEADS_LOCAL, TOK)),
            tiled((1, TILE), 1),
            tiled((TOK, TILE), 1),
        ],
        out_specs=[tiled((TOK, TILE), 1), tiled((TOK, TILE), 1)],
        out_shape=[shape((TOK, CH), F32), shape((TOK, CH), F32)],
        scratch_shapes=[pltpu.VMEM((TOK, SPAN), F32), pltpu.VMEM((HEADS_LOCAL, TOK), F32)],
        compiler_params=params(LIMIT["inside"]),
        cost_estimate=pl.CostEstimate(flops=4 * 10**9, bytes_accessed=6 * 10**6, transcendentals=2 * 10**6),
        name="inside",
    )(xs, bs, cs, run, decay_t, step_t, jnp.repeat(d_skip, HEAD_DIM)[None, :], z_in)

    before = pl.pallas_call(
        prefix,
        grid=(1,),
        in_specs=[whole((PARTS, PAY, STATE))],
        out_specs=whole((PARTS, PIECE, STATE)),
        out_shape=shape((PARTS, PIECE, STATE), BF16),
        compiler_params=params(LIMIT["prefix"]),
        name="prefix",
    )(got)
    incoming = lax.all_to_all(before, "seq", 0, 0, tiled=True).reshape(CH, STATE)

    model = out_weight.shape[1]
    half = model // 2
    step_cols = 512
    normed, up_a, down_a = pl.pallas_call(
        norm_first,
        grid=(TOK // ROWS,),
        in_specs=[
            tiled((ROWS, CH), 0),
            tiled((ROWS, CH), 0),
            tiled((ROWS, STATE), 0),
            block((8, HEADS_LOCAL), SPAN // 8 - 1, 0),
            whole((CH, STATE)),
            whole((CH, STATE)),
            whole((1, CH)),
            pl.BlockSpec(memory_space=pl.ANY),
        ],
        out_specs=[whole((TOK, CH)), whole((SHARE, half)), whole((SHARE, half))],
        out_shape=[shape((TOK, CH), BF16), shape((SHARE, half), BF16), shape((SHARE, half), BF16)],
        scratch_shapes=[
            pltpu.VMEM((CH, STATE), BF16),
            pltpu.VMEM((CH, half), BF16),
            pltpu.VMEM((2 * SHARE, CH), BF16),
            pltpu.SemaphoreType.DMA,
        ],
        compiler_params=params(LIMIT["norm_first"]),
        name="norm_first",
    )(y, grow, cs, run, first, incoming, norm_gain[None, :], out_weight)
    part = pl.pallas_call(
        project,
        grid=(model // step_cols,),
        in_specs=[whole((TOK, CH)), tiled((CH, step_cols), 1)],
        out_specs=tiled((TOK, step_cols), 1),
        out_shape=shape((TOK, model), F32),
        compiler_params=params(LIMIT["project"]),
        cost_estimate=pl.CostEstimate(flops=2 * 10**10, bytes_accessed=16 * 10**6, transcendentals=0),
        name="project",
    )(normed, out_weight)

    count = lax.axis_size("tp")
    place = lax.axis_index("tp").astype(jnp.int32)[None]
    scale = jnp.exp2(out_exponent.astype(F32)) * out_sign.astype(F32)

    def chunk(distance, group):
        return pl.BlockSpec((SHARE, half), lambda i, at: (lax.rem(at[0] + distance + count, count), group))

    message = pl.BlockSpec((SHARE, half), lambda i, at: (0, 0))

    def call(kernel, in_specs, outs, out_specs, *operands):
        return pl.pallas_call(
            kernel,
            grid_spec=pltpu.PrefetchScalarGridSpec(
                num_scalar_prefetch=1, grid=(1,), in_specs=in_specs, out_specs=out_specs
            ),
            out_shape=outs,
            compiler_params=params(LIMIT["ring"]),
            cost_estimate=pl.CostEstimate(flops=10**6, bytes_accessed=10**6, transcendentals=0),
            name=kernel.__name__,
        )(place, *operands)

    sent = shape((SHARE, half), BF16)
    up_b, down_b = call(first_hop, [chunk(3, 1), chunk(-4, 1)], [sent, sent], [message, message], part, part)
    ends = []
    for group, up in enumerate((count // 2, count // 2 - 1)):
        starts = (up_a, down_a) if group == 0 else (up_b, down_b)
        for value, sign, hops in ((starts[0], 1, up), (starts[1], -1, count - 1 - up)):
            for k in range(hops - 1, -1, -1):
                value = ring(value, sign)
                if k > 0:
                    value = call(add_hop, [message, chunk(sign * k, group)], sent, message, value, part)
            ends.append(value)
    return call(
        finish,
        [pl.BlockSpec((SHARE, model), lambda i, at: (at[0], 0))]
        + [message] * 4
        + [pl.BlockSpec((1, model), lambda i, at: (0, 0))],
        shape((SHARE, model), BF16),
        pl.BlockSpec((SHARE, model), lambda i, at: (0, 0)),
        part,
        *ends,
        scale[None, :],
    )


def solution(mesh):
    return jax.shard_map(
        local,
        mesh=mesh,
        in_specs=(
            P("seq", "tp"),
            P("seq", "tp"),
            P("seq", "tp"),
            P("seq", "tp"),
            P("seq", "tp"),
            P("seq", "tp"),
            P(None, "tp"),
            P(None, "tp"),
            P(None, "tp"),
            P("tp"),
            P("tp"),
            P("tp", None),
            P(),
            P(),
        ),
        out_specs=P(("seq", "tp"), None),
        check_vma=False,
    )
```

time: 128 us -> 119 us (0.930)
  Pallas kernels: 29.9 us -> 54.5 us
  local copies, waits for them, and re-layouts: 25.8 us -> 1.38 us
  waiting for transfers between devices: 30.5 us -> 19.8 us
  starting transfers between devices: 35.8 us -> 41.8 us
  other arithmetic: 4.12 us -> 0.01 us
    unnamed x62 -> x16, local copies, waits for them, and re-layouts: 22.8 us -> 0.64 us
    pallas_call x6 -> x18, Pallas kernels: 24.6 us -> 45.8 us  [the longest x12 14.9 us: call(): pl.pallas_call(kernel, grid_spec=pltpu.PrefetchScalarGridSpec(num_scalar_...]
    ppermute x14, waiting for transfers between devices: 18.3 us -> 11.8 us  [ring(): lax.ppermute(value, 'tp', [(k, (k + step) % count) for k in range(count)])]
    ppermute x1, waiting for transfers between devices: 3.68 us -> 0.01 us  [local(): rim = lax.ppermute(tail, 'seq', [(k, k + 1) for k in range(seq - 1)])]
    pallas_call x1, Pallas kernels: 5.34 us -> 8.66 us  [local(): pl.pallas_call(inside, grid=(tiles,), in_specs=[tiled((TOK, TILE), 1), wh...]
    all_to_all x1, starting transfers between devices: 5.5 us -> 8.76 us  [local(): got = lax.all_to_all(pay, 'seq', 0, 0, tiled=True)]
    ppermute x14, starting transfers between devices: 23.2 us -> 26 us  [ring(): lax.ppermute(value, 'tp', [(k, (k + step) % count) for k in range(count)])]
    slice x4 -> x0, local copies, waits for them, and re-layouts: 2.75 us -> none  [the longest x1 0.77 us: local(): x_in[TOK - 16:]]
  transfers between devices with their start and end apart: 17 -> 17, of which waited for: 8 -> 7; matrix products, arithmetic and copies ran while one was open for 4% -> 1% of each run, Pallas kernels for 9% -> 34%
where the time goes in v2:
time: 119 us; the launch traced here: 118 us
  Pallas kernels  54.5 us (46%)
  starting transfers between devices  41.8 us (35%)
  waiting for transfers between devices  19.8 us (17%)
  local copies, waits for them, and re-layouts  1.38 us (1%)
    ppermute x14, starting transfers between devices, ring(): lax.ppermute(value, 'tp', [(k, (k + step) % count) for k in range(count)])  26 us
    pallas_call x12, Pallas kernels, call(): pl.pallas_call(kernel, grid_spec=pltpu.PrefetchScalarGridSpec(num_scalar_...  14.9 us
    ppermute x14, waiting for transfers between devices, ring(): lax.ppermute(value, 'tp', [(k, (k + step) % count) for k in range(count)])  11.8 us
    pallas_call x1, Pallas kernels, local(): pl.pallas_call(project, grid=(model // step_cols,), in_specs=[whole((TOK,...  11.2 us
    all_to_all x1, starting transfers between devices, local(): got = lax.all_to_all(pay, 'seq', 0, 0, tiled=True)  8.76 us
    pallas_call x1, Pallas kernels, local(): pl.pallas_call(inside, grid=(tiles,), in_specs=[tiled((TOK, TILE), 1), wh...  8.66 us
    pallas_call x1, Pallas kernels, local(): pl.pallas_call(scan_in, grid=(tiles,), in_specs=[tiled((TOK, TILE), 1), w...  8.32 us
    all_to_all x1, waiting for transfers between devices, local(): got = lax.all_to_all(pay, 'seq', 0, 0, tiled=True)  7.96 us
  transfers between devices with their start and end apart: 17, of which 7 were waited for; matrix products, arithmetic and copies ran while one was open for 1% of the time, Pallas kernels for 34%

profile of v2, /device:TPU:2, one launch (start us, length us, event | category | flops | bytes accessed | tf_op | source)
XLA Modules:
  0.0 117.7 jit_solution(6981868838379590839)
XLA Ops:
  0.0 1.4 %tail_rows.1 = bf16[16,1280]{1,0:T(8,128)(2,1)} custom-call(bf16[512,1024]{1,0:T(8,128)(2,1)} %x.5, bf16[512,128]{1,0:T(8,128)(2,1)} %b.5, bf16[512,128]{1,0:T(8,128)(2,1)} %c.5), custom_call_target="tpu_custom_call" | custom-call | tf_op jit(solution)/shard_map/tail_rows/pallas_call | solution.py:274
  1.4 1.9 %collective-permute-start = (bf16[16,1280]{1,0:T(8,128)(2,1)}, bf16[16,1280]{1,0:T(8,128)(2,1)S(1)}, u32[]{:S(2)}, u32[]{:S(2)}) collective-permute-start(bf16[16,1280]{1,0:T(8,128)(2,1)} %tail_rows.1), channel_id=1, source_target_pairs={{0,8},{8,16},{16,24},{24,32},{32,40},{40,48},{48,56},{56,64},{64,7... | collective-permute-start | bytes 122888 | tf_op jit(solution)/shard_map/ppermute | solution.py:283
  3.3 8.3 %scan_in.1 = (bf16[512,1024]{1,0:T(8,128)(2,1)}, bf16[512,128]{1,0:T(8,128)(2,1)}, bf16[512,128]{1,0:T(8,128)(2,1)}, f32[512,16]{1,0:T(8,128)}, f32[512,16]{1,0:...) custom-call(bf16[512,1024]{1,0:T(8,128)(2,1)} %x.5, bf16[512,128]{1,0:T(8,128)(2,1)} %b.5, bf16[512,128]{1,0:T(8,128)(2,1)} %c.5, ...), custom_call_target="tpu_custom_call" | custom-call | flops 1000000000 | bytes 4000000 | tf_op jit(solution)/shard_map/scan_in/pallas_call | solution.py:284
  12.3 2.8 %scan_edge.1 = (bf16[512,1024]{1,0:T(8,128)(2,1)}, bf16[512,128]{1,0:T(8,128)(2,1)}, bf16[512,128]{1,0:T(8,128)(2,1)}, f32[1024,128]{1,0:T(8,128)}, bf16[32,48,128]{2,1,0:T(8,128)(2,1)}) custom-call(bf16[16,1280]{1,0:T(8,128)(2,1)} %copy-done.4, bf16[512,1024]{1,0:T(8,128)(2,1)} %x.5, ...), custom_call_target="tpu_custom_call", output_to_operand_aliasing={{0}: (12, {}), {1}: (13, {}), {2}: (14, {})} | custom-call | tf_op jit(solution)/shard_map/scan_edge/pallas_call | solution.py:321
  15.1 8.8 %all-to-all-start = ((bf16[32,48,128]{2,1,0:T(8,128)(2,1)}), bf16[32,48,128]{2,1,0:T(8,128)(2,1)S(1)}, u32[]{:S(2)}, u32[]{:S(2)}) async-start(bf16[32,48,128]{2,1,0:T(8,128)(2,1)} %get-tuple-element.37), calls=%async_computation | async-start | bytes 786432 | tf_op jit(solution)/shard_map/all_to_all | solution.py:360
  24.6 8.0 %all-to-all-done.got = bf16[32,48,128]{2,1,0:T(8,128)(2,1)S(1)} async-done(((bf16[32,48,128]{2,1,0:T(8,128)(2,1)}), bf16[32,48,128]{2,1,0:T(8,128)(2,1)S(1)}, u32[]{:S(2)}, u32[]{:S(2)}) %all-to-all-start) | async-done | bytes 393248 | tf_op jit(solution)/shard_map/all_to_all | solution.py:360
  33.4 5.1 %all-to-all-start.1 = ((bf16[32,32,128]{2,1,0:T(8,128)(2,1)}), bf16[32,32,128]{2,1,0:T(8,128)(2,1)S(1)}, u32[]{:S(2)}, u32[]{:S(2)}) async-start(bf16[32,32,128]{2,1,0:T(8,128)(2,1)} %prefix.1), calls=%async_computation.1 | async-start | bytes 524288 | tf_op jit(solution)/shard_map/all_to_all | solution.py:391
  38.5 8.7 %inside.1 = (f32[512,1024]{1,0:T(8,128)}, f32[512,1024]{1,0:T(8,128)}) custom-call(bf16[512,1024]{1,0:T(8,128)(2,1)} %get-tuple-element.31.xs, bf16[512,128]{1,0:T(8,128)(2,1)} %get-tuple-element.32.bs, bf16[512,128]{1,0:T(8,128)(2,1)} %get-tuple-element.33.cs, f32[512,16]{1,0:T(8,128)} %get-tuple-element.25.run0.run1.run, f32[16,512]{1,0:T(8,128)} %bitcast.12, ...), custom_call_target="tpu_custom_call" | custom-call | flops 4000000000 | bytes 6000000 | tf_op jit(solution)/shard_map/inside/pallas_call | solution.py:361
  47.2 6.5 %norm_first.1 = (bf16[512,1024]{1,0:T(8,128)(2,1)}, bf16[64,2048]{1,0:T(8,128)(2,1)S(1)}, bf16[64,2048]{1,0:T(8,128)(2,1)S(1)}) custom-call(f32[512,1024]{1,0:T(8,128)} %get-tuple-element.34.y, f32[512,1024]{1,0:T(8,128)} %get-tuple-element.35.grow, bf16[512,128]{1,0:T(8,128)(2,1)S(1)} %copy-done.1, f32[512,16]{1,0:T(8,128)S(1)} %copy-done, ...), custom_call_target="tpu_custom_call" | custom-call | tf_op jit(solution)/shard_map/norm_first/pallas_call | solution.py:396
  53.7 2.0 %collective-permute-start.1 = (bf16[64,2048]{1,0:T(8,128)(2,1)S(1)}, bf16[64,2048]{1,0:T(8,128)(2,1)S(1)}, u32[]{:S(2)}, u32[]{:S(2)}) collective-permute-start(bf16[64,2048]{1,0:T(8,128)(2,1)S(1)} %get-tuple-element.39), channel_id=1, source_target_pairs={{0,1},{1,2},{2,3},{3,4},{4,5},{5,6},{6,7},{7,0},{8,9},{9,10},{10,1... | collective-permute-start | bytes 786440 | tf_op jit(solution)/shard_map/ppermute | solution.py:256
  55.7 11.2 %project.1.part.part_up.part_down.own = f32[512,4096]{1,0:T(8,128)} custom-call(bf16[512,1024]{1,0:T(8,128)(2,1)} %get-tuple-element.38.normed, bf16[1024,4096]{1,0:T(8,128)(2,1)} %weight.3), custom_call_target="tpu_custom_call" | custom-call | flops 20000000000 | bytes 16000000 | tf_op jit(solution)/shard_map/project/pallas_call | solution.py:420
  66.9 1.3 %first_hop.1 = (bf16[64,2048]{1,0:T(8,128)(2,1)S(1)}, bf16[64,2048]{1,0:T(8,128)(2,1)S(1)}) custom-call(s32[1]{0:T(128)} %bitcast.place, f32[512,4096]{1,0:T(8,128)} %project.1.part.part_up.part_down.own, f32[512,4096]{1,0:T(8,128)} %project.1.part.part_up.part_down.own), custom_call_target="tpu_custom_call" | custom-call | flops 1000000 | bytes 1000000 | tf_op jit(solution)/shard_map/first_hop/pallas_call | solution.py:441
  68.1 4.1 %collective-permute-start.11 = (bf16[64,2048]{1,0:T(8,128)(2,1)S(1)}, bf16[64,2048]{1,0:T(8,128)(2,1)S(1)}, u32[]{:S(2)}, u32[]{:S(2)}) collective-permute-start(bf16[64,2048]{1,0:T(8,128)(2,1)S(1)} %get-tuple-element.42), channel_id=1, source_target_pairs={{0,7},{1,0},{2,1},{3,2},{4,3},{5,4},{6,5},{7,6},{8,15},{9,8},{10,9... | collective-permute-start | bytes 786440 | tf_op jit(solution)/shard_map/ppermute | solution.py:256
  72.2 2.0 %collective-permute-start.5 = (bf16[64,2048]{1,0:T(8,128)(2,1)S(1)}, bf16[64,2048]{1,0:T(8,128)(2,1)S(1)}, u32[]{:S(2)}, u32[]{:S(2)}) collective-permute-start(bf16[64,2048]{1,0:T(8,128)(2,1)S(1)} %get-tuple-element.40), channel_id=1, source_target_pairs={{0,7},{1,0},{2,1},{3,2},{4,3},{5,4},{6,5},{7,6},{8,15},{9,8},{10,9... | collective-permute-start | bytes 786440 | tf_op jit(solution)/shard_map/ppermute | solution.py:256
  75.4 3.5 %collective-permute-done.11.came = bf16[64,2048]{1,0:T(8,128)(2,1)S(1)} collective-permute-done((bf16[64,2048]{1,0:T(8,128)(2,1)S(1)}, bf16[64,2048]{1,0:T(8,128)(2,1)S(1)}, u32[]{:S(2)}, u32[]{:S(2)}) %collective-permute-start.11) | collective-permute-done | bytes 262176 | tf_op jit(solution)/shard_map/ppermute | solution.py:256
  79.9 3.9 %collective-permute-start.12 = (bf16[64,2048]{1,0:T(8,128)(2,1)S(1)}, bf16[64,2048]{1,0:T(8,128)(2,1)S(1)}, u32[]{:S(2)}, u32[]{:S(2)}) collective-permute-start(bf16[64,2048]{1,0:T(8,128)(2,1)S(1)} %add_hop.17), channel_id=1, source_target_pairs={{0,7},{1,0},{2,1},{3,2},{4,3},{5,4},{6,5},{7,6},{8,15},{9,8},{10,9... | collective-permute-start | bytes 786440 | tf_op jit(solution)/shard_map/ppermute | solution.py:256
  85.5 3.8 %collective-permute-start.6 = (bf16[64,2048]{1,0:T(8,128)(2,1)S(1)}, bf16[64,2048]{1,0:T(8,128)(2,1)S(1)}, u32[]{:S(2)}, u32[]{:S(2)}) collective-permute-start(bf16[64,2048]{1,0:T(8,128)(2,1)S(1)} %add_hop.13), channel_id=1, source_target_pairs={{0,7},{1,0},{2,1},{3,2},{4,3},{5,4},{6,5},{7,6},{8,15},{9,8},{10,9... | collective-permute-start | bytes 786440 | tf_op jit(solution)/shard_map/ppermute | solution.py:256
  92.8 3.3 %collective-permute-start.13 = (bf16[64,2048]{1,0:T(8,128)(2,1)S(1)}, bf16[64,2048]{1,0:T(8,128)(2,1)S(1)}, u32[]{:S(2)}, u32[]{:S(2)}) collective-permute-start(bf16[64,2048]{1,0:T(8,128)(2,1)S(1)} %add_hop.18), channel_id=1, source_target_pairs={{0,7},{1,0},{2,1},{3,2},{4,3},{5,4},{6,5},{7,6},{8,15},{9,8},{10,9... | collective-permute-start | bytes 786440 | tf_op jit(solution)/shard_map/ppermute | solution.py:256
  97.2 3.2 %collective-permute-start.7 = (bf16[64,2048]{1,0:T(8,128)(2,1)S(1)}, bf16[64,2048]{1,0:T(8,128)(2,1)S(1)}, u32[]{:S(2)}, u32[]{:S(2)}) collective-permute-start(bf16[64,2048]{1,0:T(8,128)(2,1)S(1)} %add_hop.14), channel_id=1, source_target_pairs={{0,7},{1,0},{2,1},{3,2},{4,3},{5,4},{6,5},{7,6},{8,15},{9,8},{10,9... | collective-permute-start | bytes 786440 | tf_op jit(solution)/shard_map/ppermute | solution.py:256
  102.1 2.0 %collective-permute-done.3.came = bf16[64,2048]{1,0:T(8,128)(2,1)S(1)} collective-permute-done((bf16[64,2048]{1,0:T(8,128)(2,1)S(1)}, bf16[64,2048]{1,0:T(8,128)(2,1)S(1)}, u32[]{:S(2)}, u32[]{:S(2)}) %collective-permute-start.3) | collective-permute-done | bytes 262176 | tf_op jit(solution)/shard_map/ppermute | solution.py:256
  106.4 3.3 %collective-permute-start.14 = (bf16[64,2048]{1,0:T(8,128)(2,1)S(1)}, bf16[64,2048]{1,0:T(8,128)(2,1)S(1)}, u32[]{:S(2)}, u32[]{:S(2)}) collective-permute-start(bf16[64,2048]{1,0:T(8,128)(2,1)S(1)} %add_hop.19), channel_id=1, source_target_pairs={{0,7},{1,0},{2,1},{3,2},{4,3},{5,4},{6,5},{7,6},{8,15},{9,8},{10,9... | collective-permute-start | bytes 786440 | tf_op jit(solution)/shard_map/ppermute | solution.py:256
  109.7 2.4 %collective-permute-done.10.up_b = bf16[64,2048]{1,0:T(8,128)(2,1)S(1)} collective-permute-done((bf16[64,2048]{1,0:T(8,128)(2,1)S(1)}, bf16[64,2048]{1,0:T(8,128)(2,1)S(1)}, u32[]{:S(2)}, u32[]{:S(2)}) %collective-permute-start.10) | collective-permute-done | bytes 262176 | tf_op jit(solution)/shard_map/ppermute | solution.py:256
  112.2 2.8 %collective-permute-done.4.up_a = bf16[64,2048]{1,0:T(8,128)(2,1)S(1)} collective-permute-done((bf16[64,2048]{1,0:T(8,128)(2,1)S(1)}, bf16[64,2048]{1,0:T(8,128)(2,1)S(1)}, u32[]{:S(2)}, u32[]{:S(2)}) %collective-permute-start.4) | collective-permute-done | bytes 262176 | tf_op jit(solution)/shard_map/ppermute | solution.py:256
  115.0 2.7 %finish.1 = bf16[64,4096]{1,0:T(8,128)(2,1)} custom-call(s32[1]{0:T(128)} %bitcast.place, f32[512,4096]{1,0:T(8,128)} %project.1.part.part_up.part_down.own, bf16[64,2048]{1,0:T(8,128)(2,1)S(1)} %collective-permute-done.4.up_a, bf16[64,2048]{1,0:T(8,128)(2,1)S(1)} %collective-permute-done.7.down_a, bf16[64,2048]{1,0:T(8,128)(2,1)S(1)} %collective-permute-done.10.up_b, ...), custom_call_target="tpu_custom_call" | custom-call | flops 1000000 | bytes 1000000 | tf_op jit(solution)/shard_map/finish/pallas_call | solution.py:441
  (48 shorter events, 14.7 us)
Async XLA Ops:
  0.0 23.9 %copy-start.7 = (f32[16]{0:T(128)S(1)}, f32[16]{0:T(128)}, u32[]{:S(2)}) copy-start(f32[16]{0:T(128)} %param.23) | copy-start | bytes 196
  1.4 10.2 %collective-permute-start = (bf16[16,1280]{1,0:T(8,128)(2,1)}, bf16[16,1280]{1,0:T(8,128)(2,1)S(1)}, u32[]{:S(2)}, u32[]{:S(2)}) collective-permute-start(bf16[16,1280]{1,0:T(8,128)(2,1)} %tail_rows.1), channel_id=1, source_target_pairs={{0,8},{8,16},{16,24},{24,32},{32,40},{40,48},{48,56},{56,64},{64,7... | collective-permute-start | bytes 122888 | tf_op jit(solution)/shard_map/ppermute | solution.py:283
  15.1 32.1 %copy-start = (f32[512,16]{1,0:T(8,128)S(1)}, f32[512,16]{1,0:T(8,128)}, u32[]{:S(2)}) copy-start(f32[512,16]{1,0:T(8,128)} %get-tuple-element.25.run0.run1.run) | copy-start | bytes 98308
  15.1 32.1 %copy-start.1 = (bf16[512,128]{1,0:T(8,128)(2,1)S(1)}, bf16[512,128]{1,0:T(8,128)(2,1)}, u32[]{:S(2)}) copy-start(bf16[512,128]{1,0:T(8,128)(2,1)} %get-tuple-element.33.cs) | copy-start | bytes 393220
  15.1 32.1 %copy-start.2 = (f32[1024,128]{1,0:T(8,128)S(1)}, f32[1024,128]{1,0:T(8,128)}, u32[]{:S(2)}) copy-start(f32[1024,128]{1,0:T(8,128)} %get-tuple-element.36.first) | copy-start | bytes 1572868
  15.1 32.1 %copy-start.3 = (f32[1024]{0:T(1024)S(1)}, f32[1024]{0:T(1024)}, u32[]{:S(2)}) copy-start(f32[1024]{0:T(1024)} %param.24) | copy-start | bytes 12292
  15.1 17.5 %all-to-all-start = ((bf16[32,48,128]{2,1,0:T(8,128)(2,1)}), bf16[32,48,128]{2,1,0:T(8,128)(2,1)S(1)}, u32[]{:S(2)}, u32[]{:S(2)}) async-start(bf16[32,48,128]{2,1,0:T(8,128)(2,1)} %get-tuple-element.37), calls=%async_computation | async-start | bytes 786432 | tf_op jit(solution)/shard_map/all_to_all | solution.py:360
  33.4 13.8 %all-to-all-start.1 = ((bf16[32,32,128]{2,1,0:T(8,128)(2,1)}), bf16[32,32,128]{2,1,0:T(8,128)(2,1)S(1)}, u32[]{:S(2)}, u32[]{:S(2)}) async-start(bf16[32,32,128]{2,1,0:T(8,128)(2,1)} %prefix.1), calls=%async_computation.1 | async-start | bytes 524288 | tf_op jit(solution)/shard_map/all_to_all | solution.py:391
  53.7 20.5 %collective-permute-start.1 = (bf16[64,2048]{1,0:T(8,128)(2,1)S(1)}, bf16[64,2048]{1,0:T(8,128)(2,1)S(1)}, u32[]{:S(2)}, u32[]{:S(2)}) collective-permute-start(bf16[64,2048]{1,0:T(8,128)(2,1)S(1)} %get-tuple-element.39), channel_id=1, source_target_pairs={{0,1},{1,2},{2,3},{3,4},{4,5},{5,6},{6,7},{7,0},{8,9},{9,10},{10,1... | collective-permute-start | bytes 786440 | tf_op jit(solution)/shard_map/ppermute | solution.py:256
  68.1 10.7 %collective-permute-start.11 = (bf16[64,2048]{1,0:T(8,128)(2,1)S(1)}, bf16[64,2048]{1,0:T(8,128)(2,1)S(1)}, u32[]{:S(2)}, u32[]{:S(2)}) collective-permute-start(bf16[64,2048]{1,0:T(8,128)(2,1)S(1)} %get-tuple-element.42), channel_id=1, source_target_pairs={{0,7},{1,0},{2,1},{3,2},{4,3},{5,4},{6,5},{7,6},{8,15},{9,8},{10,9... | collective-permute-start | bytes 786440 | tf_op jit(solution)/shard_map/ppermute | solution.py:256
  72.2 12.3 %collective-permute-start.5 = (bf16[64,2048]{1,0:T(8,128)(2,1)S(1)}, bf16[64,2048]{1,0:T(8,128)(2,1)S(1)}, u32[]{:S(2)}, u32[]{:S(2)}) collective-permute-start(bf16[64,2048]{1,0:T(8,128)(2,1)S(1)} %get-tuple-element.40), channel_id=1, source_target_pairs={{0,7},{1,0},{2,1},{3,2},{4,3},{5,4},{6,5},{7,6},{8,15},{9,8},{10,9... | collective-permute-start | bytes 786440 | tf_op jit(solution)/shard_map/ppermute | solution.py:256
  74.2 15.2 %collective-permute-start.8 = (bf16[64,2048]{1,0:T(8,128)(2,1)S(1)}, bf16[64,2048]{1,0:T(8,128)(2,1)S(1)}, u32[]{:S(2)}, u32[]{:S(2)}) collective-permute-start(bf16[64,2048]{1,0:T(8,128)(2,1)S(1)} %get-tuple-element.41), channel_id=1, source_target_pairs={{0,1},{1,2},{2,3},{3,4},{4,5},{5,6},{6,7},{7,0},{8,9},{9,10},{10,1... | collective-permute-start | bytes 786440 | tf_op jit(solution)/shard_map/ppermute | solution.py:256
  75.3 15.2 %collective-permute-start.2 = (bf16[64,2048]{1,0:T(8,128)(2,1)S(1)}, bf16[64,2048]{1,0:T(8,128)(2,1)S(1)}, u32[]{:S(2)}, u32[]{:S(2)}) collective-permute-start(bf16[64,2048]{1,0:T(8,128)(2,1)S(1)} %add_hop.10), channel_id=1, source_target_pairs={{0,1},{1,2},{2,3},{3,4},{4,5},{5,6},{6,7},{7,0},{8,9},{9,10},{10,1... | collective-permute-start | bytes 786440 | tf_op jit(solution)/shard_map/ppermute | solution.py:256
  79.9 11.8 %collective-permute-start.12 = (bf16[64,2048]{1,0:T(8,128)(2,1)S(1)}, bf16[64,2048]{1,0:T(8,128)(2,1)S(1)}, u32[]{:S(2)}, u32[]{:S(2)}) collective-permute-start(bf16[64,2048]{1,0:T(8,128)(2,1)S(1)} %add_hop.17), channel_id=1, source_target_pairs={{0,7},{1,0},{2,1},{3,2},{4,3},{5,4},{6,5},{7,6},{8,15},{9,8},{10,9... | collective-permute-start | bytes 786440 | tf_op jit(solution)/shard_map/ppermute | solution.py:256
  85.5 10.6 %collective-permute-start.6 = (bf16[64,2048]{1,0:T(8,128)(2,1)S(1)}, bf16[64,2048]{1,0:T(8,128)(2,1)S(1)}, u32[]{:S(2)}, u32[]{:S(2)}) collective-permute-start(bf16[64,2048]{1,0:T(8,128)(2,1)S(1)} %add_hop.13), channel_id=1, source_target_pairs={{0,7},{1,0},{2,1},{3,2},{4,3},{5,4},{6,5},{7,6},{8,15},{9,8},{10,9... | collective-permute-start | bytes 786440 | tf_op jit(solution)/shard_map/ppermute | solution.py:256
  90.4 10.5 %collective-permute-start.9 = (bf16[64,2048]{1,0:T(8,128)(2,1)S(1)}, bf16[64,2048]{1,0:T(8,128)(2,1)S(1)}, u32[]{:S(2)}, u32[]{:S(2)}) collective-permute-start(bf16[64,2048]{1,0:T(8,128)(2,1)S(1)} %add_hop.15), channel_id=1, source_target_pairs={{0,1},{1,2},{2,3},{3,4},{4,5},{5,6},{6,7},{7,0},{8,9},{9,10},{10,1... | collective-permute-start | bytes 786440 | tf_op jit(solution)/shard_map/ppermute | solution.py:256
  91.6 12.5 %collective-permute-start.3 = (bf16[64,2048]{1,0:T(8,128)(2,1)S(1)}, bf16[64,2048]{1,0:T(8,128)(2,1)S(1)}, u32[]{:S(2)}, u32[]{:S(2)}) collective-permute-start(bf16[64,2048]{1,0:T(8,128)(2,1)S(1)} %add_hop.11), channel_id=1, source_target_pairs={{0,1},{1,2},{2,3},{3,4},{4,5},{5,6},{6,7},{7,0},{8,9},{9,10},{10,1... | collective-permute-start | bytes 786440 | tf_op jit(solution)/shard_map/ppermute | solution.py:256
  92.8 12.5 %collective-permute-start.13 = (bf16[64,2048]{1,0:T(8,128)(2,1)S(1)}, bf16[64,2048]{1,0:T(8,128)(2,1)S(1)}, u32[]{:S(2)}, u32[]{:S(2)}) collective-permute-start(bf16[64,2048]{1,0:T(8,128)(2,1)S(1)} %add_hop.18), channel_id=1, source_target_pairs={{0,7},{1,0},{2,1},{3,2},{4,3},{5,4},{6,5},{7,6},{8,15},{9,8},{10,9... | collective-permute-start | bytes 786440 | tf_op jit(solution)/shard_map/ppermute | solution.py:256
  97.2 12.6 %collective-permute-start.7 = (bf16[64,2048]{1,0:T(8,128)(2,1)S(1)}, bf16[64,2048]{1,0:T(8,128)(2,1)S(1)}, u32[]{:S(2)}, u32[]{:S(2)}) collective-permute-start(bf16[64,2048]{1,0:T(8,128)(2,1)S(1)} %add_hop.14), channel_id=1, source_target_pairs={{0,7},{1,0},{2,1},{3,2},{4,3},{5,4},{6,5},{7,6},{8,15},{9,8},{10,9... | collective-permute-start | bytes 786440 | tf_op jit(solution)/shard_map/ppermute | solution.py:256
  102.0 7.7 %copy-start.5 = (s32[4096]{0:T(1024)S(1)}, s32[4096]{0:T(1024)}, u32[]{:S(2)}) copy-start(s32[4096]{0:T(1024)} %param.27) | copy-start | bytes 49156
  102.0 7.7 %copy-start.6 = (s32[4096]{0:T(1024)S(1)}, s32[4096]{0:T(1024)}, u32[]{:S(2)}) copy-start(s32[4096]{0:T(1024)} %param.26) | copy-start | bytes 49156
  102.0 10.1 %collective-permute-start.10 = (bf16[64,2048]{1,0:T(8,128)(2,1)S(1)}, bf16[64,2048]{1,0:T(8,128)(2,1)S(1)}, u32[]{:S(2)}, u32[]{:S(2)}) collective-permute-start(bf16[64,2048]{1,0:T(8,128)(2,1)S(1)} %add_hop.16), channel_id=1, source_target_pairs={{0,1},{1,2},{2,3},{3,4},{4,5},{5,6},{6,7},{7,0},{8,9},{9,10},{10,1... | collective-permute-start | bytes 786440 | tf_op jit(solution)/shard_map/ppermute | solution.py:256
  105.2 9.8 %collective-permute-start.4 = (bf16[64,2048]{1,0:T(8,128)(2,1)S(1)}, bf16[64,2048]{1,0:T(8,128)(2,1)S(1)}, u32[]{:S(2)}, u32[]{:S(2)}) collective-permute-start(bf16[64,2048]{1,0:T(8,128)(2,1)S(1)} %add_hop.12), channel_id=1, source_target_pairs={{0,1},{1,2},{2,3},{3,4},{4,5},{5,6},{6,7},{7,0},{8,9},{9,10},{10,1... | collective-permute-start | bytes 786440 | tf_op jit(solution)/shard_map/ppermute | solution.py:256
  106.4 8.6 %collective-permute-start.14 = (bf16[64,2048]{1,0:T(8,128)(2,1)S(1)}, bf16[64,2048]{1,0:T(8,128)(2,1)S(1)}, u32[]{:S(2)}, u32[]{:S(2)}) collective-permute-start(bf16[64,2048]{1,0:T(8,128)(2,1)S(1)} %add_hop.19), channel_id=1, source_target_pairs={{0,7},{1,0},{2,1},{3,2},{4,3},{5,4},{6,5},{7,6},{8,15},{9,8},{10,9... | collective-permute-start | bytes 786440 | tf_op jit(solution)/shard_map/ppermute | solution.py:256
  (1 other events, 0.6 us)

commit v3 on v2

--- a/solution.py
+++ b/solution.py
@@ -1,3 +1,4 @@
+import functools
 import math
 
 import jax
@@ -20,8 +21,9 @@
 TILE = 256
 ROWS = 128
 SHARE = 64
+BEFORE = 3
 MIB = 1024 * 1024
-LIMIT = dict(tail_rows=58, scan_in=58, scan_edge=58, inside=58, prefix=16, norm_first=52, project=58, ring=50)
+LIMIT = dict(tail_rows=58, scan_in=58, scan_edge=58, inside=58, prefix=16, norm_first=50, project=50, ring=50)
 
 F32 = jnp.float32
 BF16 = jnp.bfloat16
@@ -183,16 +185,17 @@
     carried = dot(cs[...], start[...], ((1,), (1,)))
     gated = y[...] + grow[...] * carried
     meansq = jnp.sum(gated * gated, axis=1, keepdims=True) * (1.0 / CH)
-    rows = pl.ds(pl.multiple_of(step * ROWS, ROWS), ROWS)
-    normed_o[rows] = (gated * lax.rsqrt(meansq + 1e-05) * gain[...]).astype(BF16)
+    normed = (gated * lax.rsqrt(meansq + 1e-05) * gain[...]).astype(BF16)
+    place = lax.axis_index("tp")
+    for k in range(ROWS // SHARE):
+        at = lax.rem(step * (ROWS // SHARE) + k - place + 8 + BEFORE, 8) * SHARE
+        normed_o[pl.ds(pl.multiple_of(at, SHARE), SHARE)] = normed[k * SHARE : (k + 1) * SHARE]
 
     @pl.when(step == TOK // ROWS - 1)
     def _():
-        place = lax.axis_index("tp")
-        for k, distance in enumerate((4, 5)):
-            at = pl.multiple_of(lax.rem(place + distance, 8) * SHARE, SHARE)
-            picked[k * SHARE : (k + 1) * SHARE] = normed_o[pl.ds(at, SHARE)]
         fetch.wait()
+        picked[0:SHARE] = normed_o[rolled(4)]
+        picked[SHARE:] = normed_o[rolled(-3)]
         for k in range(held.shape[1] // 512):
             lanes = slice(k * 512, (k + 1) * 512)
             both = dot(picked[...], held[:, lanes]).astype(BF16)
@@ -200,20 +203,36 @@
             down_o[:, lanes] = both[SHARE:]
 
 
-def project(normed, weight, part_o):
-    part_o[...] = dot(normed[...], weight[...])
-
-
-def add_hop(place, came, part, out):
+def rolled(distance):
+    first = (distance + BEFORE) % 8 * SHARE
+    return slice(first, first + SHARE)
+
+
+def project_first(normed, weight, up_o, down_o, picked):
+    picked[0:SHARE] = normed[rolled(3)]
+    picked[SHARE:] = normed[rolled(-4)]
+    both = dot(picked[...], weight[...]).astype(BF16)
+    up_o[...] = both[:SHARE]
+    down_o[...] = both[SHARE:]
+
+
+def project_rest(lowest, normed, weight, *outs):
+    first = rolled(lowest).start
+    sums = dot(normed[first : first + len(outs) * SHARE], weight[...])
+    for k, out in enumerate(outs):
+        out[...] = sums[k * SHARE : (k + 1) * SHARE]
+
+
+def add_one(came, part, out):
     out[...] = (came[...].astype(F32) + part[...]).astype(BF16)
 
 
-def first_hop(place, part_up, part_down, up_o, down_o):
-    up_o[...] = part_up[...].astype(BF16)
-    down_o[...] = part_down[...].astype(BF16)
-
-
-def finish(place, own, up_a, down_a, up_b, down_b, scale, out):
+def add_two(came_up, came_down, part_up, part_down, up_o, down_o):
+    up_o[...] = (came_up[...].astype(F32) + part_up[...]).astype(BF16)
+    down_o[...] = (came_down[...].astype(F32) + part_down[...]).astype(BF16)
+
+
+def finish(own_a, own_b, up_a, down_a, up_b, down_b, scale, out):
     row = lax.broadcasted_iota(jnp.int32, (HAD_BLOCK, HAD_BLOCK), 0)
     column = lax.broadcasted_iota(jnp.int32, (HAD_BLOCK, HAD_BLOCK), 1)
     ones = row & column
@@ -222,9 +241,9 @@
     ones = ones ^ (ones >> 1)
     table = (1 - 2 * (ones & 1)).astype(F32).astype(BF16)
     half = up_a.shape[1]
-    for group, (up, down) in enumerate(((up_a, down_a), (up_b, down_b))):
+    for group, (own, up, down) in enumerate(((own_a, up_a, down_a), (own_b, up_b, down_b))):
         at = slice(group * half, (group + 1) * half)
-        total = (own[:, at] + up[...].astype(F32) + down[...].astype(F32)) * scale[:, at]
+        total = (own[...] + up[...].astype(F32) + down[...].astype(F32)) * scale[:, at]
         stacked = jnp.concatenate(
             [total[:, k * HAD_BLOCK : (k + 1) * HAD_BLOCK] for k in range(half // HAD_BLOCK)], 0
         )
@@ -379,6 +398,7 @@
         name="inside",
     )(xs, bs, cs, run, decay_t, step_t, jnp.repeat(d_skip, HEAD_DIM)[None, :], z_in)
 
+    got, y, grow = lax.optimization_barrier((got, y, grow))
     before = pl.pallas_call(
         prefix,
         grid=(1,),
@@ -417,60 +437,73 @@
         compiler_params=params(LIMIT["norm_first"]),
         name="norm_first",
     )(y, grow, cs, run, first, incoming, norm_gain[None, :], out_weight)
-    part = pl.pallas_call(
-        project,
-        grid=(model // step_cols,),
-        in_specs=[whole((TOK, CH)), tiled((CH, step_cols), 1)],
-        out_specs=tiled((TOK, step_cols), 1),
-        out_shape=shape((TOK, model), F32),
+    tiles = half // step_cols
+    up_b, down_b = pl.pallas_call(
+        project_first,
+        grid=(tiles,),
+        in_specs=[whole((TOK, CH)), pl.BlockSpec((CH, step_cols), lambda i: (0, i + tiles))],
+        out_specs=[tiled((SHARE, step_cols), 1)] * 2,
+        out_shape=[shape((SHARE, half), BF16)] * 2,
+        scratch_shapes=[pltpu.VMEM((2 * SHARE, CH), BF16)],
         compiler_params=params(LIMIT["project"]),
-        cost_estimate=pl.CostEstimate(flops=2 * 10**10, bytes_accessed=16 * 10**6, transcendentals=0),
-        name="project",
+        cost_estimate=pl.CostEstimate(flops=10, bytes_accessed=10, transcendentals=0),
+        name="project_first",
     )(normed, out_weight)
-
-    count = lax.axis_size("tp")
-    place = lax.axis_index("tp").astype(jnp.int32)[None]
+    parts = []
+    for group, lowest in enumerate((-2, -3)):
+        parts.append(
+            pl.pallas_call(
+                functools.partial(project_rest, lowest),
+                grid=(tiles,),
+                in_specs=[
+                    whole((TOK, CH)),
+                    pl.BlockSpec((CH, step_cols), lambda i, group=group: (0, i + group * tiles)),
+                ],
+                out_specs=[tiled((SHARE, step_cols), 1)] * 6,
+                out_shape=[shape((SHARE, half), F32)] * 6,
+                compiler_params=params(LIMIT["project"]),
+                cost_estimate=pl.CostEstimate(flops=10, bytes_accessed=10, transcendentals=0),
+                name="project_rest",
+            )(normed, out_weight)
+        )
     scale = jnp.exp2(out_exponent.astype(F32)) * out_sign.astype(F32)
 
-    def chunk(distance, group):
-        return pl.BlockSpec((SHARE, half), lambda i, at: (lax.rem(at[0] + distance + count, count), group))
-
-    message = pl.BlockSpec((SHARE, half), lambda i, at: (0, 0))
-
-    def call(kernel, in_specs, outs, out_specs, *operands):
+    def add(kernel, *operands):
+        sent = shape((SHARE, half), BF16)
         return pl.pallas_call(
             kernel,
-            grid_spec=pltpu.PrefetchScalarGridSpec(
-                num_scalar_prefetch=1, grid=(1,), in_specs=in_specs, out_specs=out_specs
-            ),
-            out_shape=outs,
+            in_specs=[pl.BlockSpec(memory_space=pltpu.VMEM)] * len(operands),
+            out_specs=[pl.BlockSpec(memory_space=pltpu.VMEM)] * (len(operands) // 2),
+            out_shape=[sent] * (len(operands) // 2),
             compiler_params=params(LIMIT["ring"]),
             cost_estimate=pl.CostEstimate(flops=10**6, bytes_accessed=10**6, transcendentals=0),
             name=kernel.__name__,
-        )(place, *operands)
-
-    sent = shape((SHARE, half), BF16)
-    up_b, down_b = call(first_hop, [chunk(3, 1), chunk(-4, 1)], [sent, sent], [message, message], part, part)
+        )(*operands)
+
     ends = []
-    for group, up in enumerate((count // 2, count // 2 - 1)):
-        starts = (up_a, down_a) if group == 0 else (up_b, down_b)
-        for value, sign, hops in ((starts[0], 1, up), (starts[1], -1, count - 1 - up)):
-            for k in range(hops - 1, -1, -1):
-                value = ring(value, sign)
-                if k > 0:
-                    value = call(add_hop, [message, chunk(sign * k, group)], sent, message, value, part)
-            ends.append(value)
-    return call(
+    for group, (up, down) in enumerate(((up_a, down_a), (up_b, down_b))):
+        lowest = (-2, -3)[group]
+        mine = {distance: parts[group][distance - lowest] for distance in range(lowest, lowest + 6)}
+        for hop in range(2):
+            up, down = ring(up, 1), ring(down, -1)
+            far = 3 - hop if group == 0 else 2 - hop
+            up, down = add(add_two, up, down, mine[far], mine[-(5 - far - 2 * hop)])
+        up, down = ring(up, 1), ring(down, -1)
+        if group == 0:
+            (up,) = add(add_one, up, mine[1])
+            up = ring(up, 1)
+        else:
+            (down,) = add(add_one, down, mine[-1])
+            down = ring(down, -1)
+        ends += [mine[0], up, down]
+    return pl.pallas_call(
         finish,
-        [pl.BlockSpec((SHARE, model), lambda i, at: (at[0], 0))]
-        + [message] * 4
-        + [pl.BlockSpec((1, model), lambda i, at: (0, 0))],
-        shape((SHARE, model), BF16),
-        pl.BlockSpec((SHARE, model), lambda i, at: (0, 0)),
-        part,
-        *ends,
-        scale[None, :],
-    )
+        in_specs=[pl.BlockSpec(memory_space=pltpu.VMEM)] * 7,
+        out_specs=pl.BlockSpec(memory_space=pltpu.VMEM),
+        out_shape=shape((SHARE, model), BF16),
+        compiler_params=params(LIMIT["ring"]),
+        name="finish",
+    )(ends[0], ends[3], ends[1], ends[2], ends[4], ends[5], scale[None, :])
 
 
 def solution(mesh):

time: 119 us -> 113 us (0.950)
  blocking collectives: 0 us -> 14.9 us
  Pallas kernels: 54.5 us -> 42.2 us
  waiting for transfers between devices: 19.8 us -> 15.5 us
  starting transfers between devices: 41.8 us -> 37.8 us
    all_to_all x0 -> x1, blocking collectives: none -> 14.9 us  [local(): lax.all_to_all(before, 'seq', 0, 0, tiled=True).reshape(CH, STATE)]
    pallas_call x13 -> x10, Pallas kernels: 26 us -> 15.5 us  [the longest x2 9.6 us: local(): pl.pallas_call(functools.partial(project_rest, lowest), grid=(tiles,), in...]
    all_to_all x1, waiting for transfers between devices: 7.96 us -> 0.01 us  [local(): got = lax.all_to_all(pay, 'seq', 0, 0, tiled=True)]
    all_to_all x1 -> x0, starting transfers between devices: 5.12 us -> none  [local(): lax.all_to_all(before, 'seq', 0, 0, tiled=True).reshape(CH, STATE)]
    ppermute x14, waiting for transfers between devices: 11.8 us -> 15.4 us  [ring(): lax.ppermute(value, 'tp', [(k, (k + step) % count) for k in range(count)])]
    ppermute x14, starting transfers between devices: 26 us -> 27.3 us  [ring(): lax.ppermute(value, 'tp', [(k, (k + step) % count) for k in range(count)])]
  transfers between devices with their start and end apart: 17 -> 16, of which waited for: 7 -> 7; matrix products, arithmetic and copies ran while one was open for 1% -> 1% of each run, Pallas kernels for 34% -> 24%
where the time goes in v3:
time: 113 us; the launch traced here: 112 us
  Pallas kernels  42.2 us (37%)
  starting transfers between devices  37.8 us (33%)
  waiting for transfers between devices  15.5 us (14%)
  blocking collectives  14.9 us (13%)
  local copies, waits for them, and re-layouts  1.39 us (1%)
    ppermute x14, starting transfers between devices, ring(): lax.ppermute(value, 'tp', [(k, (k + step) % count) for k in range(count)])  27.3 us
    ppermute x14, waiting for transfers between devices, ring(): lax.ppermute(value, 'tp', [(k, (k + step) % count) for k in range(count)])  15.4 us
    all_to_all x1, blocking collectives, local(): lax.all_to_all(before, 'seq', 0, 0, tiled=True).reshape(CH, STATE)  14.9 us
    pallas_call x2, Pallas kernels, local(): pl.pallas_call(functools.partial(project_rest, lowest), grid=(tiles,), in...  9.6 us
    pallas_call x1, Pallas kernels, local(): pl.pallas_call(inside, grid=(tiles,), in_specs=[tiled((TOK, TILE), 1), wh...  8.73 us
    all_to_all x1, starting transfers between devices, local(): got = lax.all_to_all(pay, 'seq', 0, 0, tiled=True)  8.61 us
    pallas_call x1, Pallas kernels, local(): pl.pallas_call(scan_in, grid=(tiles,), in_specs=[tiled((TOK, TILE), 1), w...  8.31 us
    pallas_call x1, Pallas kernels, local(): pl.pallas_call(norm_first, grid=(TOK // ROWS,), in_specs=[tiled((ROWS, CH...  5.42 us
  transfers between devices with their start and end apart: 16, of which 7 were waited for; matrix products, arithmetic and copies ran while one was open for 1% of the time, Pallas kernels for 24%

profile of v3, /device:TPU:2, one launch (start us, length us, event | category | flops | bytes accessed | tf_op | source)
XLA Modules:
  0.0 112.0 jit_solution(14027606057276155628)
XLA Ops:
  0.0 1.4 %tail_rows.1 = bf16[16,1280]{1,0:T(8,128)(2,1)} custom-call(bf16[512,1024]{1,0:T(8,128)(2,1)} %x.5, bf16[512,128]{1,0:T(8,128)(2,1)} %b.5, bf16[512,128]{1,0:T(8,128)(2,1)} %c.5), custom_call_target="tpu_custom_call" | custom-call | tf_op jit(solution)/shard_map/tail_rows/pallas_call | solution.py:293
  1.4 1.9 %collective-permute-start = (bf16[16,1280]{1,0:T(8,128)(2,1)}, bf16[16,1280]{1,0:T(8,128)(2,1)S(1)}, u32[]{:S(2)}, u32[]{:S(2)}) collective-permute-start(bf16[16,1280]{1,0:T(8,128)(2,1)} %tail_rows.1), channel_id=1, source_target_pairs={{0,8},{8,16},{16,24},{24,32},{32,40},{40,48},{48,56},{56,64},{64,7... | collective-permute-start | bytes 122888 | tf_op jit(solution)/shard_map/ppermute | solution.py:302
  3.3 8.3 %scan_in.1 = (bf16[512,1024]{1,0:T(8,128)(2,1)}, bf16[512,128]{1,0:T(8,128)(2,1)}, bf16[512,128]{1,0:T(8,128)(2,1)}, f32[512,16]{1,0:T(8,128)}, f32[512,16]{1,0:...) custom-call(bf16[512,1024]{1,0:T(8,128)(2,1)} %x.5, bf16[512,128]{1,0:T(8,128)(2,1)} %b.5, bf16[512,128]{1,0:T(8,128)(2,1)} %c.5, ...), custom_call_target="tpu_custom_call" | custom-call | flops 1000000000 | bytes 4000000 | tf_op jit(solution)/shard_map/scan_in/pallas_call | solution.py:303
  12.2 2.8 %scan_edge.1 = (bf16[512,1024]{1,0:T(8,128)(2,1)}, bf16[512,128]{1,0:T(8,128)(2,1)}, bf16[512,128]{1,0:T(8,128)(2,1)}, f32[1024,128]{1,0:T(8,128)}, bf16[32,48,128]{2,1,0:T(8,128)(2,1)}) custom-call(bf16[16,1280]{1,0:T(8,128)(2,1)} %copy-done.5, bf16[512,1024]{1,0:T(8,128)(2,1)} %x.5, ...), custom_call_target="tpu_custom_call", output_to_operand_aliasing={{0}: (12, {}), {1}: (13, {}), {2}: (14, {})} | custom-call | tf_op jit(solution)/shard_map/scan_edge/pallas_call | solution.py:340
  15.0 8.6 %all-to-all-start = ((bf16[32,48,128]{2,1,0:T(8,128)(2,1)}), bf16[32,48,128]{2,1,0:T(8,128)(2,1)S(1)}, u32[]{:S(2)}, u32[]{:S(2)}) async-start(bf16[32,48,128]{2,1,0:T(8,128)(2,1)} %get-tuple-element.54), calls=%async_computation | async-start | bytes 786432 | tf_op jit(solution)/shard_map/all_to_all | solution.py:379
  24.4 8.7 %inside.1 = (f32[512,1024]{1,0:T(8,128)}, f32[512,1024]{1,0:T(8,128)}) custom-call(bf16[512,1024]{1,0:T(8,128)(2,1)} %get-tuple-element.55.xs, bf16[512,128]{1,0:T(8,128)(2,1)} %get-tuple-element.56.bs, bf16[512,128]{1,0:T(8,128)(2,1)} %get-tuple-element.57.cs, f32[512,16]{1,0:T(8,128)} %get-tuple-element.48.run0.run1.run, f32[16,512]{1,0:T(8,128)} %bitcast.11, ...), custom_call_target="tpu_custom_call" | custom-call | flops 4000000000 | bytes 6000000 | tf_op jit(solution)/shard_map/inside/pallas_call | solution.py:380
  33.3 14.9 %all_to_all.10 = bf16[32,32,128]{2,1,0:T(8,128)(2,1)S(1)} all-to-all(bf16[32,32,128]{2,1,0:T(8,128)(2,1)S(1)} %prefix.1), channel_id=1, replica_groups=mesh['seq'=32,'tp'=8] {'seq'}, dimensions={0} | all-to-all | bytes 524288 | tf_op jit(solution)/shard_map/all_to_all | solution.py:411
  48.2 5.4 %norm_first.1 = (bf16[512,1024]{1,0:T(8,128)(2,1)S(1)}, bf16[64,2048]{1,0:T(8,128)(2,1)S(1)}, bf16[64,2048]{1,0:T(8,128)(2,1)S(1)}) custom-call(f32[512,1024]{1,0:T(8,128)} %get-tuple-element.60.y, f32[512,1024]{1,0:T(8,128)} %get-tuple-element.61.grow, bf16[512,128]{1,0:T(8,128)(2,1)S(1)} %copy-done.2, f32[512,16]{1,0:T(8,128)S(1)} %copy-done.1, ...), custom_call_target="tpu_custom_call" | custom-call | tf_op jit(solution)/shard_map/norm_first/pallas_call | solution.py:416
  53.6 3.9 %project_first.1 = (bf16[64,2048]{1,0:T(8,128)(2,1)S(1)}, bf16[64,2048]{1,0:T(8,128)(2,1)S(1)}) custom-call(bf16[512,1024]{1,0:T(8,128)(2,1)S(1)} %get-tuple-element.64.normed, bf16[1024,4096]{1,0:T(8,128)(2,1)} %weight.7), custom_call_target="tpu_custom_call" | custom-call | flops 10 | bytes 10 | tf_op jit(solution)/shard_map/project_first/pallas_call | solution.py:441
  57.6 2.0 %collective-permute-start.8 = (bf16[64,2048]{1,0:T(8,128)(2,1)S(1)}, bf16[64,2048]{1,0:T(8,128)(2,1)S(1)}, u32[]{:S(2)}, u32[]{:S(2)}) collective-permute-start(bf16[64,2048]{1,0:T(8,128)(2,1)S(1)} %get-tuple-element.78), channel_id=1, source_target_pairs={{0,1},{1,2},{2,3},{3,4},{4,5},{5,6},{6,7},{7,0},{8,9},{9,10},{10,1... | collective-permute-start | bytes 786440 | tf_op jit(solution)/shard_map/ppermute | solution.py:275
  59.6 4.0 %collective-permute-start.9 = (bf16[64,2048]{1,0:T(8,128)(2,1)S(1)}, bf16[64,2048]{1,0:T(8,128)(2,1)S(1)}, u32[]{:S(2)}, u32[]{:S(2)}) collective-permute-start(bf16[64,2048]{1,0:T(8,128)(2,1)S(1)} %get-tuple-element.79), channel_id=1, source_target_pairs={{0,7},{1,0},{2,1},{3,2},{4,3},{5,4},{6,5},{7,6},{8,15},{9,8},{10,9... | collective-permute-start | bytes 786440 | tf_op jit(solution)/shard_map/ppermute | solution.py:275
  63.6 3.2 %collective-permute-start.2 = (bf16[64,2048]{1,0:T(8,128)(2,1)S(1)}, bf16[64,2048]{1,0:T(8,128)(2,1)S(1)}, u32[]{:S(2)}, u32[]{:S(2)}) collective-permute-start(bf16[64,2048]{1,0:T(8,128)(2,1)S(1)} %get-tuple-element.68), channel_id=1, source_target_pairs={{0,7},{1,0},{2,1},{3,2},{4,3},{5,4},{6,5},{7,6},{8,15},{9,8},{10,9... | collective-permute-start | bytes 786440 | tf_op jit(solution)/shard_map/ppermute | solution.py:275
  66.8 4.8 %project_rest.3 = (f32[64,2048]{1,0:T(8,128)S(1)}, f32[64,2048]{1,0:T(8,128)S(1)}, f32[64,2048]{1,0:T(8,128)S(1)}, f32[64,2048]{1,0:T(8,128)S(1)}, f32[64,2048]{1,0:T(8,128)S(1)}, /*index=5*/f32[64,2048]{1,0:T(8,128)S(1)}) custom-call(bf16[512,1024]{1,0:T(8,128)(2,1)} %copy-done, bf16[1024,4096]{1,0:T(8,128)(2,1)} %weight.7), custom_call_target="tpu_custom_call" | custom-call | flops 10 | bytes 10 | tf_op jit(solution)/shard_map/project_rest/pallas_call | solution.py:455
  71.6 4.8 %project_rest.2 = (f32[64,2048]{1,0:T(8,128)S(1)}, f32[64,2048]{1,0:T(8,128)S(1)}, f32[64,2048]{1,0:T(8,128)S(1)}, f32[64,2048]{1,0:T(8,128)S(1)}, f32[64,2048]{1,0:T(8,128)S(1)}, /*index=5*/f32[64,2048]{1,0:T(8,128)S(1)}) custom-call(bf16[512,1024]{1,0:T(8,128)(2,1)} %copy-done, bf16[1024,4096]{1,0:T(8,128)(2,1)} %weight.7), custom_call_target="tpu_custom_call" | custom-call | flops 10 | bytes 10 | tf_op jit(solution)/shard_map/project_rest/pallas_call | solution.py:455
  76.7 3.2 %collective-permute-start.11 = (bf16[64,2048]{1,0:T(8,128)(2,1)S(1)}, bf16[64,2048]{1,0:T(8,128)(2,1)S(1)}, u32[]{:S(2)}, u32[]{:S(2)}) collective-permute-start(bf16[64,2048]{1,0:T(8,128)(2,1)S(1)} %get-tuple-element.83), channel_id=1, source_target_pairs={{0,7},{1,0},{2,1},{3,2},{4,3},{5,4},{6,5},{7,6},{8,15},{9,8},{10,9... | collective-permute-start | bytes 786440 | tf_op jit(solution)/shard_map/ppermute | solution.py:275
  80.1 3.2 %collective-permute-start.4 = (bf16[64,2048]{1,0:T(8,128)(2,1)S(1)}, bf16[64,2048]{1,0:T(8,128)(2,1)S(1)}, u32[]{:S(2)}, u32[]{:S(2)}) collective-permute-start(bf16[64,2048]{1,0:T(8,128)(2,1)S(1)} %get-tuple-element.72), channel_id=1, source_target_pairs={{0,7},{1,0},{2,1},{3,2},{4,3},{5,4},{6,5},{7,6},{8,15},{9,8},{10,9... | collective-permute-start | bytes 786440 | tf_op jit(solution)/shard_map/ppermute | solution.py:275
  83.3 3.8 %collective-permute-done.10.came_up = bf16[64,2048]{1,0:T(8,128)(2,1)S(1)} collective-permute-done((bf16[64,2048]{1,0:T(8,128)(2,1)S(1)}, bf16[64,2048]{1,0:T(8,128)(2,1)S(1)}, u32[]{:S(2)}, u32[]{:S(2)}) %collective-permute-start.10) | collective-permute-done | bytes 262176 | tf_op jit(solution)/shard_map/ppermute | solution.py:275
  87.2 3.3 %collective-permute-start.13 = (bf16[64,2048]{1,0:T(8,128)(2,1)S(1)}, bf16[64,2048]{1,0:T(8,128)(2,1)S(1)}, u32[]{:S(2)}, u32[]{:S(2)}) collective-permute-start(bf16[64,2048]{1,0:T(8,128)(2,1)S(1)} %get-tuple-element.87), channel_id=1, source_target_pairs={{0,7},{1,0},{2,1},{3,2},{4,3},{5,4},{6,5},{7,6},{8,15},{9,8},{10,9... | collective-permute-start | bytes 786440 | tf_op jit(solution)/shard_map/ppermute | solution.py:275
  92.6 3.2 %collective-permute-start.12 = (bf16[64,2048]{1,0:T(8,128)(2,1)S(1)}, bf16[64,2048]{1,0:T(8,128)(2,1)S(1)}, u32[]{:S(2)}, u32[]{:S(2)}) collective-permute-start(bf16[64,2048]{1,0:T(8,128)(2,1)S(1)} %get-tuple-element.86), channel_id=1, source_target_pairs={{0,1},{1,2},{2,3},{3,4},{4,5},{5,6},{6,7},{7,0},{8,9},{9,10},{10,1... | collective-permute-start | bytes 786440 | tf_op jit(solution)/shard_map/ppermute | solution.py:275
  96.3 1.6 %collective-permute-done.13.came = bf16[64,2048]{1,0:T(8,128)(2,1)S(1)} collective-permute-done((bf16[64,2048]{1,0:T(8,128)(2,1)S(1)}, bf16[64,2048]{1,0:T(8,128)(2,1)S(1)}, u32[]{:S(2)}, u32[]{:S(2)}) %collective-permute-start.13) | collective-permute-done | bytes 262176 | tf_op jit(solution)/shard_map/ppermute | solution.py:275
  97.9 3.8 %collective-permute-start.14 = (bf16[64,2048]{1,0:T(8,128)(2,1)S(1)}, bf16[64,2048]{1,0:T(8,128)(2,1)S(1)}, u32[]{:S(2)}, u32[]{:S(2)}) collective-permute-start(bf16[64,2048]{1,0:T(8,128)(2,1)S(1)} %add_one.3), channel_id=1, source_target_pairs={{0,7},{1,0},{2,1},{3,2},{4,3},{5,4},{6,5},{7,6},{8,15},{9,8},{10,9... | collective-permute-start | bytes 786440 | tf_op jit(solution)/shard_map/ppermute | solution.py:275
  102.8 4.9 %collective-permute-done.12.up_b = bf16[64,2048]{1,0:T(8,128)(2,1)S(1)} collective-permute-done((bf16[64,2048]{1,0:T(8,128)(2,1)S(1)}, bf16[64,2048]{1,0:T(8,128)(2,1)S(1)}, u32[]{:S(2)}, u32[]{:S(2)}) %collective-permute-start.12) | collective-permute-done | bytes 262176 | tf_op jit(solution)/shard_map/ppermute | solution.py:275
  107.7 2.8 %collective-permute-done.6.up_a = bf16[64,2048]{1,0:T(8,128)(2,1)S(1)} collective-permute-done((bf16[64,2048]{1,0:T(8,128)(2,1)S(1)}, bf16[64,2048]{1,0:T(8,128)(2,1)S(1)}, u32[]{:S(2)}, u32[]{:S(2)}) %collective-permute-start.6) | collective-permute-done | bytes 262176 | tf_op jit(solution)/shard_map/ppermute | solution.py:275
  110.5 1.5 %finish.1 = bf16[64,4096]{1,0:T(8,128)(2,1)} custom-call(f32[64,2048]{1,0:T(8,128)S(1)} %get-tuple-element.65.own_a, f32[64,2048]{1,0:T(8,128)S(1)} %get-tuple-element.66.own_b, bf16[64,2048]{1,0:T(8,128)(2,1)S(1)} %collective-permute-done.6.up_a, bf16[64,2048]{1,0:T(8,128)(2,1)S(1)} %collective-permute-done.7.down_a, ...), custom_call_target="tpu_custom_call" | custom-call | tf_op jit(solution)/shard_map/finish/pallas_call | solution.py:499
  (46 shorter events, 5.6 us)
Async XLA Ops:
  1.4 10.2 %collective-permute-start = (bf16[16,1280]{1,0:T(8,128)(2,1)}, bf16[16,1280]{1,0:T(8,128)(2,1)S(1)}, u32[]{:S(2)}, u32[]{:S(2)}) collective-permute-start(bf16[16,1280]{1,0:T(8,128)(2,1)} %tail_rows.1), channel_id=1, source_target_pairs={{0,8},{8,16},{16,24},{24,32},{32,40},{40,48},{48,56},{56,64},{64,7... | collective-permute-start | bytes 122888 | tf_op jit(solution)/shard_map/ppermute | solution.py:302
  12.2 11.4 %copy-start.8 = (f32[16]{0:T(128)S(1)}, f32[16]{0:T(128)}, u32[]{:S(2)}) copy-start(f32[16]{0:T(128)} %param.23) | copy-start | bytes 196
  15.0 18.1 %all-to-all-start = ((bf16[32,48,128]{2,1,0:T(8,128)(2,1)}), bf16[32,48,128]{2,1,0:T(8,128)(2,1)S(1)}, u32[]{:S(2)}, u32[]{:S(2)}) async-start(bf16[32,48,128]{2,1,0:T(8,128)(2,1)} %get-tuple-element.54), calls=%async_computation | async-start | bytes 786432 | tf_op jit(solution)/shard_map/all_to_all | solution.py:379
  24.4 23.8 %copy-start.1 = (f32[512,16]{1,0:T(8,128)S(1)}, f32[512,16]{1,0:T(8,128)}, u32[]{:S(2)}) copy-start(f32[512,16]{1,0:T(8,128)} %get-tuple-element.48.run0.run1.run) | copy-start | bytes 98308
  24.4 23.8 %copy-start.2 = (bf16[512,128]{1,0:T(8,128)(2,1)S(1)}, bf16[512,128]{1,0:T(8,128)(2,1)}, u32[]{:S(2)}) copy-start(bf16[512,128]{1,0:T(8,128)(2,1)} %get-tuple-element.57.cs) | copy-start | bytes 393220
  24.4 23.8 %copy-start.3 = (f32[1024,128]{1,0:T(8,128)S(1)}, f32[1024,128]{1,0:T(8,128)}, u32[]{:S(2)}) copy-start(f32[1024,128]{1,0:T(8,128)} %get-tuple-element.62.first) | copy-start | bytes 1572868
  24.4 23.8 %copy-start.4 = (f32[1024]{0:T(1024)S(1)}, f32[1024]{0:T(1024)}, u32[]{:S(2)}) copy-start(f32[1024]{0:T(1024)} %param.24) | copy-start | bytes 12292
  53.6 4.0 %copy-start = (bf16[512,1024]{1,0:T(8,128)(2,1)}, bf16[512,1024]{1,0:T(8,128)(2,1)S(1)}, u32[]{:S(2)}) copy-start(bf16[512,1024]{1,0:T(8,128)(2,1)S(1)} %get-tuple-element.64.normed) | copy-start | bytes 3145732
  57.6 18.9 %collective-permute-start.8 = (bf16[64,2048]{1,0:T(8,128)(2,1)S(1)}, bf16[64,2048]{1,0:T(8,128)(2,1)S(1)}, u32[]{:S(2)}, u32[]{:S(2)}) collective-permute-start(bf16[64,2048]{1,0:T(8,128)(2,1)S(1)} %get-tuple-element.78), channel_id=1, source_target_pairs={{0,1},{1,2},{2,3},{3,4},{4,5},{5,6},{6,7},{7,0},{8,9},{9,10},{10,1... | collective-permute-start | bytes 786440 | tf_op jit(solution)/shard_map/ppermute | solution.py:275
  59.6 16.9 %collective-permute-start.9 = (bf16[64,2048]{1,0:T(8,128)(2,1)S(1)}, bf16[64,2048]{1,0:T(8,128)(2,1)S(1)}, u32[]{:S(2)}, u32[]{:S(2)}) collective-permute-start(bf16[64,2048]{1,0:T(8,128)(2,1)S(1)} %get-tuple-element.79), channel_id=1, source_target_pairs={{0,7},{1,0},{2,1},{3,2},{4,3},{5,4},{6,5},{7,6},{8,15},{9,8},{10,9... | collective-permute-start | bytes 786440 | tf_op jit(solution)/shard_map/ppermute | solution.py:275
  63.6 16.3 %collective-permute-start.1 = (bf16[64,2048]{1,0:T(8,128)(2,1)S(1)}, bf16[64,2048]{1,0:T(8,128)(2,1)S(1)}, u32[]{:S(2)}, u32[]{:S(2)}) collective-permute-start(bf16[64,2048]{1,0:T(8,128)(2,1)S(1)} %get-tuple-element.67), channel_id=1, source_target_pairs={{0,1},{1,2},{2,3},{3,4},{4,5},{5,6},{6,7},{7,0},{8,9},{9,10},{10,1... | collective-permute-start | bytes 786440 | tf_op jit(solution)/shard_map/ppermute | solution.py:275
  63.6 16.3 %collective-permute-start.2 = (bf16[64,2048]{1,0:T(8,128)(2,1)S(1)}, bf16[64,2048]{1,0:T(8,128)(2,1)S(1)}, u32[]{:S(2)}, u32[]{:S(2)}) collective-permute-start(bf16[64,2048]{1,0:T(8,128)(2,1)S(1)} %get-tuple-element.68), channel_id=1, source_target_pairs={{0,7},{1,0},{2,1},{3,2},{4,3},{5,4},{6,5},{7,6},{8,15},{9,8},{10,9... | collective-permute-start | bytes 786440 | tf_op jit(solution)/shard_map/ppermute | solution.py:275
  76.6 10.5 %collective-permute-start.10 = (bf16[64,2048]{1,0:T(8,128)(2,1)S(1)}, bf16[64,2048]{1,0:T(8,128)(2,1)S(1)}, u32[]{:S(2)}, u32[]{:S(2)}) collective-permute-start(bf16[64,2048]{1,0:T(8,128)(2,1)S(1)} %get-tuple-element.82), channel_id=1, source_target_pairs={{0,1},{1,2},{2,3},{3,4},{4,5},{5,6},{6,7},{7,0},{8,9},{9,10},{10,1... | collective-permute-start | bytes 786440 | tf_op jit(solution)/shard_map/ppermute | solution.py:275
  76.7 10.4 %collective-permute-start.11 = (bf16[64,2048]{1,0:T(8,128)(2,1)S(1)}, bf16[64,2048]{1,0:T(8,128)(2,1)S(1)}, u32[]{:S(2)}, u32[]{:S(2)}) collective-permute-start(bf16[64,2048]{1,0:T(8,128)(2,1)S(1)} %get-tuple-element.83), channel_id=1, source_target_pairs={{0,7},{1,0},{2,1},{3,2},{4,3},{5,4},{6,5},{7,6},{8,15},{9,8},{10,9... | collective-permute-start | bytes 786440 | tf_op jit(solution)/shard_map/ppermute | solution.py:275
  80.0 11.1 %collective-permute-start.3 = (bf16[64,2048]{1,0:T(8,128)(2,1)S(1)}, bf16[64,2048]{1,0:T(8,128)(2,1)S(1)}, u32[]{:S(2)}, u32[]{:S(2)}) collective-permute-start(bf16[64,2048]{1,0:T(8,128)(2,1)S(1)} %get-tuple-element.71), channel_id=1, source_target_pairs={{0,1},{1,2},{2,3},{3,4},{4,5},{5,6},{6,7},{7,0},{8,9},{9,10},{10,1... | collective-permute-start | bytes 786440 | tf_op jit(solution)/shard_map/ppermute | solution.py:275
  80.1 12.2 %collective-permute-start.4 = (bf16[64,2048]{1,0:T(8,128)(2,1)S(1)}, bf16[64,2048]{1,0:T(8,128)(2,1)S(1)}, u32[]{:S(2)}, u32[]{:S(2)}) collective-permute-start(bf16[64,2048]{1,0:T(8,128)(2,1)S(1)} %get-tuple-element.72), channel_id=1, source_target_pairs={{0,7},{1,0},{2,1},{3,2},{4,3},{5,4},{6,5},{7,6},{8,15},{9,8},{10,9... | collective-permute-start | bytes 786440 | tf_op jit(solution)/shard_map/ppermute | solution.py:275
  87.2 15.5 %copy-start.6 = (s32[4096]{0:T(1024)S(1)}, s32[4096]{0:T(1024)}, u32[]{:S(2)}) copy-start(s32[4096]{0:T(1024)} %param.27) | copy-start | bytes 49156
  87.2 15.5 %copy-start.7 = (s32[4096]{0:T(1024)S(1)}, s32[4096]{0:T(1024)}, u32[]{:S(2)}) copy-start(s32[4096]{0:T(1024)} %param.26) | copy-start | bytes 49156
  87.2 10.7 %collective-permute-start.13 = (bf16[64,2048]{1,0:T(8,128)(2,1)S(1)}, bf16[64,2048]{1,0:T(8,128)(2,1)S(1)}, u32[]{:S(2)}, u32[]{:S(2)}) collective-permute-start(bf16[64,2048]{1,0:T(8,128)(2,1)S(1)} %get-tuple-element.87), channel_id=1, source_target_pairs={{0,7},{1,0},{2,1},{3,2},{4,3},{5,4},{6,5},{7,6},{8,15},{9,8},{10,9... | collective-permute-start | bytes 786440 | tf_op jit(solution)/shard_map/ppermute | solution.py:275
  92.4 10.0 %collective-permute-start.5 = (bf16[64,2048]{1,0:T(8,128)(2,1)S(1)}, bf16[64,2048]{1,0:T(8,128)(2,1)S(1)}, u32[]{:S(2)}, u32[]{:S(2)}) collective-permute-start(bf16[64,2048]{1,0:T(8,128)(2,1)S(1)} %get-tuple-element.75), channel_id=1, source_target_pairs={{0,1},{1,2},{2,3},{3,4},{4,5},{5,6},{6,7},{7,0},{8,9},{9,10},{10,1... | collective-permute-start | bytes 786440 | tf_op jit(solution)/shard_map/ppermute | solution.py:275
  92.6 15.1 %collective-permute-start.12 = (bf16[64,2048]{1,0:T(8,128)(2,1)S(1)}, bf16[64,2048]{1,0:T(8,128)(2,1)S(1)}, u32[]{:S(2)}, u32[]{:S(2)}) collective-permute-start(bf16[64,2048]{1,0:T(8,128)(2,1)S(1)} %get-tuple-element.86), channel_id=1, source_target_pairs={{0,1},{1,2},{2,3},{3,4},{4,5},{5,6},{6,7},{7,0},{8,9},{9,10},{10,1... | collective-permute-start | bytes 786440 | tf_op jit(solution)/shard_map/ppermute | solution.py:275
  95.8 11.8 %collective-permute-start.7 = (bf16[64,2048]{1,0:T(8,128)(2,1)S(1)}, bf16[64,2048]{1,0:T(8,128)(2,1)S(1)}, u32[]{:S(2)}, u32[]{:S(2)}) collective-permute-start(bf16[64,2048]{1,0:T(8,128)(2,1)S(1)} %get-tuple-element.77), channel_id=1, source_target_pairs={{0,7},{1,0},{2,1},{3,2},{4,3},{5,4},{6,5},{7,6},{8,15},{9,8},{10,9... | collective-permute-start | bytes 786440 | tf_op jit(solution)/shard_map/ppermute | solution.py:275
  97.9 9.7 %collective-permute-start.14 = (bf16[64,2048]{1,0:T(8,128)(2,1)S(1)}, bf16[64,2048]{1,0:T(8,128)(2,1)S(1)}, u32[]{:S(2)}, u32[]{:S(2)}) collective-permute-start(bf16[64,2048]{1,0:T(8,128)(2,1)S(1)} %add_one.3), channel_id=1, source_target_pairs={{0,7},{1,0},{2,1},{3,2},{4,3},{5,4},{6,5},{7,6},{8,15},{9,8},{10,9... | collective-permute-start | bytes 786440 | tf_op jit(solution)/shard_map/ppermute | solution.py:275
  102.4 8.1 %collective-permute-start.6 = (bf16[64,2048]{1,0:T(8,128)(2,1)S(1)}, bf16[64,2048]{1,0:T(8,128)(2,1)S(1)}, u32[]{:S(2)}, u32[]{:S(2)}) collective-permute-start(bf16[64,2048]{1,0:T(8,128)(2,1)S(1)} %add_one.2), channel_id=1, source_target_pairs={{0,1},{1,2},{2,3},{3,4},{4,5},{5,6},{6,7},{7,0},{8,9},{9,10},{10,1... | collective-permute-start | bytes 786440 | tf_op jit(solution)/shard_map/ppermute | solution.py:275
  (1 other events, 0.6 us)

commit v4 on v3

--- a/solution.py
+++ b/solution.py
@@ -23,7 +23,8 @@
 SHARE = 64
 BEFORE = 3
 MIB = 1024 * 1024
-LIMIT = dict(tail_rows=58, scan_in=58, scan_edge=58, inside=58, prefix=16, norm_first=50, project=50, ring=50)
+LIMIT = dict(tail_rows=58, scan_in=58, scan_edge=58, inside=58, prefix=16, norm_project=44, ring=24)
+PART = jnp.float32
 
 F32 = jnp.float32
 BF16 = jnp.bfloat16
@@ -168,63 +169,55 @@
     grow_o[...] = dot(jnp.exp(run[...]), head_rows(tile * per_tile, TILE), precision=HIGHEST) * gate
 
 
-def norm_first(y, grow, cs, run, first, incoming, gain, weight, normed_o, up_o, down_o, start, held, picked, sem):
-    step = pl.program_id(0)
-    fetch = pltpu.make_async_copy(weight.at[:, 0 : held.shape[1]], held, sem)
-
-    @pl.when(step == 0)
-    def _():
-        fetch.start()
-        start[...] = incoming[...]
-
-    @pl.when(step == SPAN // ROWS)
-    def _():
-        decay = jnp.exp(head_columns(0, CH, run[7:8]))
-        start[...] = (decay * incoming[...].astype(F32) + first[...]).astype(BF16)
-
-    carried = dot(cs[...], start[...], ((1,), (1,)))
-    gated = y[...] + grow[...] * carried
-    meansq = jnp.sum(gated * gated, axis=1, keepdims=True) * (1.0 / CH)
-    normed = (gated * lax.rsqrt(meansq + 1e-05) * gain[...]).astype(BF16)
-    place = lax.axis_index("tp")
-    for k in range(ROWS // SHARE):
-        at = lax.rem(step * (ROWS // SHARE) + k - place + 8 + BEFORE, 8) * SHARE
-        normed_o[pl.ds(pl.multiple_of(at, SHARE), SHARE)] = normed[k * SHARE : (k + 1) * SHARE]
-
-    @pl.when(step == TOK // ROWS - 1)
-    def _():
-        fetch.wait()
-        picked[0:SHARE] = normed_o[rolled(4)]
-        picked[SHARE:] = normed_o[rolled(-3)]
-        for k in range(held.shape[1] // 512):
-            lanes = slice(k * 512, (k + 1) * 512)
-            both = dot(picked[...], held[:, lanes]).astype(BF16)
-            up_o[:, lanes] = both[:SHARE]
-            down_o[:, lanes] = both[SHARE:]
-
-
 def rolled(distance):
     first = (distance + BEFORE) % 8 * SHARE
     return slice(first, first + SHARE)
 
 
-def project_first(normed, weight, up_o, down_o, picked):
-    picked[0:SHARE] = normed[rolled(3)]
-    picked[SHARE:] = normed[rolled(-4)]
-    both = dot(picked[...], weight[...]).astype(BF16)
-    up_o[...] = both[:SHARE]
-    down_o[...] = both[SHARE:]
-
-
-def project_rest(lowest, normed, weight, *outs):
-    first = rolled(lowest).start
-    sums = dot(normed[first : first + len(outs) * SHARE], weight[...])
-    for k, out in enumerate(outs):
-        out[...] = sums[k * SHARE : (k + 1) * SHARE]
-
-
-def add_one(came, part, out):
+def norm_project(y, grow, cs, run, first, incoming, gain, weight, *refs):
+    outs, (normed, held, y_s, grow_s, sems) = refs[:-5], refs[-5:]
+    half = outs[0].shape[1]
+    steps = TOK // ROWS
+    copies = []
+    for step in range(steps):
+        rows = slice(step * ROWS, (step + 1) * ROWS)
+        copies.append(pltpu.make_async_copy(y.at[rows], y_s.at[rows], sems.at[2 * step]))
+        copies.append(pltpu.make_async_copy(grow.at[rows], grow_s.at[rows], sems.at[2 * step + 1]))
+    for group in range(2):
+        lanes = slice(group * half, (group + 1) * half)
+        copies.append(pltpu.make_async_copy(weight.at[:, lanes], held.at[:, lanes], sems.at[2 * steps + group]))
+    for copy in copies:
+        copy.start()
+    place = lax.axis_index("tp")
+    start = incoming[...]
+    for step in range(steps):
+        if step == SPAN // ROWS:
+            decay = jnp.exp(head_columns(0, CH, run[SPAN - 1 : SPAN]))
+            start = (decay * incoming[...].astype(F32) + first[...]).astype(BF16)
+        rows = slice(step * ROWS, (step + 1) * ROWS)
+        carried = dot(cs[rows], start, ((1,), (1,)))
+        copies[2 * step].wait()
+        copies[2 * step + 1].wait()
+        gated = y_s[rows] + grow_s[rows] * carried
+        meansq = jnp.sum(gated * gated, axis=1, keepdims=True) * (1.0 / CH)
+        result = (gated * lax.rsqrt(meansq + 1e-05) * gain[...]).astype(BF16)
+        for k in range(ROWS // SHARE):
+            at = lax.rem(step * (ROWS // SHARE) + k - place + 8 + BEFORE, 8) * SHARE
+            normed[pl.ds(pl.multiple_of(at, SHARE), SHARE)] = result[k * SHARE : (k + 1) * SHARE]
+    for group in range(2):
+        copies[2 * steps + group].wait()
+        targets = [(outs[8 * group], 4 - group), (outs[8 * group + 1], -3 - group)]
+        targets += [(outs[8 * group + 2 + k], k - 2 - group) for k in range(6)]
+        for j in range(half // 512):
+            lanes = slice(group * half + j * 512, group * half + (j + 1) * 512)
+            sums = dot(normed[...], held[:, lanes])
+            for out, distance in targets:
+                out[:, j * 512 : (j + 1) * 512] = sums[rolled(distance)].astype(out.dtype)
+
+
+def add_last(came, came_end, part, own, out, total):
     out[...] = (came[...].astype(F32) + part[...]).astype(BF16)
+    total[...] = own[...] + came_end[...].astype(F32)
 
 
 def add_two(came_up, came_down, part_up, part_down, up_o, down_o):
@@ -232,7 +225,7 @@
     down_o[...] = (came_down[...].astype(F32) + part_down[...]).astype(BF16)
 
 
-def finish(own_a, own_b, up_a, down_a, up_b, down_b, scale, out):
+def finish(total_a, total_b, came_a, came_b, scale, out):
     row = lax.broadcasted_iota(jnp.int32, (HAD_BLOCK, HAD_BLOCK), 0)
     column = lax.broadcasted_iota(jnp.int32, (HAD_BLOCK, HAD_BLOCK), 1)
     ones = row & column
@@ -240,10 +233,10 @@
     ones = ones ^ (ones >> 2)
     ones = ones ^ (ones >> 1)
     table = (1 - 2 * (ones & 1)).astype(F32).astype(BF16)
-    half = up_a.shape[1]
-    for group, (own, up, down) in enumerate(((own_a, up_a, down_a), (own_b, up_b, down_b))):
+    half = came_a.shape[1]
+    for group, (total, came) in enumerate(((total_a, came_a), (total_b, came_b))):
         at = slice(group * half, (group + 1) * half)
-        total = (own[...] + up[...].astype(F32) + down[...].astype(F32)) * scale[:, at]
+        total = (total[...] + came[...].astype(F32)) * scale[:, at]
         stacked = jnp.concatenate(
             [total[:, k * HAD_BLOCK : (k + 1) * HAD_BLOCK] for k in range(half // HAD_BLOCK)], 0
         )
@@ -412,69 +405,38 @@
 
     model = out_weight.shape[1]
     half = model // 2
-    step_cols = 512
-    normed, up_a, down_a = pl.pallas_call(
-        norm_first,
-        grid=(TOK // ROWS,),
-        in_specs=[
-            tiled((ROWS, CH), 0),
-            tiled((ROWS, CH), 0),
-            tiled((ROWS, STATE), 0),
-            block((8, HEADS_LOCAL), SPAN // 8 - 1, 0),
-            whole((CH, STATE)),
-            whole((CH, STATE)),
-            whole((1, CH)),
-            pl.BlockSpec(memory_space=pl.ANY),
-        ],
-        out_specs=[whole((TOK, CH)), whole((SHARE, half)), whole((SHARE, half))],
-        out_shape=[shape((TOK, CH), BF16), shape((SHARE, half), BF16), shape((SHARE, half), BF16)],
+    vmem = pl.BlockSpec(memory_space=pltpu.VMEM)
+    anywhere = pl.BlockSpec(memory_space=pl.ANY)
+    outs = ([shape((SHARE, half), BF16)] * 2 + [shape((SHARE, half), PART)] * 6) * 2
+    sums = pl.pallas_call(
+        norm_project,
+        in_specs=[anywhere] * 2 + [vmem] * 5 + [anywhere],
+        out_specs=[vmem] * 16,
+        out_shape=outs,
         scratch_shapes=[
-            pltpu.VMEM((CH, STATE), BF16),
-            pltpu.VMEM((CH, half), BF16),
-            pltpu.VMEM((2 * SHARE, CH), BF16),
-            pltpu.SemaphoreType.DMA,
-        ],
-        compiler_params=params(LIMIT["norm_first"]),
-        name="norm_first",
+            pltpu.VMEM((TOK, CH), BF16),
+            pltpu.VMEM((CH, model), BF16),
+            pltpu.VMEM((TOK, CH), F32),
+            pltpu.VMEM((TOK, CH), F32),
+            pltpu.SemaphoreType.DMA((2 * (TOK // ROWS) + 2,)),
+        ],
+        compiler_params=params(LIMIT["norm_project"]),
+        cost_estimate=pl.CostEstimate(flops=10**9, bytes_accessed=10**7, transcendentals=0),
+        name="norm_project",
     )(y, grow, cs, run, first, incoming, norm_gain[None, :], out_weight)
-    tiles = half // step_cols
-    up_b, down_b = pl.pallas_call(
-        project_first,
-        grid=(tiles,),
-        in_specs=[whole((TOK, CH)), pl.BlockSpec((CH, step_cols), lambda i: (0, i + tiles))],
-        out_specs=[tiled((SHARE, step_cols), 1)] * 2,
-        out_shape=[shape((SHARE, half), BF16)] * 2,
-        scratch_shapes=[pltpu.VMEM((2 * SHARE, CH), BF16)],
-        compiler_params=params(LIMIT["project"]),
-        cost_estimate=pl.CostEstimate(flops=10, bytes_accessed=10, transcendentals=0),
-        name="project_first",
-    )(normed, out_weight)
-    parts = []
-    for group, lowest in enumerate((-2, -3)):
-        parts.append(
-            pl.pallas_call(
-                functools.partial(project_rest, lowest),
-                grid=(tiles,),
-                in_specs=[
-                    whole((TOK, CH)),
-                    pl.BlockSpec((CH, step_cols), lambda i, group=group: (0, i + group * tiles)),
-                ],
-                out_specs=[tiled((SHARE, step_cols), 1)] * 6,
-                out_shape=[shape((SHARE, half), F32)] * 6,
-                compiler_params=params(LIMIT["project"]),
-                cost_estimate=pl.CostEstimate(flops=10, bytes_accessed=10, transcendentals=0),
-                name="project_rest",
-            )(normed, out_weight)
-        )
+    up_a, down_a = sums[0:2]
+    up_b, down_b = sums[8:10]
+    parts = [sums[2:8], sums[10:16]]
     scale = jnp.exp2(out_exponent.astype(F32)) * out_sign.astype(F32)
 
-    def add(kernel, *operands):
-        sent = shape((SHARE, half), BF16)
+    sent = shape((SHARE, half), BF16)
+
+    def add(kernel, second, *operands):
         return pl.pallas_call(
             kernel,
-            in_specs=[pl.BlockSpec(memory_space=pltpu.VMEM)] * len(operands),
-            out_specs=[pl.BlockSpec(memory_space=pltpu.VMEM)] * (len(operands) // 2),
-            out_shape=[sent] * (len(operands) // 2),
+            in_specs=[vmem] * 4,
+            out_specs=[vmem] * 2,
+            out_shape=[sent, second],
             compiler_params=params(LIMIT["ring"]),
             cost_estimate=pl.CostEstimate(flops=10**6, bytes_accessed=10**6, transcendentals=0),
             name=kernel.__name__,
@@ -487,23 +449,20 @@
         for hop in range(2):
             up, down = ring(up, 1), ring(down, -1)
             far = 3 - hop if group == 0 else 2 - hop
-            up, down = add(add_two, up, down, mine[far], mine[-(5 - far - 2 * hop)])
+            up, down = add(add_two, sent, up, down, mine[far], mine[-(5 - far - 2 * hop)])
         up, down = ring(up, 1), ring(down, -1)
-        if group == 0:
-            (up,) = add(add_one, up, mine[1])
-            up = ring(up, 1)
-        else:
-            (down,) = add(add_one, down, mine[-1])
-            down = ring(down, -1)
-        ends += [mine[0], up, down]
+        sign = 1 if group == 0 else -1
+        came, came_end = (up, down) if group == 0 else (down, up)
+        value, total = add(add_last, shape((SHARE, half), F32), came, came_end, mine[sign], mine[0])
+        ends += [total, ring(value, sign)]
     return pl.pallas_call(
         finish,
-        in_specs=[pl.BlockSpec(memory_space=pltpu.VMEM)] * 7,
-        out_specs=pl.BlockSpec(memory_space=pltpu.VMEM),
+        in_specs=[vmem] * 5,
+        out_specs=vmem,
         out_shape=shape((SHARE, model), BF16),
         compiler_params=params(LIMIT["ring"]),
         name="finish",
-    )(ends[0], ends[3], ends[1], ends[2], ends[4], ends[5], scale[None, :])
+    )(ends[0], ends[2], ends[1], ends[3], scale[None, :])
 
 
 def solution(mesh):

time: 113 us -> 108 us (0.956)
  Pallas kernels: 42.2 us -> 31.6 us
  waiting for transfers between devices: 15.5 us -> 24.6 us
  starting transfers between devices: 37.8 us -> 35.2 us
    pallas_call x11 -> x8, Pallas kernels: 20.9 us -> 10.2 us  [the longest x1 8.26 us: local(): pl.pallas_call(norm_project, in_specs=[anywhere] * 2 + [vmem] * 5 + [anyw...]
    ppermute x14, waiting for transfers between devices: 15.4 us -> 24.6 us  [ring(): lax.ppermute(value, 'tp', [(k, (k + step) % count) for k in range(count)])]
    ppermute x14, starting transfers between devices: 27.3 us -> 24.7 us  [ring(): lax.ppermute(value, 'tp', [(k, (k + step) % count) for k in range(count)])]
  transfers between devices with their start and end apart: 16 -> 16, of which waited for: 7 -> 11; matrix products, arithmetic and copies ran while one was open for 1% -> 1% of each run, Pallas kernels for 24% -> 16%
where the time goes in v4:
time: 108 us
  starting transfers between devices  35.2 us (33%)
  Pallas kernels  31.6 us (29%)
  waiting for transfers between devices  24.6 us (23%)
  blocking collectives  14.9 us (14%)
  local copies, waits for them, and re-layouts  1.38 us (1%)
    ppermute x14, starting transfers between devices, ring(): lax.ppermute(value, 'tp', [(k, (k + step) % count) for k in range(count)])  24.7 us
    ppermute x14, waiting for transfers between devices, ring(): lax.ppermute(value, 'tp', [(k, (k + step) % count) for k in range(count)])  24.6 us
    all_to_all x1, blocking collectives, local(): lax.all_to_all(before, 'seq', 0, 0, tiled=True).reshape(CH, STATE)  14.9 us
    pallas_call x1, Pallas kernels, local(): pl.pallas_call(inside, grid=(tiles,), in_specs=[tiled((TOK, TILE), 1), wh...  8.74 us
    all_to_all x1, starting transfers between devices, local(): got = lax.all_to_all(pay, 'seq', 0, 0, tiled=True)  8.61 us
    pallas_call x1, Pallas kernels, local(): pl.pallas_call(scan_in, grid=(tiles,), in_specs=[tiled((TOK, TILE), 1), w...  8.32 us
    pallas_call x1, Pallas kernels, local(): pl.pallas_call(norm_project, in_specs=[anywhere] * 2 + [vmem] * 5 + [anyw...  8.26 us
    pallas_call x1, Pallas kernels, local(): pl.pallas_call(scan_edge, grid=(1,), in_specs=[whole((16, CH + 2 * STATE)...  2.8 us
  transfers between devices with their start and end apart: 16, of which 11 were waited for; matrix products, arithmetic and copies ran while one was open for 1% of the time, Pallas kernels for 16%

profile of v4, /device:TPU:2, one launch (start us, length us, event | category | flops | bytes accessed | tf_op | source)
XLA Modules:
  0.0 107.8 jit_solution(15846143319244393159)
XLA Ops:
  1.4 1.9 %collective-permute-start = (bf16[16,1280]{1,0:T(8,128)(2,1)}, bf16[16,1280]{1,0:T(8,128)(2,1)S(1)}, u32[]{:S(2)}, u32[]{:S(2)}) collective-permute-start(bf16[16,1280]{1,0:T(8,128)(2,1)} %tail_rows.1), channel_id=1, source_target_pairs={{0,8},{8,16},{16,24},{24,32},{32,40},{40,48},{48,56},{56,64},{64,7... | collective-permute-start | bytes 122888 | tf_op jit(solution)/shard_map/ppermute | solution.py:295
  3.3 8.3 %scan_in.1 = (bf16[512,1024]{1,0:T(8,128)(2,1)}, bf16[512,128]{1,0:T(8,128)(2,1)}, bf16[512,128]{1,0:T(8,128)(2,1)}, f32[512,16]{1,0:T(8,128)}, f32[512,16]{1,0:...) custom-call(bf16[512,1024]{1,0:T(8,128)(2,1)} %x.5, bf16[512,128]{1,0:T(8,128)(2,1)} %b.5, bf16[512,128]{1,0:T(8,128)(2,1)} %c.5, ...), custom_call_target="tpu_custom_call" | custom-call | flops 1000000000 | bytes 4000000 | tf_op jit(solution)/shard_map/scan_in/pallas_call | solution.py:296
  12.3 2.8 %scan_edge.1 = (bf16[512,1024]{1,0:T(8,128)(2,1)}, bf16[512,128]{1,0:T(8,128)(2,1)}, bf16[512,128]{1,0:T(8,128)(2,1)}, f32[1024,128]{1,0:T(8,128)}, bf16[32,48,128]{2,1,0:T(8,128)(2,1)}) custom-call(bf16[16,1280]{1,0:T(8,128)(2,1)} %copy-done.4, bf16[512,1024]{1,0:T(8,128)(2,1)} %x.5, ...), custom_call_target="tpu_custom_call", output_to_operand_aliasing={{0}: (12, {}), {1}: (13, {}), {2}: (14, {})} | custom-call | tf_op jit(solution)/shard_map/scan_edge/pallas_call | solution.py:333
  15.1 8.6 %all-to-all-start = ((bf16[32,48,128]{2,1,0:T(8,128)(2,1)}), bf16[32,48,128]{2,1,0:T(8,128)(2,1)S(1)}, u32[]{:S(2)}, u32[]{:S(2)}) async-start(bf16[32,48,128]{2,1,0:T(8,128)(2,1)} %get-tuple-element.57), calls=%async_computation | async-start | bytes 786432 | tf_op jit(solution)/shard_map/all_to_all | solution.py:372
  24.4 8.7 %inside.1 = (f32[512,1024]{1,0:T(8,128)}, f32[512,1024]{1,0:T(8,128)}) custom-call(bf16[512,1024]{1,0:T(8,128)(2,1)} %get-tuple-element.58.xs, bf16[512,128]{1,0:T(8,128)(2,1)} %get-tuple-element.59.bs, bf16[512,128]{1,0:T(8,128)(2,1)} %get-tuple-element.60.cs, f32[512,16]{1,0:T(8,128)} %get-tuple-element.51.run0.run1.run, f32[16,512]{1,0:T(8,128)} %bitcast.11, ...), custom_call_target="tpu_custom_call" | custom-call | flops 4000000000 | bytes 6000000 | tf_op jit(solution)/shard_map/inside/pallas_call | solution.py:373
  33.3 14.9 %all_to_all.10 = bf16[32,32,128]{2,1,0:T(8,128)(2,1)S(1)} all-to-all(bf16[32,32,128]{2,1,0:T(8,128)(2,1)S(1)} %prefix.1), channel_id=1, replica_groups=mesh['seq'=32,'tp'=8] {'seq'}, dimensions={0} | all-to-all | bytes 524288 | tf_op jit(solution)/shard_map/all_to_all | solution.py:404
  48.2 8.3 %norm_project.1 = (bf16[64,2048]{1,0:T(8,128)(2,1)S(1)}, bf16[64,2048]{1,0:T(8,128)(2,1)S(1)}, f32[64,2048]{1,0:T(8,128)S(1)}, f32[64,2048]{1,0:T(8,128)S(1)}, f...) custom-call(f32[512,1024]{1,0:T(8,128)} %get-tuple-element.63.y, ...), custom_call_target="tpu_custom_call" | custom-call | flops 1000000000 | bytes 10000000 | tf_op jit(solution)/shard_map/norm_project/pallas_call | solution.py:411
  56.5 2.0 %collective-permute-start.7 = (bf16[64,2048]{1,0:T(8,128)(2,1)S(1)}, bf16[64,2048]{1,0:T(8,128)(2,1)S(1)}, u32[]{:S(2)}, u32[]{:S(2)}) collective-permute-start(bf16[64,2048]{1,0:T(8,128)(2,1)S(1)} %get-tuple-element.80), channel_id=1, source_target_pairs={{0,1},{1,2},{2,3},{3,4},{4,5},{5,6},{6,7},{7,0},{8,9},{9,10},{10,1... | collective-permute-start | bytes 786440 | tf_op jit(solution)/shard_map/ppermute | solution.py:268
  58.5 4.0 %collective-permute-start.8 = (bf16[64,2048]{1,0:T(8,128)(2,1)S(1)}, bf16[64,2048]{1,0:T(8,128)(2,1)S(1)}, u32[]{:S(2)}, u32[]{:S(2)}) collective-permute-start(bf16[64,2048]{1,0:T(8,128)(2,1)S(1)} %get-tuple-element.81), channel_id=1, source_target_pairs={{0,7},{1,0},{2,1},{3,2},{4,3},{5,4},{6,5},{7,6},{8,15},{9,8},{10,9... | collective-permute-start | bytes 786440 | tf_op jit(solution)/shard_map/ppermute | solution.py:268
  62.5 3.2 %collective-permute-start.2 = (bf16[64,2048]{1,0:T(8,128)(2,1)S(1)}, bf16[64,2048]{1,0:T(8,128)(2,1)S(1)}, u32[]{:S(2)}, u32[]{:S(2)}) collective-permute-start(bf16[64,2048]{1,0:T(8,128)(2,1)S(1)} %get-tuple-element.68), channel_id=1, source_target_pairs={{0,7},{1,0},{2,1},{3,2},{4,3},{5,4},{6,5},{7,6},{8,15},{9,8},{10,9... | collective-permute-start | bytes 786440 | tf_op jit(solution)/shard_map/ppermute | solution.py:268
  65.8 3.7 %collective-permute-done.7.came_up = bf16[64,2048]{1,0:T(8,128)(2,1)S(1)} collective-permute-done((bf16[64,2048]{1,0:T(8,128)(2,1)S(1)}, bf16[64,2048]{1,0:T(8,128)(2,1)S(1)}, u32[]{:S(2)}, u32[]{:S(2)}) %collective-permute-start.7) | collective-permute-done | bytes 262176 | tf_op jit(solution)/shard_map/ppermute | solution.py:268
  69.6 3.4 %collective-permute-start.10 = (bf16[64,2048]{1,0:T(8,128)(2,1)S(1)}, bf16[64,2048]{1,0:T(8,128)(2,1)S(1)}, u32[]{:S(2)}, u32[]{:S(2)}) collective-permute-start(bf16[64,2048]{1,0:T(8,128)(2,1)S(1)} %get-tuple-element.85), channel_id=1, source_target_pairs={{0,7},{1,0},{2,1},{3,2},{4,3},{5,4},{6,5},{7,6},{8,15},{9,8},{10,9... | collective-permute-start | bytes 786440 | tf_op jit(solution)/shard_map/ppermute | solution.py:268
  73.0 1.8 %collective-permute-done.1.came_up = bf16[64,2048]{1,0:T(8,128)(2,1)S(1)} collective-permute-done((bf16[64,2048]{1,0:T(8,128)(2,1)S(1)}, bf16[64,2048]{1,0:T(8,128)(2,1)S(1)}, u32[]{:S(2)}, u32[]{:S(2)}) %collective-permute-start.1) | collective-permute-done | bytes 262176 | tf_op jit(solution)/shard_map/ppermute | solution.py:268
  75.3 3.4 %collective-permute-start.4 = (bf16[64,2048]{1,0:T(8,128)(2,1)S(1)}, bf16[64,2048]{1,0:T(8,128)(2,1)S(1)}, u32[]{:S(2)}, u32[]{:S(2)}) collective-permute-start(bf16[64,2048]{1,0:T(8,128)(2,1)S(1)} %get-tuple-element.72), channel_id=1, source_target_pairs={{0,7},{1,0},{2,1},{3,2},{4,3},{5,4},{6,5},{7,6},{8,15},{9,8},{10,9... | collective-permute-start | bytes 786440 | tf_op jit(solution)/shard_map/ppermute | solution.py:268
  78.7 1.7 %collective-permute-done.10.came_down = bf16[64,2048]{1,0:T(8,128)(2,1)S(1)} collective-permute-done((bf16[64,2048]{1,0:T(8,128)(2,1)S(1)}, bf16[64,2048]{1,0:T(8,128)(2,1)S(1)}, u32[]{:S(2)}, u32[]{:S(2)}) %collective-permute-start.10) | collective-permute-done | bytes 262176 | tf_op jit(solution)/shard_map/ppermute | solution.py:268
  80.4 3.1 %collective-permute-done.9.came_up = bf16[64,2048]{1,0:T(8,128)(2,1)S(1)} collective-permute-done((bf16[64,2048]{1,0:T(8,128)(2,1)S(1)}, bf16[64,2048]{1,0:T(8,128)(2,1)S(1)}, u32[]{:S(2)}, u32[]{:S(2)}) %collective-permute-start.9) | collective-permute-done | bytes 262176 | tf_op jit(solution)/shard_map/ppermute | solution.py:268
  86.7 1.9 %collective-permute-start.5 = (bf16[64,2048]{1,0:T(8,128)(2,1)S(1)}, bf16[64,2048]{1,0:T(8,128)(2,1)S(1)}, u32[]{:S(2)}, u32[]{:S(2)}) collective-permute-start(bf16[64,2048]{1,0:T(8,128)(2,1)S(1)} %get-tuple-element.75), channel_id=1, source_target_pairs={{0,1},{1,2},{2,3},{3,4},{4,5},{5,6},{6,7},{7,0},{8,9},{9,10},{10,1... | collective-permute-start | bytes 786440 | tf_op jit(solution)/shard_map/ppermute | solution.py:268
  90.0 2.4 %collective-permute-done.11.came = bf16[64,2048]{1,0:T(8,128)(2,1)S(1)} collective-permute-done((bf16[64,2048]{1,0:T(8,128)(2,1)S(1)}, bf16[64,2048]{1,0:T(8,128)(2,1)S(1)}, u32[]{:S(2)}, u32[]{:S(2)}) %collective-permute-start.11) | collective-permute-done | bytes 262176 | tf_op jit(solution)/shard_map/ppermute | solution.py:268
  92.4 2.3 %collective-permute-done.12.came_end = bf16[64,2048]{1,0:T(8,128)(2,1)S(1)} collective-permute-done((bf16[64,2048]{1,0:T(8,128)(2,1)S(1)}, bf16[64,2048]{1,0:T(8,128)(2,1)S(1)}, u32[]{:S(2)}, u32[]{:S(2)}) %collective-permute-start.12) | collective-permute-done | bytes 262176 | tf_op jit(solution)/shard_map/ppermute | solution.py:268
  95.5 2.3 %collective-permute-done.5.came = bf16[64,2048]{1,0:T(8,128)(2,1)S(1)} collective-permute-done((bf16[64,2048]{1,0:T(8,128)(2,1)S(1)}, bf16[64,2048]{1,0:T(8,128)(2,1)S(1)}, u32[]{:S(2)}, u32[]{:S(2)}) %collective-permute-start.5) | collective-permute-done | bytes 262176 | tf_op jit(solution)/shard_map/ppermute | solution.py:268
  98.2 2.0 %collective-permute-start.13 = (bf16[64,2048]{1,0:T(8,128)(2,1)S(1)}, bf16[64,2048]{1,0:T(8,128)(2,1)S(1)}, u32[]{:S(2)}, u32[]{:S(2)}) collective-permute-start(bf16[64,2048]{1,0:T(8,128)(2,1)S(1)} %get-tuple-element.93), channel_id=1, source_target_pairs={{0,1},{1,2},{2,3},{3,4},{4,5},{5,6},{6,7},{7,0},{8,9},{9,10},{10,1... | collective-permute-start | bytes 786440 | tf_op jit(solution)/shard_map/ppermute | solution.py:268
  100.2 2.0 %collective-permute-done.14.came_b = bf16[64,2048]{1,0:T(8,128)(2,1)S(1)} collective-permute-done((bf16[64,2048]{1,0:T(8,128)(2,1)S(1)}, bf16[64,2048]{1,0:T(8,128)(2,1)S(1)}, u32[]{:S(2)}, u32[]{:S(2)}) %collective-permute-start.14) | collective-permute-done | bytes 262176 | tf_op jit(solution)/shard_map/ppermute | solution.py:268
  102.2 4.2 %collective-permute-done.13.came_a = bf16[64,2048]{1,0:T(8,128)(2,1)S(1)} collective-permute-done((bf16[64,2048]{1,0:T(8,128)(2,1)S(1)}, bf16[64,2048]{1,0:T(8,128)(2,1)S(1)}, u32[]{:S(2)}, u32[]{:S(2)}) %collective-permute-start.13) | collective-permute-done | bytes 262176 | tf_op jit(solution)/shard_map/ppermute | solution.py:268
  106.4 1.4 %finish.1 = bf16[64,4096]{1,0:T(8,128)(2,1)} custom-call(f32[64,2048]{1,0:T(8,128)S(1)} %get-tuple-element.79.total_a, f32[64,2048]{1,0:T(8,128)S(1)} %get-tuple-element.92.total_b, bf16[64,2048]{1,0:T(8,128)(2,1)S(1)} %collective-permute-done.13.came_a, bf16[64,2048]{1,0:T(8,128)(2,1)S(1)} %collective-permute-done.14.came_b, f32[1,4096]{1,0:T(1,128)S(1)} %bitcast.6), custom_call_target="tpu_custom_call" | custom-call | tf_op jit(solution)/shard_map/finish/pallas_call | solution.py:458
  (41 shorter events, 9.3 us)
Async XLA Ops:
  1.4 10.2 %collective-permute-start = (bf16[16,1280]{1,0:T(8,128)(2,1)}, bf16[16,1280]{1,0:T(8,128)(2,1)S(1)}, u32[]{:S(2)}, u32[]{:S(2)}) collective-permute-start(bf16[16,1280]{1,0:T(8,128)(2,1)} %tail_rows.1), channel_id=1, source_target_pairs={{0,8},{8,16},{16,24},{24,32},{32,40},{40,48},{48,56},{56,64},{64,7... | collective-permute-start | bytes 122888 | tf_op jit(solution)/shard_map/ppermute | solution.py:295
  11.6 0.6 copy-start.4
  12.3 11.4 %copy-start.7 = (f32[16]{0:T(128)S(1)}, f32[16]{0:T(128)}, u32[]{:S(2)}) copy-start(f32[16]{0:T(128)} %param.23) | copy-start | bytes 196
  15.1 18.1 %all-to-all-start = ((bf16[32,48,128]{2,1,0:T(8,128)(2,1)}), bf16[32,48,128]{2,1,0:T(8,128)(2,1)S(1)}, u32[]{:S(2)}, u32[]{:S(2)}) async-start(bf16[32,48,128]{2,1,0:T(8,128)(2,1)} %get-tuple-element.57), calls=%async_computation | async-start | bytes 786432 | tf_op jit(solution)/shard_map/all_to_all | solution.py:372
  24.4 23.8 %copy-start = (f32[512,16]{1,0:T(8,128)S(1)}, f32[512,16]{1,0:T(8,128)}, u32[]{:S(2)}) copy-start(f32[512,16]{1,0:T(8,128)} %get-tuple-element.51.run0.run1.run) | copy-start | bytes 98308
  24.4 23.8 %copy-start.1 = (bf16[512,128]{1,0:T(8,128)(2,1)S(1)}, bf16[512,128]{1,0:T(8,128)(2,1)}, u32[]{:S(2)}) copy-start(bf16[512,128]{1,0:T(8,128)(2,1)} %get-tuple-element.60.cs) | copy-start | bytes 393220
  24.4 23.8 %copy-start.2 = (f32[1024,128]{1,0:T(8,128)S(1)}, f32[1024,128]{1,0:T(8,128)}, u32[]{:S(2)}) copy-start(f32[1024,128]{1,0:T(8,128)} %get-tuple-element.65.first) | copy-start | bytes 1572868
  24.4 23.8 %copy-start.3 = (f32[1024]{0:T(1024)S(1)}, f32[1024]{0:T(1024)}, u32[]{:S(2)}) copy-start(f32[1024]{0:T(1024)} %param.24) | copy-start | bytes 12292
  56.5 13.0 %collective-permute-start.7 = (bf16[64,2048]{1,0:T(8,128)(2,1)S(1)}, bf16[64,2048]{1,0:T(8,128)(2,1)S(1)}, u32[]{:S(2)}, u32[]{:S(2)}) collective-permute-start(bf16[64,2048]{1,0:T(8,128)(2,1)S(1)} %get-tuple-element.80), channel_id=1, source_target_pairs={{0,1},{1,2},{2,3},{3,4},{4,5},{5,6},{6,7},{7,0},{8,9},{9,10},{10,1... | collective-permute-start | bytes 786440 | tf_op jit(solution)/shard_map/ppermute | solution.py:268
  58.5 11.0 %collective-permute-start.8 = (bf16[64,2048]{1,0:T(8,128)(2,1)S(1)}, bf16[64,2048]{1,0:T(8,128)(2,1)S(1)}, u32[]{:S(2)}, u32[]{:S(2)}) collective-permute-start(bf16[64,2048]{1,0:T(8,128)(2,1)S(1)} %get-tuple-element.81), channel_id=1, source_target_pairs={{0,7},{1,0},{2,1},{3,2},{4,3},{5,4},{6,5},{7,6},{8,15},{9,8},{10,9... | collective-permute-start | bytes 786440 | tf_op jit(solution)/shard_map/ppermute | solution.py:268
  62.5 12.3 %collective-permute-start.1 = (bf16[64,2048]{1,0:T(8,128)(2,1)S(1)}, bf16[64,2048]{1,0:T(8,128)(2,1)S(1)}, u32[]{:S(2)}, u32[]{:S(2)}) collective-permute-start(bf16[64,2048]{1,0:T(8,128)(2,1)S(1)} %get-tuple-element.67), channel_id=1, source_target_pairs={{0,1},{1,2},{2,3},{3,4},{4,5},{5,6},{6,7},{7,0},{8,9},{9,10},{10,1... | collective-permute-start | bytes 786440 | tf_op jit(solution)/shard_map/ppermute | solution.py:268
  62.5 12.3 %collective-permute-start.2 = (bf16[64,2048]{1,0:T(8,128)(2,1)S(1)}, bf16[64,2048]{1,0:T(8,128)(2,1)S(1)}, u32[]{:S(2)}, u32[]{:S(2)}) collective-permute-start(bf16[64,2048]{1,0:T(8,128)(2,1)S(1)} %get-tuple-element.68), channel_id=1, source_target_pairs={{0,7},{1,0},{2,1},{3,2},{4,3},{5,4},{6,5},{7,6},{8,15},{9,8},{10,9... | collective-permute-start | bytes 786440 | tf_op jit(solution)/shard_map/ppermute | solution.py:268
  69.6 10.8 %collective-permute-start.10 = (bf16[64,2048]{1,0:T(8,128)(2,1)S(1)}, bf16[64,2048]{1,0:T(8,128)(2,1)S(1)}, u32[]{:S(2)}, u32[]{:S(2)}) collective-permute-start(bf16[64,2048]{1,0:T(8,128)(2,1)S(1)} %get-tuple-element.85), channel_id=1, source_target_pairs={{0,7},{1,0},{2,1},{3,2},{4,3},{5,4},{6,5},{7,6},{8,15},{9,8},{10,9... | collective-permute-start | bytes 786440 | tf_op jit(solution)/shard_map/ppermute | solution.py:268
  73.0 10.4 %collective-permute-start.9 = (bf16[64,2048]{1,0:T(8,128)(2,1)S(1)}, bf16[64,2048]{1,0:T(8,128)(2,1)S(1)}, u32[]{:S(2)}, u32[]{:S(2)}) collective-permute-start(bf16[64,2048]{1,0:T(8,128)(2,1)S(1)} %get-tuple-element.84), channel_id=1, source_target_pairs={{0,1},{1,2},{2,3},{3,4},{4,5},{5,6},{6,7},{7,0},{8,9},{9,10},{10,1... | collective-permute-start | bytes 786440 | tf_op jit(solution)/shard_map/ppermute | solution.py:268
  74.9 11.7 %collective-permute-start.3 = (bf16[64,2048]{1,0:T(8,128)(2,1)S(1)}, bf16[64,2048]{1,0:T(8,128)(2,1)S(1)}, u32[]{:S(2)}, u32[]{:S(2)}) collective-permute-start(bf16[64,2048]{1,0:T(8,128)(2,1)S(1)} %get-tuple-element.71), channel_id=1, source_target_pairs={{0,1},{1,2},{2,3},{3,4},{4,5},{5,6},{6,7},{7,0},{8,9},{9,10},{10,1... | collective-permute-start | bytes 786440 | tf_op jit(solution)/shard_map/ppermute | solution.py:268
  75.3 11.3 %collective-permute-start.4 = (bf16[64,2048]{1,0:T(8,128)(2,1)S(1)}, bf16[64,2048]{1,0:T(8,128)(2,1)S(1)}, u32[]{:S(2)}, u32[]{:S(2)}) collective-permute-start(bf16[64,2048]{1,0:T(8,128)(2,1)S(1)} %get-tuple-element.72), channel_id=1, source_target_pairs={{0,7},{1,0},{2,1},{3,2},{4,3},{5,4},{6,5},{7,6},{8,15},{9,8},{10,9... | collective-permute-start | bytes 786440 | tf_op jit(solution)/shard_map/ppermute | solution.py:268
  83.5 8.8 %collective-permute-start.11 = (bf16[64,2048]{1,0:T(8,128)(2,1)S(1)}, bf16[64,2048]{1,0:T(8,128)(2,1)S(1)}, u32[]{:S(2)}, u32[]{:S(2)}) collective-permute-start(bf16[64,2048]{1,0:T(8,128)(2,1)S(1)} %get-tuple-element.88), channel_id=1, source_target_pairs={{0,7},{1,0},{2,1},{3,2},{4,3},{5,4},{6,5},{7,6},{8,15},{9,8},{10,9... | collective-permute-start | bytes 786440 | tf_op jit(solution)/shard_map/ppermute | solution.py:268
  84.3 10.5 %collective-permute-start.12 = (bf16[64,2048]{1,0:T(8,128)(2,1)S(1)}, bf16[64,2048]{1,0:T(8,128)(2,1)S(1)}, u32[]{:S(2)}, u32[]{:S(2)}) collective-permute-start(bf16[64,2048]{1,0:T(8,128)(2,1)S(1)} %get-tuple-element.89), channel_id=1, source_target_pairs={{0,1},{1,2},{2,3},{3,4},{4,5},{5,6},{6,7},{7,0},{8,9},{9,10},{10,1... | collective-permute-start | bytes 786440 | tf_op jit(solution)/shard_map/ppermute | solution.py:268
  86.6 13.6 %copy-start.5 = (s32[4096]{0:T(1024)S(1)}, s32[4096]{0:T(1024)}, u32[]{:S(2)}) copy-start(s32[4096]{0:T(1024)} %param.27) | copy-start | bytes 49156
  86.6 13.6 %copy-start.6 = (s32[4096]{0:T(1024)S(1)}, s32[4096]{0:T(1024)}, u32[]{:S(2)}) copy-start(s32[4096]{0:T(1024)} %param.26) | copy-start | bytes 49156
  86.7 11.1 %collective-permute-start.5 = (bf16[64,2048]{1,0:T(8,128)(2,1)S(1)}, bf16[64,2048]{1,0:T(8,128)(2,1)S(1)}, u32[]{:S(2)}, u32[]{:S(2)}) collective-permute-start(bf16[64,2048]{1,0:T(8,128)(2,1)S(1)} %get-tuple-element.75), channel_id=1, source_target_pairs={{0,1},{1,2},{2,3},{3,4},{4,5},{5,6},{6,7},{7,0},{8,9},{9,10},{10,1... | collective-permute-start | bytes 786440 | tf_op jit(solution)/shard_map/ppermute | solution.py:268
  88.6 9.5 %collective-permute-start.6 = (bf16[64,2048]{1,0:T(8,128)(2,1)S(1)}, bf16[64,2048]{1,0:T(8,128)(2,1)S(1)}, u32[]{:S(2)}, u32[]{:S(2)}) collective-permute-start(bf16[64,2048]{1,0:T(8,128)(2,1)S(1)} %get-tuple-element.76), channel_id=1, source_target_pairs={{0,7},{1,0},{2,1},{3,2},{4,3},{5,4},{6,5},{7,6},{8,15},{9,8},{10,9... | collective-permute-start | bytes 786440 | tf_op jit(solution)/shard_map/ppermute | solution.py:268
  94.8 7.4 %collective-permute-start.14 = (bf16[64,2048]{1,0:T(8,128)(2,1)S(1)}, bf16[64,2048]{1,0:T(8,128)(2,1)S(1)}, u32[]{:S(2)}, u32[]{:S(2)}) collective-permute-start(bf16[64,2048]{1,0:T(8,128)(2,1)S(1)} %get-tuple-element.94), channel_id=1, source_target_pairs={{0,7},{1,0},{2,1},{3,2},{4,3},{5,4},{6,5},{7,6},{8,15},{9,8},{10,9... | collective-permute-start | bytes 786440 | tf_op jit(solution)/shard_map/ppermute | solution.py:268
  98.2 8.2 %collective-permute-start.13 = (bf16[64,2048]{1,0:T(8,128)(2,1)S(1)}, bf16[64,2048]{1,0:T(8,128)(2,1)S(1)}, u32[]{:S(2)}, u32[]{:S(2)}) collective-permute-start(bf16[64,2048]{1,0:T(8,128)(2,1)S(1)} %get-tuple-element.93), channel_id=1, source_target_pairs={{0,1},{1,2},{2,3},{3,4},{4,5},{5,6},{6,7},{7,0},{8,9},{9,10},{10,1... | collective-permute-start | bytes 786440 | tf_op jit(solution)/shard_map/ppermute | solution.py:268

commit v5 on v4

--- a/solution.py
+++ b/solution.py
@@ -19,12 +19,12 @@
 PIECE = 32
 PAY = 48
 TILE = 256
+SCAN_TILE = 512
 ROWS = 128
 SHARE = 64
 BEFORE = 3
 MIB = 1024 * 1024
 LIMIT = dict(tail_rows=58, scan_in=58, scan_edge=58, inside=58, prefix=16, norm_project=44, ring=24)
-PART = jnp.float32
 
 F32 = jnp.float32
 BF16 = jnp.bfloat16
@@ -33,6 +33,25 @@
 
 def dot(a, b, dims=((1,), (0,)), precision=None):
     return lax.dot_general(a, b, (dims, ((), ())), precision=precision, preferred_element_type=F32)
+
+
+def split(value, axis):
+    high = value.astype(BF16)
+    rest = value - high.astype(F32)
+    middle = rest.astype(BF16)
+    low = (rest - middle.astype(F32)).astype(BF16)
+    return jnp.concatenate([high.astype(F32), middle.astype(F32), low.astype(F32)], axis).astype(BF16)
+
+
+def expand(parts, first, channels):
+    pattern = head_rows(first, channels)
+    return dot(parts, jnp.concatenate([pattern] * 3, 0).astype(BF16))
+
+
+def per_token(table, value_t):
+    parts = dot(table, split(value_t, 0), ((1,), (1,)))
+    h = HEADS_LOCAL
+    return parts[:, 0:h] + parts[:, h : 2 * h] + parts[:, 2 * h : 3 * h]
 
 
 def conv_silu(pad, rim, values, taps):
@@ -63,7 +82,7 @@
     out[:, CH + STATE :] = c[...]
 
 
-def scan_in(x, b, c, step_t, decay_t, tap_x, tap_b, tap_c, xs_o, bs_o, cs_o, run_o, toward_o, one_o, two_o, pad):
+def scan_in(x, b, c, step_t, decay_t, tap_x, tap_b, tap_c, xs_o, bs_o, cs_o, run_o, toward_o, one_o, two_o, pad, parts):
     tile = pl.program_id(0)
 
     @pl.when(tile == 0)
@@ -73,19 +92,20 @@
         cs_o[...] = conv_silu(pad, empty, c[...], tap_c[...])
         later = lax.broadcasted_iota(jnp.int32, (SPAN, SPAN), 0)
         earlier = lax.broadcasted_iota(jnp.int32, (SPAN, SPAN), 1)
-        lower = (later >= earlier).astype(F32)
-        same = (later == earlier).astype(F32)
+        lower = (later >= earlier).astype(F32).astype(BF16)
+        same = (later == earlier).astype(F32).astype(BF16)
         for k in range(2):
             rows = slice(k * SPAN, (k + 1) * SPAN)
-            running = dot(lower, decay_t[:, rows], ((1,), (1,)), precision=HIGHEST)
-            step = dot(same, step_t[:, rows], ((1,), (1,)), precision=HIGHEST)
+            running = per_token(lower, decay_t[:, rows])
+            step = per_token(same, step_t[:, rows])
             run_o[rows] = running
-            toward_o[rows] = jnp.exp(running[SPAN - 1 :] - running) * step
-
-    xs = conv_silu(pad, jnp.zeros((16, TILE), BF16), x[...], tap_x[...])
+            toward = jnp.exp(running[SPAN - 1 :] - running) * step
+            toward_o[rows] = toward
+            parts[rows] = split(toward, 1)
+
+    xs = conv_silu(pad, jnp.zeros((16, x.shape[1]), BF16), x[...], tap_x[...])
     xs_o[...] = xs
-    first = tile * (TILE // HEAD_DIM)
-    wide = dot(toward_o[...], head_rows(first, TILE), precision=HIGHEST)
+    wide = expand(parts[...], tile * (xs.shape[1] // HEAD_DIM), xs.shape[1])
     row = lax.broadcasted_iota(jnp.int32, (TOK, 1), 0)
     feed = jnp.where(row < 8, 0.0, xs.astype(F32) * wide).astype(BF16)
     one_o[...] = dot(feed[:SPAN], bs_o[:SPAN], ((0,), (0,)))
@@ -107,7 +127,7 @@
     xs_o[...] = xs
     bs_o[...] = bs
     cs_o[...] = conv_head(rim[:, CH + STATE :], c[...], tap_c[...])
-    wide = dot(toward[...], head_rows(0, CH), precision=HIGHEST)
+    wide = expand(split(toward[...], 1), 0, CH)
     row = lax.broadcasted_iota(jnp.int32, (16, 1), 0)
     feed = jnp.where(row < 8, xs.astype(F32) * wide, 0.0).astype(BF16)
     first = one[...] + dot(feed, bs, ((0,), (0,)))
@@ -136,19 +156,21 @@
             state = grow[k] * state + got[k, 0:PIECE, :].astype(F32)
 
 
-def inside(xs, bs, cs, run, decay_t, step_t, skip, z, y_o, grow_o, scores, run_t):
+def inside(xs, bs, cs, run, decay_t, step_t, skip, z, y_o, grow_o, scores, run_t, grown):
     tile = pl.program_id(0)
 
     @pl.when(tile == 0)
     def _():
         later = lax.broadcasted_iota(jnp.int32, (SPAN, SPAN), 0)
         earlier = lax.broadcasted_iota(jnp.int32, (SPAN, SPAN), 1)
-        upper = (later <= earlier).astype(F32)
+        upper = (later <= earlier).astype(F32).astype(BF16)
         for k in range(2):
             rows = slice(k * SPAN, (k + 1) * SPAN)
+            grown[rows] = split(jnp.exp(run[rows]), 1)
             raw = dot(cs[rows], bs[rows], ((1,), (1,)))
             scores[rows] = jnp.where(later >= earlier, raw, 0.0)
-            run_t[:, rows] = dot(decay_t[:, rows], upper, precision=HIGHEST)
+            parts = dot(split(decay_t[:, rows], 0), upper)
+            run_t[:, rows] = parts[0:16] + parts[16:32] + parts[32:48]
 
     per_tile = TILE // HEAD_DIM
     head_lane = lax.broadcasted_iota(jnp.int32, (HEADS_LOCAL, 1), 0)
@@ -166,7 +188,7 @@
             y_o[rows, lanes] = dot(weights, xs[rows, lanes])
     gate = jax.nn.silu(z[...].astype(F32))
     y_o[...] = (y_o[...] + skip[...] * xs[...].astype(F32)) * gate
-    grow_o[...] = dot(jnp.exp(run[...]), head_rows(tile * per_tile, TILE), precision=HIGHEST) * gate
+    grow_o[...] = expand(grown[...], tile * per_tile, TILE) * gate
 
 
 def rolled(distance):
@@ -176,7 +198,7 @@
 
 def norm_project(y, grow, cs, run, first, incoming, gain, weight, *refs):
     outs, (normed, held, y_s, grow_s, sems) = refs[:-5], refs[-5:]
-    half = outs[0].shape[1]
+    half = 2 * outs[0].shape[1]
     steps = TOK // ROWS
     copies = []
     for step in range(steps):
@@ -206,18 +228,23 @@
             normed[pl.ds(pl.multiple_of(at, SHARE), SHARE)] = result[k * SHARE : (k + 1) * SHARE]
     for group in range(2):
         copies[2 * steps + group].wait()
-        targets = [(outs[8 * group], 4 - group), (outs[8 * group + 1], -3 - group)]
-        targets += [(outs[8 * group + 2 + k], k - 2 - group) for k in range(6)]
+        mine = outs[9 * group : 9 * group + 9]
         for j in range(half // 512):
             lanes = slice(group * half + j * 512, group * half + (j + 1) * 512)
             sums = dot(normed[...], held[:, lanes])
-            for out, distance in targets:
-                out[:, j * 512 : (j + 1) * 512] = sums[rolled(distance)].astype(out.dtype)
-
-
-def add_last(came, came_end, part, own, out, total):
-    out[...] = (came[...].astype(F32) + part[...]).astype(BF16)
-    total[...] = own[...] + came_end[...].astype(F32)
+            far = mine[2 * j * 512 // half]
+            inner = j * 512 % (half // 2)
+            far[:, inner : inner + 512] = sums[rolled(4)].astype(BF16)
+            for k in range(7):
+                mine[2 + k][:, j * 512 : (j + 1) * 512] = sums[rolled(k - 3)]
+
+
+def add_far(came_up, came_down, part_up, part_down, up_o, down_o):
+    part = came_up.shape[1]
+    up_o[:, :part] = (came_up[...].astype(F32) + part_up[:, :part]).astype(BF16)
+    up_o[:, part:] = part_up[:, part:].astype(BF16)
+    down_o[:, :part] = part_down[:, :part].astype(BF16)
+    down_o[:, part:] = (came_down[...].astype(F32) + part_down[:, part:]).astype(BF16)
 
 
 def add_two(came_up, came_down, part_up, part_down, up_o, down_o):
@@ -225,7 +252,7 @@
     down_o[...] = (came_down[...].astype(F32) + part_down[...]).astype(BF16)
 
 
-def finish(total_a, total_b, came_a, came_b, scale, out):
+def finish(own_a, up_a, down_a, own_b, up_b, down_b, scale, out):
     row = lax.broadcasted_iota(jnp.int32, (HAD_BLOCK, HAD_BLOCK), 0)
     column = lax.broadcasted_iota(jnp.int32, (HAD_BLOCK, HAD_BLOCK), 1)
     ones = row & column
@@ -233,10 +260,10 @@
     ones = ones ^ (ones >> 2)
     ones = ones ^ (ones >> 1)
     table = (1 - 2 * (ones & 1)).astype(F32).astype(BF16)
-    half = came_a.shape[1]
-    for group, (total, came) in enumerate(((total_a, came_a), (total_b, came_b))):
+    half = up_a.shape[1]
+    for group, (own, up, down) in enumerate(((own_a, up_a, down_a), (own_b, up_b, down_b))):
         at = slice(group * half, (group + 1) * half)
-        total = (total[...] + came[...].astype(F32)) * scale[:, at]
+        total = (own[...] + up[...].astype(F32) + down[...].astype(F32)) * scale[:, at]
         stacked = jnp.concatenate(
             [total[:, k * HAD_BLOCK : (k + 1) * HAD_BLOCK] for k in range(half // HAD_BLOCK)], 0
         )
@@ -295,25 +322,25 @@
     rim = lax.ppermute(tail, "seq", [(k, k + 1) for k in range(seq - 1)])
     xs, bs, cs, run, toward, one, two = pl.pallas_call(
         scan_in,
-        grid=(tiles,),
+        grid=(CH // SCAN_TILE,),
         in_specs=[
-            tiled((TOK, TILE), 1),
+            tiled((TOK, SCAN_TILE), 1),
             whole((TOK, STATE)),
             whole((TOK, STATE)),
             whole((HEADS_LOCAL, TOK)),
             whole((HEADS_LOCAL, TOK)),
-            tiled((4, TILE), 1),
+            tiled((4, SCAN_TILE), 1),
             whole((4, STATE)),
             whole((4, STATE)),
         ],
         out_specs=[
-            tiled((TOK, TILE), 1),
+            tiled((TOK, SCAN_TILE), 1),
             whole((TOK, STATE)),
             whole((TOK, STATE)),
             whole((TOK, HEADS_LOCAL)),
             whole((TOK, HEADS_LOCAL)),
-            tiled((TILE, STATE), 0),
-            tiled((TILE, STATE), 0),
+            tiled((SCAN_TILE, STATE), 0),
+            tiled((SCAN_TILE, STATE), 0),
         ],
         out_shape=[
             shape((TOK, CH), BF16),
@@ -324,7 +351,7 @@
             shape((CH, STATE), F32),
             shape((CH, STATE), F32),
         ],
-        scratch_shapes=[pltpu.VMEM((TOK + 8, TILE), F32)],
+        scratch_shapes=[pltpu.VMEM((TOK + 8, SCAN_TILE), F32), pltpu.VMEM((TOK, 3 * HEADS_LOCAL), BF16)],
         compiler_params=params(LIMIT["scan_in"]),
         cost_estimate=pl.CostEstimate(flops=10**9, bytes_accessed=4 * 10**6, transcendentals=10**6),
         name="scan_in",
@@ -385,13 +412,17 @@
         ],
         out_specs=[tiled((TOK, TILE), 1), tiled((TOK, TILE), 1)],
         out_shape=[shape((TOK, CH), F32), shape((TOK, CH), F32)],
-        scratch_shapes=[pltpu.VMEM((TOK, SPAN), F32), pltpu.VMEM((HEADS_LOCAL, TOK), F32)],
+        scratch_shapes=[
+            pltpu.VMEM((TOK, SPAN), F32),
+            pltpu.VMEM((HEADS_LOCAL, TOK), F32),
+            pltpu.VMEM((TOK, 3 * HEADS_LOCAL), BF16),
+        ],
         compiler_params=params(LIMIT["inside"]),
         cost_estimate=pl.CostEstimate(flops=4 * 10**9, bytes_accessed=6 * 10**6, transcendentals=2 * 10**6),
         name="inside",
     )(xs, bs, cs, run, decay_t, step_t, jnp.repeat(d_skip, HEAD_DIM)[None, :], z_in)
 
-    got, y, grow = lax.optimization_barrier((got, y, grow))
+
     before = pl.pallas_call(
         prefix,
         grid=(1,),
@@ -407,11 +438,11 @@
     half = model // 2
     vmem = pl.BlockSpec(memory_space=pltpu.VMEM)
     anywhere = pl.BlockSpec(memory_space=pl.ANY)
-    outs = ([shape((SHARE, half), BF16)] * 2 + [shape((SHARE, half), PART)] * 6) * 2
+    outs = ([shape((SHARE, half // 2), BF16)] * 2 + [shape((SHARE, half), F32)] * 7) * 2
     sums = pl.pallas_call(
         norm_project,
         in_specs=[anywhere] * 2 + [vmem] * 5 + [anywhere],
-        out_specs=[vmem] * 16,
+        out_specs=[vmem] * 18,
         out_shape=outs,
         scratch_shapes=[
             pltpu.VMEM((TOK, CH), BF16),
@@ -424,45 +455,37 @@
         cost_estimate=pl.CostEstimate(flops=10**9, bytes_accessed=10**7, transcendentals=0),
         name="norm_project",
     )(y, grow, cs, run, first, incoming, norm_gain[None, :], out_weight)
-    up_a, down_a = sums[0:2]
-    up_b, down_b = sums[8:10]
-    parts = [sums[2:8], sums[10:16]]
     scale = jnp.exp2(out_exponent.astype(F32)) * out_sign.astype(F32)
 
     sent = shape((SHARE, half), BF16)
 
-    def add(kernel, second, *operands):
+    def add(kernel, *operands):
         return pl.pallas_call(
             kernel,
             in_specs=[vmem] * 4,
             out_specs=[vmem] * 2,
-            out_shape=[sent, second],
+            out_shape=[sent] * 2,
             compiler_params=params(LIMIT["ring"]),
             cost_estimate=pl.CostEstimate(flops=10**6, bytes_accessed=10**6, transcendentals=0),
             name=kernel.__name__,
         )(*operands)
 
     ends = []
-    for group, (up, down) in enumerate(((up_a, down_a), (up_b, down_b))):
-        lowest = (-2, -3)[group]
-        mine = {distance: parts[group][distance - lowest] for distance in range(lowest, lowest + 6)}
-        for hop in range(2):
+    for group in range(2):
+        up, down = sums[9 * group : 9 * group + 2]
+        mine = {distance: sums[9 * group + 5 + distance] for distance in range(-3, 4)}
+        for distance in (3, 2, 1):
             up, down = ring(up, 1), ring(down, -1)
-            far = 3 - hop if group == 0 else 2 - hop
-            up, down = add(add_two, sent, up, down, mine[far], mine[-(5 - far - 2 * hop)])
-        up, down = ring(up, 1), ring(down, -1)
-        sign = 1 if group == 0 else -1
-        came, came_end = (up, down) if group == 0 else (down, up)
-        value, total = add(add_last, shape((SHARE, half), F32), came, came_end, mine[sign], mine[0])
-        ends += [total, ring(value, sign)]
+            up, down = add(add_far if distance == 3 else add_two, up, down, mine[distance], mine[-distance])
+        ends += [mine[0], ring(up, 1), ring(down, -1)]
     return pl.pallas_call(
         finish,
-        in_specs=[vmem] * 5,
+        in_specs=[vmem] * 7,
         out_specs=vmem,
         out_shape=shape((SHARE, model), BF16),
         compiler_params=params(LIMIT["ring"]),
         name="finish",
-    )(ends[0], ends[2], ends[1], ends[3], scale[None, :])
+    )(*ends, scale[None, :])
 
 
 def solution(mesh):

time: 108 us -> 103 us (0.954)
  blocking collectives: 14.9 us -> 0 us
  starting transfers between devices: 35.2 us -> 44.7 us
  waiting for transfers between devices: 24.6 us -> 27.5 us
  Pallas kernels: 31.6 us -> 29.1 us
    all_to_all x1 -> x0, blocking collectives: 14.9 us -> none  [local(): lax.all_to_all(before, 'seq', 0, 0, tiled=True).reshape(CH, STATE)]
    all_to_all x1, waiting for transfers between devices: 0.01 us -> 7.98 us  [local(): got = lax.all_to_all(pay, 'seq', 0, 0, tiled=True)]
    all_to_all x0 -> x1, starting transfers between devices: none -> 5.12 us  [local(): lax.all_to_all(before, 'seq', 0, 0, tiled=True).reshape(CH, STATE)]
    ppermute x14 -> x16, waiting for transfers between devices: 24.6 us -> 19.5 us  [ring(): lax.ppermute(value, 'tp', [(k, (k + step) % count) for k in range(count)])]
    ppermute x14 -> x16, starting transfers between devices: 24.7 us -> 29 us  [ring(): lax.ppermute(value, 'tp', [(k, (k + step) % count) for k in range(count)])]
    pallas_call x2, Pallas kernels: 9.76 us -> 7.58 us  [the longest x1 6.08 us: local(): pl.pallas_call(scan_in, grid=(CH // SCAN_TILE,), in_specs=[tiled((TOK, SC...]
  transfers between devices with their start and end apart: 16 -> 19, of which waited for: 11 -> 8; matrix products, arithmetic and copies ran while one was open for 1% -> 1% of each run, Pallas kernels for 16% -> 14%
where the time goes in v5:
time: 103 us
  starting transfers between devices  44.7 us (43%)
  Pallas kernels  29.1 us (28%)
  waiting for transfers between devices  27.5 us (27%)
  local copies, waits for them, and re-layouts  1.37 us (1%)
    ppermute x16, starting transfers between devices, ring(): lax.ppermute(value, 'tp', [(k, (k + step) % count) for k in range(count)])  29 us
    ppermute x16, waiting for transfers between devices, ring(): lax.ppermute(value, 'tp', [(k, (k + step) % count) for k in range(count)])  19.5 us
    all_to_all x1, starting transfers between devices, local(): got = lax.all_to_all(pay, 'seq', 0, 0, tiled=True)  8.61 us
    pallas_call x1, Pallas kernels, local(): pl.pallas_call(norm_project, in_specs=[anywhere] * 2 + [vmem] * 5 + [anyw...  8.26 us
    all_to_all x1, waiting for transfers between devices, local(): got = lax.all_to_all(pay, 'seq', 0, 0, tiled=True)  7.98 us
    pallas_call x1, Pallas kernels, local(): pl.pallas_call(inside, grid=(tiles,), in_specs=[tiled((TOK, TILE), 1), wh...  7.74 us
    pallas_call x1, Pallas kernels, local(): pl.pallas_call(scan_in, grid=(CH // SCAN_TILE,), in_specs=[tiled((TOK, SC...  6.08 us
    all_to_all x1, starting transfers between devices, local(): lax.all_to_all(before, 'seq', 0, 0, tiled=True).reshape(CH, STATE)  5.12 us
  transfers between devices with their start and end apart: 19, of which 8 were waited for; matrix products, arithmetic and copies ran while one was open for 1% of the time, Pallas kernels for 14%

profile of v5, /device:TPU:2, one launch (start us, length us, event | category | flops | bytes accessed | tf_op | source)
XLA Modules:
  0.0 102.9 jit_solution(18110752329429487009)
XLA Ops:
  1.4 1.9 %collective-permute-start = (bf16[16,1280]{1,0:T(8,128)(2,1)}, bf16[16,1280]{1,0:T(8,128)(2,1)S(1)}, u32[]{:S(2)}, u32[]{:S(2)}) collective-permute-start(bf16[16,1280]{1,0:T(8,128)(2,1)} %tail_rows.1), channel_id=1, source_target_pairs={{0,8},{8,16},{16,24},{24,32},{32,40},{40,48},{48,56},{56,64},{64,7... | collective-permute-start | bytes 122888 | tf_op jit(solution)/shard_map/ppermute | solution.py:322
  3.3 6.1 %scan_in.1 = (bf16[512,1024]{1,0:T(8,128)(2,1)}, bf16[512,128]{1,0:T(8,128)(2,1)}, bf16[512,128]{1,0:T(8,128)(2,1)}, f32[512,16]{1,0:T(8,128)}, f32[512,16]{1,0:...) custom-call(bf16[512,1024]{1,0:T(8,128)(2,1)} %x.5, bf16[512,128]{1,0:T(8,128)(2,1)} %b.5, bf16[512,128]{1,0:T(8,128)(2,1)} %c.5, ...), custom_call_target="tpu_custom_call" | custom-call | flops 1000000000 | bytes 4000000 | tf_op jit(solution)/shard_map/scan_in/pallas_call | solution.py:323
  10.0 2.8 %scan_edge.1 = (bf16[512,1024]{1,0:T(8,128)(2,1)}, bf16[512,128]{1,0:T(8,128)(2,1)}, bf16[512,128]{1,0:T(8,128)(2,1)}, f32[1024,128]{1,0:T(8,128)}, bf16[32,48,128]{2,1,0:T(8,128)(2,1)}) custom-call(bf16[16,1280]{1,0:T(8,128)(2,1)} %copy-done.4, bf16[512,1024]{1,0:T(8,128)(2,1)} %x.5, ...), custom_call_target="tpu_custom_call", output_to_operand_aliasing={{0}: (12, {}), {1}: (13, {}), {2}: (14, {})} | custom-call | tf_op jit(solution)/shard_map/scan_edge/pallas_call | solution.py:360
  12.9 8.6 %all-to-all-start = ((bf16[32,48,128]{2,1,0:T(8,128)(2,1)}), bf16[32,48,128]{2,1,0:T(8,128)(2,1)S(1)}, u32[]{:S(2)}, u32[]{:S(2)}) async-start(bf16[32,48,128]{2,1,0:T(8,128)(2,1)} %get-tuple-element.62), calls=%async_computation | async-start | bytes 786432 | tf_op jit(solution)/shard_map/all_to_all | solution.py:399
  22.2 8.0 %all-to-all-done.got = bf16[32,48,128]{2,1,0:T(8,128)(2,1)S(1)} async-done(((bf16[32,48,128]{2,1,0:T(8,128)(2,1)}), bf16[32,48,128]{2,1,0:T(8,128)(2,1)S(1)}, u32[]{:S(2)}, u32[]{:S(2)}) %all-to-all-start) | async-done | bytes 393248 | tf_op jit(solution)/shard_map/all_to_all | solution.py:399
  31.0 5.1 %all-to-all-start.1 = ((bf16[32,32,128]{2,1,0:T(8,128)(2,1)}), bf16[32,32,128]{2,1,0:T(8,128)(2,1)S(1)}, u32[]{:S(2)}, u32[]{:S(2)}) async-start(bf16[32,32,128]{2,1,0:T(8,128)(2,1)} %prefix.1), calls=%async_computation.1 | async-start | bytes 524288 | tf_op jit(solution)/shard_map/all_to_all | solution.py:435
  36.2 7.7 %inside.1 = (f32[512,1024]{1,0:T(8,128)}, f32[512,1024]{1,0:T(8,128)}) custom-call(bf16[512,1024]{1,0:T(8,128)(2,1)} %get-tuple-element.56.xs, bf16[512,128]{1,0:T(8,128)(2,1)} %get-tuple-element.57.bs, bf16[512,128]{1,0:T(8,128)(2,1)} %get-tuple-element.58.cs, f32[512,16]{1,0:T(8,128)} %get-tuple-element.50.run0.run1.run, f32[16,512]{1,0:T(8,128)} %bitcast.11, ...), custom_call_target="tpu_custom_call" | custom-call | flops 4000000000 | bytes 6000000 | tf_op jit(solution)/shard_map/inside/pallas_call | solution.py:400
  44.0 8.3 %norm_project.1 = (bf16[64,1024]{1,0:T(8,128)(2,1)S(1)}, bf16[64,1024]{1,0:T(8,128)(2,1)S(1)}, f32[64,2048]{1,0:T(8,128)S(1)}, f32[64,2048]{1,0:T(8,128)S(1)}, f...) custom-call(f32[512,1024]{1,0:T(8,128)} %get-tuple-element.59.y, ...), custom_call_target="tpu_custom_call" | custom-call | flops 1000000000 | bytes 10000000 | tf_op jit(solution)/shard_map/norm_project/pallas_call | solution.py:442
  52.2 5.9 %collective-permute-start.10 = (bf16[64,1024]{1,0:T(8,128)(2,1)S(1)}, bf16[64,1024]{1,0:T(8,128)(2,1)S(1)}, u32[]{:S(2)}, u32[]{:S(2)}) collective-permute-start(bf16[64,1024]{1,0:T(8,128)(2,1)S(1)} %get-tuple-element.80), channel_id=1, source_target_pairs={{0,7},{1,0},{2,1},{3,2},{4,3},{5,4},{6,5},{7,6},{8,15},{9,8},{10,9... | collective-permute-start | bytes 393224 | tf_op jit(solution)/shard_map/ppermute | solution.py:295
  58.2 3.3 %collective-permute-start.2 = (bf16[64,1024]{1,0:T(8,128)(2,1)S(1)}, bf16[64,1024]{1,0:T(8,128)(2,1)S(1)}, u32[]{:S(2)}, u32[]{:S(2)}) collective-permute-start(bf16[64,1024]{1,0:T(8,128)(2,1)S(1)} %get-tuple-element.65), channel_id=1, source_target_pairs={{0,7},{1,0},{2,1},{3,2},{4,3},{5,4},{6,5},{7,6},{8,15},{9,8},{10,9... | collective-permute-start | bytes 393224 | tf_op jit(solution)/shard_map/ppermute | solution.py:295
  61.4 4.3 %collective-permute-done.9.came_up = bf16[64,1024]{1,0:T(8,128)(2,1)S(1)} collective-permute-done((bf16[64,1024]{1,0:T(8,128)(2,1)S(1)}, bf16[64,1024]{1,0:T(8,128)(2,1)S(1)}, u32[]{:S(2)}, u32[]{:S(2)}) %collective-permute-start.9) | collective-permute-done | bytes 131104 | tf_op jit(solution)/shard_map/ppermute | solution.py:295
  65.9 3.2 %collective-permute-start.12 = (bf16[64,2048]{1,0:T(8,128)(2,1)S(1)}, bf16[64,2048]{1,0:T(8,128)(2,1)S(1)}, u32[]{:S(2)}, u32[]{:S(2)}) collective-permute-start(bf16[64,2048]{1,0:T(8,128)(2,1)S(1)} %get-tuple-element.84), channel_id=1, source_target_pairs={{0,7},{1,0},{2,1},{3,2},{4,3},{5,4},{6,5},{7,6},{8,15},{9,8},{10,9... | collective-permute-start | bytes 786440 | tf_op jit(solution)/shard_map/ppermute | solution.py:295
  69.3 3.2 %collective-permute-start.4 = (bf16[64,2048]{1,0:T(8,128)(2,1)S(1)}, bf16[64,2048]{1,0:T(8,128)(2,1)S(1)}, u32[]{:S(2)}, u32[]{:S(2)}) collective-permute-start(bf16[64,2048]{1,0:T(8,128)(2,1)S(1)} %get-tuple-element.69), channel_id=1, source_target_pairs={{0,7},{1,0},{2,1},{3,2},{4,3},{5,4},{6,5},{7,6},{8,15},{9,8},{10,9... | collective-permute-start | bytes 786440 | tf_op jit(solution)/shard_map/ppermute | solution.py:295
  72.5 3.8 %collective-permute-done.11.came_up = bf16[64,2048]{1,0:T(8,128)(2,1)S(1)} collective-permute-done((bf16[64,2048]{1,0:T(8,128)(2,1)S(1)}, bf16[64,2048]{1,0:T(8,128)(2,1)S(1)}, u32[]{:S(2)}, u32[]{:S(2)}) %collective-permute-start.11) | collective-permute-done | bytes 262176 | tf_op jit(solution)/shard_map/ppermute | solution.py:295
  76.5 3.2 %collective-permute-start.14 = (bf16[64,2048]{1,0:T(8,128)(2,1)S(1)}, bf16[64,2048]{1,0:T(8,128)(2,1)S(1)}, u32[]{:S(2)}, u32[]{:S(2)}) collective-permute-start(bf16[64,2048]{1,0:T(8,128)(2,1)S(1)} %get-tuple-element.88), channel_id=1, source_target_pairs={{0,7},{1,0},{2,1},{3,2},{4,3},{5,4},{6,5},{7,6},{8,15},{9,8},{10,9... | collective-permute-start | bytes 786440 | tf_op jit(solution)/shard_map/ppermute | solution.py:295
  79.7 2.2 %collective-permute-done.3.came_up = bf16[64,2048]{1,0:T(8,128)(2,1)S(1)} collective-permute-done((bf16[64,2048]{1,0:T(8,128)(2,1)S(1)}, bf16[64,2048]{1,0:T(8,128)(2,1)S(1)}, u32[]{:S(2)}, u32[]{:S(2)}) %collective-permute-start.3) | collective-permute-done | bytes 262176 | tf_op jit(solution)/shard_map/ppermute | solution.py:295
  82.1 3.2 %collective-permute-start.6 = (bf16[64,2048]{1,0:T(8,128)(2,1)S(1)}, bf16[64,2048]{1,0:T(8,128)(2,1)S(1)}, u32[]{:S(2)}, u32[]{:S(2)}) collective-permute-start(bf16[64,2048]{1,0:T(8,128)(2,1)S(1)} %get-tuple-element.73), channel_id=1, source_target_pairs={{0,7},{1,0},{2,1},{3,2},{4,3},{5,4},{6,5},{7,6},{8,15},{9,8},{10,9... | collective-permute-start | bytes 786440 | tf_op jit(solution)/shard_map/ppermute | solution.py:295
  85.3 2.2 %collective-permute-done.13.came_up = bf16[64,2048]{1,0:T(8,128)(2,1)S(1)} collective-permute-done((bf16[64,2048]{1,0:T(8,128)(2,1)S(1)}, bf16[64,2048]{1,0:T(8,128)(2,1)S(1)}, u32[]{:S(2)}, u32[]{:S(2)}) %collective-permute-start.13) | collective-permute-done | bytes 262176 | tf_op jit(solution)/shard_map/ppermute | solution.py:295
  87.7 3.2 %collective-permute-start.16 = (bf16[64,2048]{1,0:T(8,128)(2,1)S(1)}, bf16[64,2048]{1,0:T(8,128)(2,1)S(1)}, u32[]{:S(2)}, u32[]{:S(2)}) collective-permute-start(bf16[64,2048]{1,0:T(8,128)(2,1)S(1)} %get-tuple-element.92), channel_id=1, source_target_pairs={{0,7},{1,0},{2,1},{3,2},{4,3},{5,4},{6,5},{7,6},{8,15},{9,8},{10,9... | collective-permute-start | bytes 786440 | tf_op jit(solution)/shard_map/ppermute | solution.py:295
  90.9 2.2 %collective-permute-done.5.came_up = bf16[64,2048]{1,0:T(8,128)(2,1)S(1)} collective-permute-done((bf16[64,2048]{1,0:T(8,128)(2,1)S(1)}, bf16[64,2048]{1,0:T(8,128)(2,1)S(1)}, u32[]{:S(2)}, u32[]{:S(2)}) %collective-permute-start.5) | collective-permute-done | bytes 262176 | tf_op jit(solution)/shard_map/ppermute | solution.py:295
  93.3 3.2 %collective-permute-start.8 = (bf16[64,2048]{1,0:T(8,128)(2,1)S(1)}, bf16[64,2048]{1,0:T(8,128)(2,1)S(1)}, u32[]{:S(2)}, u32[]{:S(2)}) collective-permute-start(bf16[64,2048]{1,0:T(8,128)(2,1)S(1)} %get-tuple-element.77), channel_id=1, source_target_pairs={{0,7},{1,0},{2,1},{3,2},{4,3},{5,4},{6,5},{7,6},{8,15},{9,8},{10,9... | collective-permute-start | bytes 786440 | tf_op jit(solution)/shard_map/ppermute | solution.py:295
  96.6 2.0 %collective-permute-done.15.up_b = bf16[64,2048]{1,0:T(8,128)(2,1)S(1)} collective-permute-done((bf16[64,2048]{1,0:T(8,128)(2,1)S(1)}, bf16[64,2048]{1,0:T(8,128)(2,1)S(1)}, u32[]{:S(2)}, u32[]{:S(2)}) %collective-permute-start.15) | collective-permute-done | bytes 262176 | tf_op jit(solution)/shard_map/ppermute | solution.py:295
  98.6 2.8 %collective-permute-done.7.up_a = bf16[64,2048]{1,0:T(8,128)(2,1)S(1)} collective-permute-done((bf16[64,2048]{1,0:T(8,128)(2,1)S(1)}, bf16[64,2048]{1,0:T(8,128)(2,1)S(1)}, u32[]{:S(2)}, u32[]{:S(2)}) %collective-permute-start.7) | collective-permute-done | bytes 262176 | tf_op jit(solution)/shard_map/ppermute | solution.py:295
  101.4 1.5 %finish.1 = bf16[64,4096]{1,0:T(8,128)(2,1)} custom-call(f32[64,2048]{1,0:T(8,128)S(1)} %get-tuple-element.63.own_a, bf16[64,2048]{1,0:T(8,128)(2,1)S(1)} %collective-permute-done.7.up_a, bf16[64,2048]{1,0:T(8,128)(2,1)S(1)} %collective-permute-done.8.down_a, f32[64,2048]{1,0:T(8,128)S(1)} %get-tuple-element.78.own_b, ...), custom_call_target="tpu_custom_call" | custom-call | tf_op jit(solution)/shard_map/finish/pallas_call | solution.py:481
  (46 shorter events, 4.6 us)
Async XLA Ops:
  1.4 8.0 %collective-permute-start = (bf16[16,1280]{1,0:T(8,128)(2,1)}, bf16[16,1280]{1,0:T(8,128)(2,1)S(1)}, u32[]{:S(2)}, u32[]{:S(2)}) collective-permute-start(bf16[16,1280]{1,0:T(8,128)(2,1)} %tail_rows.1), channel_id=1, source_target_pairs={{0,8},{8,16},{16,24},{24,32},{32,40},{40,48},{48,56},{56,64},{64,7... | collective-permute-start | bytes 122888 | tf_op jit(solution)/shard_map/ppermute | solution.py:322
  10.0 11.5 %copy-start.7 = (f32[16]{0:T(128)S(1)}, f32[16]{0:T(128)}, u32[]{:S(2)}) copy-start(f32[16]{0:T(128)} %param.23) | copy-start | bytes 196
  12.9 17.3 %all-to-all-start = ((bf16[32,48,128]{2,1,0:T(8,128)(2,1)}), bf16[32,48,128]{2,1,0:T(8,128)(2,1)S(1)}, u32[]{:S(2)}, u32[]{:S(2)}) async-start(bf16[32,48,128]{2,1,0:T(8,128)(2,1)} %get-tuple-element.62), calls=%async_computation | async-start | bytes 786432 | tf_op jit(solution)/shard_map/all_to_all | solution.py:399
  31.0 12.9 %all-to-all-start.1 = ((bf16[32,32,128]{2,1,0:T(8,128)(2,1)}), bf16[32,32,128]{2,1,0:T(8,128)(2,1)S(1)}, u32[]{:S(2)}, u32[]{:S(2)}) async-start(bf16[32,32,128]{2,1,0:T(8,128)(2,1)} %prefix.1), calls=%async_computation.1 | async-start | bytes 524288 | tf_op jit(solution)/shard_map/all_to_all | solution.py:435
  36.1 7.8 %copy-start = (f32[512,16]{1,0:T(8,128)S(1)}, f32[512,16]{1,0:T(8,128)}, u32[]{:S(2)}) copy-start(f32[512,16]{1,0:T(8,128)} %get-tuple-element.50.run0.run1.run) | copy-start | bytes 98308
  36.1 7.8 %copy-start.1 = (bf16[512,128]{1,0:T(8,128)(2,1)S(1)}, bf16[512,128]{1,0:T(8,128)(2,1)}, u32[]{:S(2)}) copy-start(bf16[512,128]{1,0:T(8,128)(2,1)} %get-tuple-element.58.cs) | copy-start | bytes 393220
  52.2 9.2 %collective-permute-start.10 = (bf16[64,1024]{1,0:T(8,128)(2,1)S(1)}, bf16[64,1024]{1,0:T(8,128)(2,1)S(1)}, u32[]{:S(2)}, u32[]{:S(2)}) collective-permute-start(bf16[64,1024]{1,0:T(8,128)(2,1)S(1)} %get-tuple-element.80), channel_id=1, source_target_pairs={{0,7},{1,0},{2,1},{3,2},{4,3},{5,4},{6,5},{7,6},{8,15},{9,8},{10,9... | collective-permute-start | bytes 393224 | tf_op jit(solution)/shard_map/ppermute | solution.py:295
  58.2 7.6 %collective-permute-start.9 = (bf16[64,1024]{1,0:T(8,128)(2,1)S(1)}, bf16[64,1024]{1,0:T(8,128)(2,1)S(1)}, u32[]{:S(2)}, u32[]{:S(2)}) collective-permute-start(bf16[64,1024]{1,0:T(8,128)(2,1)S(1)} %get-tuple-element.79), channel_id=1, source_target_pairs={{0,1},{1,2},{2,3},{3,4},{4,5},{5,6},{6,7},{7,0},{8,9},{9,10},{10,1... | collective-permute-start | bytes 393224 | tf_op jit(solution)/shard_map/ppermute | solution.py:295
  58.2 11.0 %collective-permute-start.1 = (bf16[64,1024]{1,0:T(8,128)(2,1)S(1)}, bf16[64,1024]{1,0:T(8,128)(2,1)S(1)}, u32[]{:S(2)}, u32[]{:S(2)}) collective-permute-start(bf16[64,1024]{1,0:T(8,128)(2,1)S(1)} %get-tuple-element.64), channel_id=1, source_target_pairs={{0,1},{1,2},{2,3},{3,4},{4,5},{5,6},{6,7},{7,0},{8,9},{9,10},{10,1... | collective-permute-start | bytes 393224 | tf_op jit(solution)/shard_map/ppermute | solution.py:295
  58.2 11.0 %collective-permute-start.2 = (bf16[64,1024]{1,0:T(8,128)(2,1)S(1)}, bf16[64,1024]{1,0:T(8,128)(2,1)S(1)}, u32[]{:S(2)}, u32[]{:S(2)}) collective-permute-start(bf16[64,1024]{1,0:T(8,128)(2,1)S(1)} %get-tuple-element.65), channel_id=1, source_target_pairs={{0,7},{1,0},{2,1},{3,2},{4,3},{5,4},{6,5},{7,6},{8,15},{9,8},{10,9... | collective-permute-start | bytes 393224 | tf_op jit(solution)/shard_map/ppermute | solution.py:295
  65.8 10.5 %collective-permute-start.11 = (bf16[64,2048]{1,0:T(8,128)(2,1)S(1)}, bf16[64,2048]{1,0:T(8,128)(2,1)S(1)}, u32[]{:S(2)}, u32[]{:S(2)}) collective-permute-start(bf16[64,2048]{1,0:T(8,128)(2,1)S(1)} %get-tuple-element.83), channel_id=1, source_target_pairs={{0,1},{1,2},{2,3},{3,4},{4,5},{5,6},{6,7},{7,0},{8,9},{9,10},{10,1... | collective-permute-start | bytes 786440 | tf_op jit(solution)/shard_map/ppermute | solution.py:295
  65.9 10.4 %collective-permute-start.12 = (bf16[64,2048]{1,0:T(8,128)(2,1)S(1)}, bf16[64,2048]{1,0:T(8,128)(2,1)S(1)}, u32[]{:S(2)}, u32[]{:S(2)}) collective-permute-start(bf16[64,2048]{1,0:T(8,128)(2,1)S(1)} %get-tuple-element.84), channel_id=1, source_target_pairs={{0,7},{1,0},{2,1},{3,2},{4,3},{5,4},{6,5},{7,6},{8,15},{9,8},{10,9... | collective-permute-start | bytes 786440 | tf_op jit(solution)/shard_map/ppermute | solution.py:295
  69.2 12.7 %collective-permute-start.3 = (bf16[64,2048]{1,0:T(8,128)(2,1)S(1)}, bf16[64,2048]{1,0:T(8,128)(2,1)S(1)}, u32[]{:S(2)}, u32[]{:S(2)}) collective-permute-start(bf16[64,2048]{1,0:T(8,128)(2,1)S(1)} %get-tuple-element.68), channel_id=1, source_target_pairs={{0,1},{1,2},{2,3},{3,4},{4,5},{5,6},{6,7},{7,0},{8,9},{9,10},{10,1... | collective-permute-start | bytes 786440 | tf_op jit(solution)/shard_map/ppermute | solution.py:295
  69.3 12.6 %collective-permute-start.4 = (bf16[64,2048]{1,0:T(8,128)(2,1)S(1)}, bf16[64,2048]{1,0:T(8,128)(2,1)S(1)}, u32[]{:S(2)}, u32[]{:S(2)}) collective-permute-start(bf16[64,2048]{1,0:T(8,128)(2,1)S(1)} %get-tuple-element.69), channel_id=1, source_target_pairs={{0,7},{1,0},{2,1},{3,2},{4,3},{5,4},{6,5},{7,6},{8,15},{9,8},{10,9... | collective-permute-start | bytes 786440 | tf_op jit(solution)/shard_map/ppermute | solution.py:295
  76.4 11.1 %collective-permute-start.13 = (bf16[64,2048]{1,0:T(8,128)(2,1)S(1)}, bf16[64,2048]{1,0:T(8,128)(2,1)S(1)}, u32[]{:S(2)}, u32[]{:S(2)}) collective-permute-start(bf16[64,2048]{1,0:T(8,128)(2,1)S(1)} %get-tuple-element.87), channel_id=1, source_target_pairs={{0,1},{1,2},{2,3},{3,4},{4,5},{5,6},{6,7},{7,0},{8,9},{9,10},{10,1... | collective-permute-start | bytes 786440 | tf_op jit(solution)/shard_map/ppermute | solution.py:295
  76.5 11.1 %collective-permute-start.14 = (bf16[64,2048]{1,0:T(8,128)(2,1)S(1)}, bf16[64,2048]{1,0:T(8,128)(2,1)S(1)}, u32[]{:S(2)}, u32[]{:S(2)}) collective-permute-start(bf16[64,2048]{1,0:T(8,128)(2,1)S(1)} %get-tuple-element.88), channel_id=1, source_target_pairs={{0,7},{1,0},{2,1},{3,2},{4,3},{5,4},{6,5},{7,6},{8,15},{9,8},{10,9... | collective-permute-start | bytes 786440 | tf_op jit(solution)/shard_map/ppermute | solution.py:295
  81.9 14.6 %copy-start.5 = (s32[4096]{0:T(1024)S(1)}, s32[4096]{0:T(1024)}, u32[]{:S(2)}) copy-start(s32[4096]{0:T(1024)} %param.27) | copy-start | bytes 49156
  81.9 14.6 %copy-start.6 = (s32[4096]{0:T(1024)S(1)}, s32[4096]{0:T(1024)}, u32[]{:S(2)}) copy-start(s32[4096]{0:T(1024)} %param.26) | copy-start | bytes 49156
  82.0 11.1 %collective-permute-start.5 = (bf16[64,2048]{1,0:T(8,128)(2,1)S(1)}, bf16[64,2048]{1,0:T(8,128)(2,1)S(1)}, u32[]{:S(2)}, u32[]{:S(2)}) collective-permute-start(bf16[64,2048]{1,0:T(8,128)(2,1)S(1)} %get-tuple-element.72), channel_id=1, source_target_pairs={{0,1},{1,2},{2,3},{3,4},{4,5},{5,6},{6,7},{7,0},{8,9},{9,10},{10,1... | collective-permute-start | bytes 786440 | tf_op jit(solution)/shard_map/ppermute | solution.py:295
  82.1 11.0 %collective-permute-start.6 = (bf16[64,2048]{1,0:T(8,128)(2,1)S(1)}, bf16[64,2048]{1,0:T(8,128)(2,1)S(1)}, u32[]{:S(2)}, u32[]{:S(2)}) collective-permute-start(bf16[64,2048]{1,0:T(8,128)(2,1)S(1)} %get-tuple-element.73), channel_id=1, source_target_pairs={{0,7},{1,0},{2,1},{3,2},{4,3},{5,4},{6,5},{7,6},{8,15},{9,8},{10,9... | collective-permute-start | bytes 786440 | tf_op jit(solution)/shard_map/ppermute | solution.py:295
  87.6 11.0 %collective-permute-start.15 = (bf16[64,2048]{1,0:T(8,128)(2,1)S(1)}, bf16[64,2048]{1,0:T(8,128)(2,1)S(1)}, u32[]{:S(2)}, u32[]{:S(2)}) collective-permute-start(bf16[64,2048]{1,0:T(8,128)(2,1)S(1)} %get-tuple-element.91), channel_id=1, source_target_pairs={{0,1},{1,2},{2,3},{3,4},{4,5},{5,6},{6,7},{7,0},{8,9},{9,10},{10,1... | collective-permute-start | bytes 786440 | tf_op jit(solution)/shard_map/ppermute | solution.py:295
  87.7 10.9 %collective-permute-start.16 = (bf16[64,2048]{1,0:T(8,128)(2,1)S(1)}, bf16[64,2048]{1,0:T(8,128)(2,1)S(1)}, u32[]{:S(2)}, u32[]{:S(2)}) collective-permute-start(bf16[64,2048]{1,0:T(8,128)(2,1)S(1)} %get-tuple-element.92), channel_id=1, source_target_pairs={{0,7},{1,0},{2,1},{3,2},{4,3},{5,4},{6,5},{7,6},{8,15},{9,8},{10,9... | collective-permute-start | bytes 786440 | tf_op jit(solution)/shard_map/ppermute | solution.py:295
  93.2 8.2 %collective-permute-start.7 = (bf16[64,2048]{1,0:T(8,128)(2,1)S(1)}, bf16[64,2048]{1,0:T(8,128)(2,1)S(1)}, u32[]{:S(2)}, u32[]{:S(2)}) collective-permute-start(bf16[64,2048]{1,0:T(8,128)(2,1)S(1)} %get-tuple-element.76), channel_id=1, source_target_pairs={{0,1},{1,2},{2,3},{3,4},{4,5},{5,6},{6,7},{7,0},{8,9},{9,10},{10,1... | collective-permute-start | bytes 786440 | tf_op jit(solution)/shard_map/ppermute | solution.py:295
  93.3 8.1 %collective-permute-start.8 = (bf16[64,2048]{1,0:T(8,128)(2,1)S(1)}, bf16[64,2048]{1,0:T(8,128)(2,1)S(1)}, u32[]{:S(2)}, u32[]{:S(2)}) collective-permute-start(bf16[64,2048]{1,0:T(8,128)(2,1)S(1)} %get-tuple-element.77), channel_id=1, source_target_pairs={{0,7},{1,0},{2,1},{3,2},{4,3},{5,4},{6,5},{7,6},{8,15},{9,8},{10,9... | collective-permute-start | bytes 786440 | tf_op jit(solution)/shard_map/ppermute | solution.py:295
  (3 other events, 16.2 us)

commit v6 on v5

--- a/solution.py
+++ b/solution.py
@@ -24,7 +24,7 @@
 SHARE = 64
 BEFORE = 3
 MIB = 1024 * 1024
-LIMIT = dict(tail_rows=58, scan_in=58, scan_edge=58, inside=58, prefix=16, norm_project=44, ring=24)
+LIMIT = dict(tail_rows=58, scan_in=58, scan_edge=58, inside=58, prefix=16, norm_project=47, project=44, ring=24)
 
 F32 = jnp.float32
 BF16 = jnp.bfloat16
@@ -196,8 +196,8 @@
     return slice(first, first + SHARE)
 
 
-def norm_project(y, grow, cs, run, first, incoming, gain, weight, *refs):
-    outs, (normed, held, y_s, grow_s, sems) = refs[:-5], refs[-5:]
+def norm_project(y, grow, cs, run, first, incoming, gain, weight, normed, *refs):
+    outs, (held, y_s, grow_s, sems) = refs[:-4], refs[-4:]
     half = 2 * outs[0].shape[1]
     steps = TOK // ROWS
     copies = []
@@ -228,15 +228,35 @@
             normed[pl.ds(pl.multiple_of(at, SHARE), SHARE)] = result[k * SHARE : (k + 1) * SHARE]
     for group in range(2):
         copies[2 * steps + group].wait()
-        mine = outs[9 * group : 9 * group + 9]
         for j in range(half // 512):
             lanes = slice(group * half + j * 512, group * half + (j + 1) * 512)
+            far = outs[2 * group + 2 * j * 512 // half]
+            inner = j * 512 % (half // 2)
+            if group == 1:
+                far[:, inner : inner + 512] = dot(normed[rolled(4)], held[:, lanes]).astype(BF16)
+                continue
             sums = dot(normed[...], held[:, lanes])
-            far = mine[2 * j * 512 // half]
-            inner = j * 512 % (half // 2)
             far[:, inner : inner + 512] = sums[rolled(4)].astype(BF16)
             for k in range(7):
-                mine[2 + k][:, j * 512 : (j + 1) * 512] = sums[rolled(k - 3)]
+                outs[4 + k][:, j * 512 : (j + 1) * 512] = sums[rolled(k - 3)]
+
+
+def project(group, normed, weight, *refs):
+    outs, (held, sems) = refs[:-2], refs[-2:]
+    half = outs[0].shape[1]
+    copies = []
+    for j in range(half // 512):
+        here = slice(j * 512, (j + 1) * 512)
+        there = slice(group * half + j * 512, group * half + (j + 1) * 512)
+        copies.append(pltpu.make_async_copy(weight.at[:, there], held.at[:, here], sems.at[j]))
+    for copy in copies:
+        copy.start()
+    for j, copy in enumerate(copies):
+        here = slice(j * 512, (j + 1) * 512)
+        copy.wait()
+        sums = dot(normed[0 : 7 * SHARE], held[:, here])
+        for k in range(7):
+            outs[k][:, here] = sums[k * SHARE : (k + 1) * SHARE]
 
 
 def add_far(came_up, came_down, part_up, part_down, up_o, down_o):
@@ -438,14 +458,12 @@
     half = model // 2
     vmem = pl.BlockSpec(memory_space=pltpu.VMEM)
     anywhere = pl.BlockSpec(memory_space=pl.ANY)
-    outs = ([shape((SHARE, half // 2), BF16)] * 2 + [shape((SHARE, half), F32)] * 7) * 2
-    sums = pl.pallas_call(
+    normed, *sums = pl.pallas_call(
         norm_project,
         in_specs=[anywhere] * 2 + [vmem] * 5 + [anywhere],
-        out_specs=[vmem] * 18,
-        out_shape=outs,
+        out_specs=[vmem] * 12,
+        out_shape=[shape((TOK, CH), BF16)] + [shape((SHARE, half // 2), BF16)] * 4 + [shape((SHARE, half), F32)] * 7,
         scratch_shapes=[
-            pltpu.VMEM((TOK, CH), BF16),
             pltpu.VMEM((CH, model), BF16),
             pltpu.VMEM((TOK, CH), F32),
             pltpu.VMEM((TOK, CH), F32),
@@ -455,6 +473,18 @@
         cost_estimate=pl.CostEstimate(flops=10**9, bytes_accessed=10**7, transcendentals=0),
         name="norm_project",
     )(y, grow, cs, run, first, incoming, norm_gain[None, :], out_weight)
+    fars = sums[0:4]
+    rest = pl.pallas_call(
+        functools.partial(project, 1),
+        in_specs=[vmem, anywhere],
+        out_specs=[vmem] * 7,
+        out_shape=[shape((SHARE, half), F32)] * 7,
+        scratch_shapes=[pltpu.VMEM((CH, half), BF16), pltpu.SemaphoreType.DMA((half // 512,))],
+        compiler_params=params(LIMIT["project"]),
+        cost_estimate=pl.CostEstimate(flops=10, bytes_accessed=10, transcendentals=0),
+        name="project",
+    )(normed, out_weight)
+    parts = [sums[4:11], rest]
     scale = jnp.exp2(out_exponent.astype(F32)) * out_sign.astype(F32)
 
     sent = shape((SHARE, half), BF16)
@@ -472,8 +502,8 @@
 
     ends = []
     for group in range(2):
-        up, down = sums[9 * group : 9 * group + 2]
-        mine = {distance: sums[9 * group + 5 + distance] for distance in range(-3, 4)}
+        up, down = fars[2 * group : 2 * group + 2]
+        mine = {distance: parts[group][3 + distance] for distance in range(-3, 4)}
         for distance in (3, 2, 1):
             up, down = ring(up, 1), ring(down, -1)
             up, down = add(add_far if distance == 3 else add_two, up, down, mine[distance], mine[-distance])

time: 103 us -> 103 us (level)
  waiting for transfers between devices: 27.5 us -> 24.2 us
  Pallas kernels: 29.1 us -> 31.4 us
    pallas_call x0 -> x1, Pallas kernels: none -> 3.83 us  [local(): pl.pallas_call(functools.partial(project, 1), in_specs=[vmem, anywhere],...]
    ppermute x16, waiting for transfers between devices: 19.5 us -> 16.2 us  [ring(): lax.ppermute(value, 'tp', [(k, (k + step) % count) for k in range(count)])]
    pallas_call x1, Pallas kernels: 8.26 us -> 6.77 us  [local(): pl.pallas_call(norm_project, in_specs=[anywhere] * 2 + [vmem] * 5 + [anyw...]
  transfers between devices with their start and end apart: 19 -> 19, of which waited for: 8 -> 8; matrix products, arithmetic and copies ran while one was open for 1% -> 1% of each run, Pallas kernels for 14% -> 18%
where the time goes in v6:
time: 103 us; the launch traced here: 102 us
  starting transfers between devices  45 us (44%)
  Pallas kernels  31.4 us (30%)
  waiting for transfers between devices  24.2 us (23%)
  local copies, waits for them, and re-layouts  1.38 us (1%)
    ppermute x16, starting transfers between devices, ring(): lax.ppermute(value, 'tp', [(k, (k + step) % count) for k in range(count)])  29.4 us
    ppermute x16, waiting for transfers between devices, ring(): lax.ppermute(value, 'tp', [(k, (k + step) % count) for k in range(count)])  16.2 us
    all_to_all x1, starting transfers between devices, local(): got = lax.all_to_all(pay, 'seq', 0, 0, tiled=True)  8.61 us
    all_to_all x1, waiting for transfers between devices, local(): got = lax.all_to_all(pay, 'seq', 0, 0, tiled=True)  7.97 us
    pallas_call x1, Pallas kernels, local(): pl.pallas_call(inside, grid=(tiles,), in_specs=[tiled((TOK, TILE), 1), wh...  7.76 us
    pallas_call x1, Pallas kernels, local(): pl.pallas_call(norm_project, in_specs=[anywhere] * 2 + [vmem] * 5 + [anyw...  6.77 us
    pallas_call x1, Pallas kernels, local(): pl.pallas_call(scan_in, grid=(CH // SCAN_TILE,), in_specs=[tiled((TOK, SC...  6.07 us
    all_to_all x1, starting transfers between devices, local(): lax.all_to_all(before, 'seq', 0, 0, tiled=True).reshape(CH, STATE)  5.12 us
  transfers between devices with their start and end apart: 19, of which 8 were waited for; matrix products, arithmetic and copies ran while one was open for 1% of the time, Pallas kernels for 18%

profile of v6, /device:TPU:2, one launch (start us, length us, event | category | flops | bytes accessed | tf_op | source)
XLA Modules:
  0.0 102.3 jit_solution(5186091367946546713)
XLA Ops:
  1.4 1.9 %collective-permute-start = (bf16[16,1280]{1,0:T(8,128)(2,1)}, bf16[16,1280]{1,0:T(8,128)(2,1)S(1)}, u32[]{:S(2)}, u32[]{:S(2)}) collective-permute-start(bf16[16,1280]{1,0:T(8,128)(2,1)} %tail_rows.1), channel_id=1, source_target_pairs={{0,8},{8,16},{16,24},{24,32},{32,40},{40,48},{48,56},{56,64},{64,7... | collective-permute-start | bytes 122888 | tf_op jit(solution)/shard_map/ppermute | solution.py:342
  3.3 6.1 %scan_in.1 = (bf16[512,1024]{1,0:T(8,128)(2,1)}, bf16[512,128]{1,0:T(8,128)(2,1)}, bf16[512,128]{1,0:T(8,128)(2,1)}, f32[512,16]{1,0:T(8,128)}, f32[512,16]{1,0:...) custom-call(bf16[512,1024]{1,0:T(8,128)(2,1)} %x.5, bf16[512,128]{1,0:T(8,128)(2,1)} %b.5, bf16[512,128]{1,0:T(8,128)(2,1)} %c.5, ...), custom_call_target="tpu_custom_call" | custom-call | flops 1000000000 | bytes 4000000 | tf_op jit(solution)/shard_map/scan_in/pallas_call | solution.py:343
  10.0 2.8 %scan_edge.1 = (bf16[512,1024]{1,0:T(8,128)(2,1)}, bf16[512,128]{1,0:T(8,128)(2,1)}, bf16[512,128]{1,0:T(8,128)(2,1)}, f32[1024,128]{1,0:T(8,128)}, bf16[32,48,128]{2,1,0:T(8,128)(2,1)}) custom-call(bf16[16,1280]{1,0:T(8,128)(2,1)} %copy-done.4, bf16[512,1024]{1,0:T(8,128)(2,1)} %x.5, ...), custom_call_target="tpu_custom_call", output_to_operand_aliasing={{0}: (12, {}), {1}: (13, {}), {2}: (14, {})} | custom-call | tf_op jit(solution)/shard_map/scan_edge/pallas_call | solution.py:380
  12.8 8.6 %all-to-all-start = ((bf16[32,48,128]{2,1,0:T(8,128)(2,1)}), bf16[32,48,128]{2,1,0:T(8,128)(2,1)S(1)}, u32[]{:S(2)}, u32[]{:S(2)}) async-start(bf16[32,48,128]{2,1,0:T(8,128)(2,1)} %get-tuple-element.63), calls=%async_computation | async-start | bytes 786432 | tf_op jit(solution)/shard_map/all_to_all | solution.py:419
  22.2 8.0 %all-to-all-done.got = bf16[32,48,128]{2,1,0:T(8,128)(2,1)S(1)} async-done(((bf16[32,48,128]{2,1,0:T(8,128)(2,1)}), bf16[32,48,128]{2,1,0:T(8,128)(2,1)S(1)}, u32[]{:S(2)}, u32[]{:S(2)}) %all-to-all-start) | async-done | bytes 393248 | tf_op jit(solution)/shard_map/all_to_all | solution.py:419
  31.0 5.1 %all-to-all-start.1 = ((bf16[32,32,128]{2,1,0:T(8,128)(2,1)}), bf16[32,32,128]{2,1,0:T(8,128)(2,1)S(1)}, u32[]{:S(2)}, u32[]{:S(2)}) async-start(bf16[32,32,128]{2,1,0:T(8,128)(2,1)} %prefix.1), calls=%async_computation.1 | async-start | bytes 524288 | tf_op jit(solution)/shard_map/all_to_all | solution.py:455
  36.1 7.8 %inside.1 = (f32[512,1024]{1,0:T(8,128)}, f32[512,1024]{1,0:T(8,128)}) custom-call(bf16[512,1024]{1,0:T(8,128)(2,1)} %get-tuple-element.57.xs, bf16[512,128]{1,0:T(8,128)(2,1)} %get-tuple-element.58.bs, bf16[512,128]{1,0:T(8,128)(2,1)} %get-tuple-element.59.cs, f32[512,16]{1,0:T(8,128)} %get-tuple-element.51.run0.run1.run, f32[16,512]{1,0:T(8,128)} %bitcast.11, ...), custom_call_target="tpu_custom_call" | custom-call | flops 4000000000 | bytes 6000000 | tf_op jit(solution)/shard_map/inside/pallas_call | solution.py:420
  43.9 6.8 %norm_project.1 = (bf16[512,1024]{1,0:T(8,128)(2,1)S(1)}, bf16[64,1024]{1,0:T(8,128)(2,1)S(1)}, bf16[64,1024]{1,0:T(8,128)(2,1)S(1)}, bf16[64,1024]{1,0:T(8,128)...) custom-call(f32[512,1024]{1,0:T(8,128)} %get-tuple-element.60.y, ...), custom_call_target="tpu_custom_call" | custom-call | flops 1000000000 | bytes 10000000 | tf_op jit(solution)/shard_map/norm_project/pallas_call | solution.py:461
  50.7 5.9 %collective-permute-start.10 = (bf16[64,1024]{1,0:T(8,128)(2,1)S(1)}, bf16[64,1024]{1,0:T(8,128)(2,1)S(1)}, u32[]{:S(2)}, u32[]{:S(2)}) collective-permute-start(bf16[64,1024]{1,0:T(8,128)(2,1)S(1)} %get-tuple-element.82), channel_id=1, source_target_pairs={{0,7},{1,0},{2,1},{3,2},{4,3},{5,4},{6,5},{7,6},{8,15},{9,8},{10,9... | collective-permute-start | bytes 393224 | tf_op jit(solution)/shard_map/ppermute | solution.py:315
  56.7 3.3 %collective-permute-start.2 = (bf16[64,1024]{1,0:T(8,128)(2,1)S(1)}, bf16[64,1024]{1,0:T(8,128)(2,1)S(1)}, u32[]{:S(2)}, u32[]{:S(2)}) collective-permute-start(bf16[64,1024]{1,0:T(8,128)(2,1)S(1)} %get-tuple-element.66), channel_id=1, source_target_pairs={{0,7},{1,0},{2,1},{3,2},{4,3},{5,4},{6,5},{7,6},{8,15},{9,8},{10,9... | collective-permute-start | bytes 393224 | tf_op jit(solution)/shard_map/ppermute | solution.py:315
  59.9 3.8 %project.1 = (f32[64,2048]{1,0:T(8,128)S(1)}, f32[64,2048]{1,0:T(8,128)S(1)}, f32[64,2048]{1,0:T(8,128)S(1)}, f32[64,2048]{1,0:T(8,128)S(1)}, f32[64,2048]{1,0:T...) custom-call(bf16[512,1024]{1,0:T(8,128)(2,1)S(1)} %get-tuple-element.79.normed, bf16[1024,4096]{1,0:T(8,128)(2,1)} %weight.3), custom_call_target="tpu_custom_call" | custom-call | flops 10 | bytes 10 | tf_op jit(solution)/shard_map/project/pallas_call | solution.py:477
  64.4 3.2 %collective-permute-start.12 = (bf16[64,2048]{1,0:T(8,128)(2,1)S(1)}, bf16[64,2048]{1,0:T(8,128)(2,1)S(1)}, u32[]{:S(2)}, u32[]{:S(2)}) collective-permute-start(bf16[64,2048]{1,0:T(8,128)(2,1)S(1)} %get-tuple-element.86), channel_id=1, source_target_pairs={{0,7},{1,0},{2,1},{3,2},{4,3},{5,4},{6,5},{7,6},{8,15},{9,8},{10,9... | collective-permute-start | bytes 786440 | tf_op jit(solution)/shard_map/ppermute | solution.py:315
  67.8 3.2 %collective-permute-start.4 = (bf16[64,2048]{1,0:T(8,128)(2,1)S(1)}, bf16[64,2048]{1,0:T(8,128)(2,1)S(1)}, u32[]{:S(2)}, u32[]{:S(2)}) collective-permute-start(bf16[64,2048]{1,0:T(8,128)(2,1)S(1)} %get-tuple-element.70), channel_id=1, source_target_pairs={{0,7},{1,0},{2,1},{3,2},{4,3},{5,4},{6,5},{7,6},{8,15},{9,8},{10,9... | collective-permute-start | bytes 786440 | tf_op jit(solution)/shard_map/ppermute | solution.py:315
  71.0 3.8 %collective-permute-done.11.came_up = bf16[64,2048]{1,0:T(8,128)(2,1)S(1)} collective-permute-done((bf16[64,2048]{1,0:T(8,128)(2,1)S(1)}, bf16[64,2048]{1,0:T(8,128)(2,1)S(1)}, u32[]{:S(2)}, u32[]{:S(2)}) %collective-permute-start.11) | collective-permute-done | bytes 262176 | tf_op jit(solution)/shard_map/ppermute | solution.py:315
  75.0 3.3 %collective-permute-start.14 = (bf16[64,2048]{1,0:T(8,128)(2,1)S(1)}, bf16[64,2048]{1,0:T(8,128)(2,1)S(1)}, u32[]{:S(2)}, u32[]{:S(2)}) collective-permute-start(bf16[64,2048]{1,0:T(8,128)(2,1)S(1)} %get-tuple-element.90), channel_id=1, source_target_pairs={{0,7},{1,0},{2,1},{3,2},{4,3},{5,4},{6,5},{7,6},{8,15},{9,8},{10,9... | collective-permute-start | bytes 786440 | tf_op jit(solution)/shard_map/ppermute | solution.py:315
  78.4 2.1 %collective-permute-done.3.came_up = bf16[64,2048]{1,0:T(8,128)(2,1)S(1)} collective-permute-done((bf16[64,2048]{1,0:T(8,128)(2,1)S(1)}, bf16[64,2048]{1,0:T(8,128)(2,1)S(1)}, u32[]{:S(2)}, u32[]{:S(2)}) %collective-permute-start.3) | collective-permute-done | bytes 262176 | tf_op jit(solution)/shard_map/ppermute | solution.py:315
  80.7 3.3 %collective-permute-start.6 = (bf16[64,2048]{1,0:T(8,128)(2,1)S(1)}, bf16[64,2048]{1,0:T(8,128)(2,1)S(1)}, u32[]{:S(2)}, u32[]{:S(2)}) collective-permute-start(bf16[64,2048]{1,0:T(8,128)(2,1)S(1)} %get-tuple-element.74), channel_id=1, source_target_pairs={{0,7},{1,0},{2,1},{3,2},{4,3},{5,4},{6,5},{7,6},{8,15},{9,8},{10,9... | collective-permute-start | bytes 786440 | tf_op jit(solution)/shard_map/ppermute | solution.py:315
  84.0 2.1 %collective-permute-done.13.came_up = bf16[64,2048]{1,0:T(8,128)(2,1)S(1)} collective-permute-done((bf16[64,2048]{1,0:T(8,128)(2,1)S(1)}, bf16[64,2048]{1,0:T(8,128)(2,1)S(1)}, u32[]{:S(2)}, u32[]{:S(2)}) %collective-permute-start.13) | collective-permute-done | bytes 262176 | tf_op jit(solution)/shard_map/ppermute | solution.py:315
  86.7 2.9 %collective-permute-start.16 = (bf16[64,2048]{1,0:T(8,128)(2,1)S(1)}, bf16[64,2048]{1,0:T(8,128)(2,1)S(1)}, u32[]{:S(2)}, u32[]{:S(2)}) collective-permute-start(bf16[64,2048]{1,0:T(8,128)(2,1)S(1)} %get-tuple-element.94), channel_id=1, source_target_pairs={{0,7},{1,0},{2,1},{3,2},{4,3},{5,4},{6,5},{7,6},{8,15},{9,8},{10,9... | collective-permute-start | bytes 786440 | tf_op jit(solution)/shard_map/ppermute | solution.py:315
  89.6 2.1 %collective-permute-done.5.came_up = bf16[64,2048]{1,0:T(8,128)(2,1)S(1)} collective-permute-done((bf16[64,2048]{1,0:T(8,128)(2,1)S(1)}, bf16[64,2048]{1,0:T(8,128)(2,1)S(1)}, u32[]{:S(2)}, u32[]{:S(2)}) %collective-permute-start.5) | collective-permute-done | bytes 262176 | tf_op jit(solution)/shard_map/ppermute | solution.py:315
  92.3 2.9 %collective-permute-start.8 = (bf16[64,2048]{1,0:T(8,128)(2,1)S(1)}, bf16[64,2048]{1,0:T(8,128)(2,1)S(1)}, u32[]{:S(2)}, u32[]{:S(2)}) collective-permute-start(bf16[64,2048]{1,0:T(8,128)(2,1)S(1)} %get-tuple-element.78), channel_id=1, source_target_pairs={{0,7},{1,0},{2,1},{3,2},{4,3},{5,4},{6,5},{7,6},{8,15},{9,8},{10,9... | collective-permute-start | bytes 786440 | tf_op jit(solution)/shard_map/ppermute | solution.py:315
  95.2 2.1 %collective-permute-done.15.up_b = bf16[64,2048]{1,0:T(8,128)(2,1)S(1)} collective-permute-done((bf16[64,2048]{1,0:T(8,128)(2,1)S(1)}, bf16[64,2048]{1,0:T(8,128)(2,1)S(1)}, u32[]{:S(2)}, u32[]{:S(2)}) %collective-permute-start.15) | collective-permute-done | bytes 262176 | tf_op jit(solution)/shard_map/ppermute | solution.py:315
  97.3 3.5 %collective-permute-done.7.up_a = bf16[64,2048]{1,0:T(8,128)(2,1)S(1)} collective-permute-done((bf16[64,2048]{1,0:T(8,128)(2,1)S(1)}, bf16[64,2048]{1,0:T(8,128)(2,1)S(1)}, u32[]{:S(2)}, u32[]{:S(2)}) %collective-permute-start.7) | collective-permute-done | bytes 262176 | tf_op jit(solution)/shard_map/ppermute | solution.py:315
  100.8 1.5 %finish.1 = bf16[64,4096]{1,0:T(8,128)(2,1)} custom-call(f32[64,2048]{1,0:T(8,128)S(1)} %get-tuple-element.64.own_a, bf16[64,2048]{1,0:T(8,128)(2,1)S(1)} %collective-permute-done.7.up_a, bf16[64,2048]{1,0:T(8,128)(2,1)S(1)} %collective-permute-done.8.down_a, f32[64,2048]{1,0:T(8,128)S(1)} %get-tuple-element.80.own_b, ...), custom_call_target="tpu_custom_call" | custom-call | tf_op jit(solution)/shard_map/finish/pallas_call | solution.py:511
  (47 shorter events, 5.9 us)
Async XLA Ops:
  1.4 8.0 %collective-permute-start = (bf16[16,1280]{1,0:T(8,128)(2,1)}, bf16[16,1280]{1,0:T(8,128)(2,1)S(1)}, u32[]{:S(2)}, u32[]{:S(2)}) collective-permute-start(bf16[16,1280]{1,0:T(8,128)(2,1)} %tail_rows.1), channel_id=1, source_target_pairs={{0,8},{8,16},{16,24},{24,32},{32,40},{40,48},{48,56},{56,64},{64,7... | collective-permute-start | bytes 122888 | tf_op jit(solution)/shard_map/ppermute | solution.py:342
  10.0 11.4 %copy-start.7 = (f32[16]{0:T(128)S(1)}, f32[16]{0:T(128)}, u32[]{:S(2)}) copy-start(f32[16]{0:T(128)} %param.23) | copy-start | bytes 196
  12.8 17.3 %all-to-all-start = ((bf16[32,48,128]{2,1,0:T(8,128)(2,1)}), bf16[32,48,128]{2,1,0:T(8,128)(2,1)S(1)}, u32[]{:S(2)}, u32[]{:S(2)}) async-start(bf16[32,48,128]{2,1,0:T(8,128)(2,1)} %get-tuple-element.63), calls=%async_computation | async-start | bytes 786432 | tf_op jit(solution)/shard_map/all_to_all | solution.py:419
  31.0 12.9 %all-to-all-start.1 = ((bf16[32,32,128]{2,1,0:T(8,128)(2,1)}), bf16[32,32,128]{2,1,0:T(8,128)(2,1)S(1)}, u32[]{:S(2)}, u32[]{:S(2)}) async-start(bf16[32,32,128]{2,1,0:T(8,128)(2,1)} %prefix.1), calls=%async_computation.1 | async-start | bytes 524288 | tf_op jit(solution)/shard_map/all_to_all | solution.py:455
  36.1 7.8 %copy-start = (f32[512,16]{1,0:T(8,128)S(1)}, f32[512,16]{1,0:T(8,128)}, u32[]{:S(2)}) copy-start(f32[512,16]{1,0:T(8,128)} %get-tuple-element.51.run0.run1.run) | copy-start | bytes 98308
  36.1 7.8 %copy-start.1 = (bf16[512,128]{1,0:T(8,128)(2,1)S(1)}, bf16[512,128]{1,0:T(8,128)(2,1)}, u32[]{:S(2)}) copy-start(bf16[512,128]{1,0:T(8,128)(2,1)} %get-tuple-element.59.cs) | copy-start | bytes 393220
  50.7 13.0 %collective-permute-start.10 = (bf16[64,1024]{1,0:T(8,128)(2,1)S(1)}, bf16[64,1024]{1,0:T(8,128)(2,1)S(1)}, u32[]{:S(2)}, u32[]{:S(2)}) collective-permute-start(bf16[64,1024]{1,0:T(8,128)(2,1)S(1)} %get-tuple-element.82), channel_id=1, source_target_pairs={{0,7},{1,0},{2,1},{3,2},{4,3},{5,4},{6,5},{7,6},{8,15},{9,8},{10,9... | collective-permute-start | bytes 393224 | tf_op jit(solution)/shard_map/ppermute | solution.py:315
  56.7 7.6 %collective-permute-start.9 = (bf16[64,1024]{1,0:T(8,128)(2,1)S(1)}, bf16[64,1024]{1,0:T(8,128)(2,1)S(1)}, u32[]{:S(2)}, u32[]{:S(2)}) collective-permute-start(bf16[64,1024]{1,0:T(8,128)(2,1)S(1)} %get-tuple-element.81), channel_id=1, source_target_pairs={{0,1},{1,2},{2,3},{3,4},{4,5},{5,6},{6,7},{7,0},{8,9},{9,10},{10,1... | collective-permute-start | bytes 393224 | tf_op jit(solution)/shard_map/ppermute | solution.py:315
  56.7 11.0 %collective-permute-start.1 = (bf16[64,1024]{1,0:T(8,128)(2,1)S(1)}, bf16[64,1024]{1,0:T(8,128)(2,1)S(1)}, u32[]{:S(2)}, u32[]{:S(2)}) collective-permute-start(bf16[64,1024]{1,0:T(8,128)(2,1)S(1)} %get-tuple-element.65), channel_id=1, source_target_pairs={{0,1},{1,2},{2,3},{3,4},{4,5},{5,6},{6,7},{7,0},{8,9},{9,10},{10,1... | collective-permute-start | bytes 393224 | tf_op jit(solution)/shard_map/ppermute | solution.py:315
  56.7 11.0 %collective-permute-start.2 = (bf16[64,1024]{1,0:T(8,128)(2,1)S(1)}, bf16[64,1024]{1,0:T(8,128)(2,1)S(1)}, u32[]{:S(2)}, u32[]{:S(2)}) collective-permute-start(bf16[64,1024]{1,0:T(8,128)(2,1)S(1)} %get-tuple-element.66), channel_id=1, source_target_pairs={{0,7},{1,0},{2,1},{3,2},{4,3},{5,4},{6,5},{7,6},{8,15},{9,8},{10,9... | collective-permute-start | bytes 393224 | tf_op jit(solution)/shard_map/ppermute | solution.py:315
  64.3 10.5 %collective-permute-start.11 = (bf16[64,2048]{1,0:T(8,128)(2,1)S(1)}, bf16[64,2048]{1,0:T(8,128)(2,1)S(1)}, u32[]{:S(2)}, u32[]{:S(2)}) collective-permute-start(bf16[64,2048]{1,0:T(8,128)(2,1)S(1)} %get-tuple-element.85), channel_id=1, source_target_pairs={{0,1},{1,2},{2,3},{3,4},{4,5},{5,6},{6,7},{7,0},{8,9},{9,10},{10,1... | collective-permute-start | bytes 786440 | tf_op jit(solution)/shard_map/ppermute | solution.py:315
  64.4 10.4 %collective-permute-start.12 = (bf16[64,2048]{1,0:T(8,128)(2,1)S(1)}, bf16[64,2048]{1,0:T(8,128)(2,1)S(1)}, u32[]{:S(2)}, u32[]{:S(2)}) collective-permute-start(bf16[64,2048]{1,0:T(8,128)(2,1)S(1)} %get-tuple-element.86), channel_id=1, source_target_pairs={{0,7},{1,0},{2,1},{3,2},{4,3},{5,4},{6,5},{7,6},{8,15},{9,8},{10,9... | collective-permute-start | bytes 786440 | tf_op jit(solution)/shard_map/ppermute | solution.py:315
  67.7 12.8 %collective-permute-start.3 = (bf16[64,2048]{1,0:T(8,128)(2,1)S(1)}, bf16[64,2048]{1,0:T(8,128)(2,1)S(1)}, u32[]{:S(2)}, u32[]{:S(2)}) collective-permute-start(bf16[64,2048]{1,0:T(8,128)(2,1)S(1)} %get-tuple-element.69), channel_id=1, source_target_pairs={{0,1},{1,2},{2,3},{3,4},{4,5},{5,6},{6,7},{7,0},{8,9},{9,10},{10,1... | collective-permute-start | bytes 786440 | tf_op jit(solution)/shard_map/ppermute | solution.py:315
  67.8 12.7 %collective-permute-start.4 = (bf16[64,2048]{1,0:T(8,128)(2,1)S(1)}, bf16[64,2048]{1,0:T(8,128)(2,1)S(1)}, u32[]{:S(2)}, u32[]{:S(2)}) collective-permute-start(bf16[64,2048]{1,0:T(8,128)(2,1)S(1)} %get-tuple-element.70), channel_id=1, source_target_pairs={{0,7},{1,0},{2,1},{3,2},{4,3},{5,4},{6,5},{7,6},{8,15},{9,8},{10,9... | collective-permute-start | bytes 786440 | tf_op jit(solution)/shard_map/ppermute | solution.py:315
  75.0 11.1 %collective-permute-start.13 = (bf16[64,2048]{1,0:T(8,128)(2,1)S(1)}, bf16[64,2048]{1,0:T(8,128)(2,1)S(1)}, u32[]{:S(2)}, u32[]{:S(2)}) collective-permute-start(bf16[64,2048]{1,0:T(8,128)(2,1)S(1)} %get-tuple-element.89), channel_id=1, source_target_pairs={{0,1},{1,2},{2,3},{3,4},{4,5},{5,6},{6,7},{7,0},{8,9},{9,10},{10,1... | collective-permute-start | bytes 786440 | tf_op jit(solution)/shard_map/ppermute | solution.py:315
  75.0 11.1 %collective-permute-start.14 = (bf16[64,2048]{1,0:T(8,128)(2,1)S(1)}, bf16[64,2048]{1,0:T(8,128)(2,1)S(1)}, u32[]{:S(2)}, u32[]{:S(2)}) collective-permute-start(bf16[64,2048]{1,0:T(8,128)(2,1)S(1)} %get-tuple-element.90), channel_id=1, source_target_pairs={{0,7},{1,0},{2,1},{3,2},{4,3},{5,4},{6,5},{7,6},{8,15},{9,8},{10,9... | collective-permute-start | bytes 786440 | tf_op jit(solution)/shard_map/ppermute | solution.py:315
  80.5 14.7 %copy-start.5 = (s32[4096]{0:T(1024)S(1)}, s32[4096]{0:T(1024)}, u32[]{:S(2)}) copy-start(s32[4096]{0:T(1024)} %param.27) | copy-start | bytes 49156
  80.5 14.7 %copy-start.6 = (s32[4096]{0:T(1024)S(1)}, s32[4096]{0:T(1024)}, u32[]{:S(2)}) copy-start(s32[4096]{0:T(1024)} %param.26) | copy-start | bytes 49156
  80.6 11.1 %collective-permute-start.5 = (bf16[64,2048]{1,0:T(8,128)(2,1)S(1)}, bf16[64,2048]{1,0:T(8,128)(2,1)S(1)}, u32[]{:S(2)}, u32[]{:S(2)}) collective-permute-start(bf16[64,2048]{1,0:T(8,128)(2,1)S(1)} %get-tuple-element.73), channel_id=1, source_target_pairs={{0,1},{1,2},{2,3},{3,4},{4,5},{5,6},{6,7},{7,0},{8,9},{9,10},{10,1... | collective-permute-start | bytes 786440 | tf_op jit(solution)/shard_map/ppermute | solution.py:315
  80.7 11.0 %collective-permute-start.6 = (bf16[64,2048]{1,0:T(8,128)(2,1)S(1)}, bf16[64,2048]{1,0:T(8,128)(2,1)S(1)}, u32[]{:S(2)}, u32[]{:S(2)}) collective-permute-start(bf16[64,2048]{1,0:T(8,128)(2,1)S(1)} %get-tuple-element.74), channel_id=1, source_target_pairs={{0,7},{1,0},{2,1},{3,2},{4,3},{5,4},{6,5},{7,6},{8,15},{9,8},{10,9... | collective-permute-start | bytes 786440 | tf_op jit(solution)/shard_map/ppermute | solution.py:315
  86.2 11.1 %collective-permute-start.15 = (bf16[64,2048]{1,0:T(8,128)(2,1)S(1)}, bf16[64,2048]{1,0:T(8,128)(2,1)S(1)}, u32[]{:S(2)}, u32[]{:S(2)}) collective-permute-start(bf16[64,2048]{1,0:T(8,128)(2,1)S(1)} %get-tuple-element.93), channel_id=1, source_target_pairs={{0,1},{1,2},{2,3},{3,4},{4,5},{5,6},{6,7},{7,0},{8,9},{9,10},{10,1... | collective-permute-start | bytes 786440 | tf_op jit(solution)/shard_map/ppermute | solution.py:315
  86.7 10.6 %collective-permute-start.16 = (bf16[64,2048]{1,0:T(8,128)(2,1)S(1)}, bf16[64,2048]{1,0:T(8,128)(2,1)S(1)}, u32[]{:S(2)}, u32[]{:S(2)}) collective-permute-start(bf16[64,2048]{1,0:T(8,128)(2,1)S(1)} %get-tuple-element.94), channel_id=1, source_target_pairs={{0,7},{1,0},{2,1},{3,2},{4,3},{5,4},{6,5},{7,6},{8,15},{9,8},{10,9... | collective-permute-start | bytes 786440 | tf_op jit(solution)/shard_map/ppermute | solution.py:315
  91.8 9.0 %collective-permute-start.7 = (bf16[64,2048]{1,0:T(8,128)(2,1)S(1)}, bf16[64,2048]{1,0:T(8,128)(2,1)S(1)}, u32[]{:S(2)}, u32[]{:S(2)}) collective-permute-start(bf16[64,2048]{1,0:T(8,128)(2,1)S(1)} %get-tuple-element.77), channel_id=1, source_target_pairs={{0,1},{1,2},{2,3},{3,4},{4,5},{5,6},{6,7},{7,0},{8,9},{9,10},{10,1... | collective-permute-start | bytes 786440 | tf_op jit(solution)/shard_map/ppermute | solution.py:315
  92.3 8.5 %collective-permute-start.8 = (bf16[64,2048]{1,0:T(8,128)(2,1)S(1)}, bf16[64,2048]{1,0:T(8,128)(2,1)S(1)}, u32[]{:S(2)}, u32[]{:S(2)}) collective-permute-start(bf16[64,2048]{1,0:T(8,128)(2,1)S(1)} %get-tuple-element.78), channel_id=1, source_target_pairs={{0,7},{1,0},{2,1},{3,2},{4,3},{5,4},{6,5},{7,6},{8,15},{9,8},{10,9... | collective-permute-start | bytes 786440 | tf_op jit(solution)/shard_map/ppermute | solution.py:315
  (3 other events, 16.2 us)

commit v7 on v6

--- a/solution.py
+++ b/solution.py
@@ -82,6 +82,16 @@
     out[:, CH + STATE :] = c[...]
 
 
+def head_spread(row):
+    a = lax.broadcasted_iota(jnp.int32, (HEADS_LOCAL, HEADS_LOCAL), 0)
+    b = lax.broadcasted_iota(jnp.int32, (HEADS_LOCAL, HEADS_LOCAL), 1)
+    column = jnp.sum(jnp.where(a == b, row, 0.0), axis=1, keepdims=True)
+    channel = lax.broadcasted_iota(jnp.int32, (CH, 3 * HEADS_LOCAL), 0)
+    head = lax.broadcasted_iota(jnp.int32, (CH, 3 * HEADS_LOCAL), 1)
+    pattern = (channel // HEAD_DIM == head % HEADS_LOCAL).astype(F32).astype(BF16)
+    return dot(pattern, split(jnp.broadcast_to(column, (HEADS_LOCAL, STATE)), 0))
+
+
 def scan_in(x, b, c, step_t, decay_t, tap_x, tap_b, tap_c, xs_o, bs_o, cs_o, run_o, toward_o, one_o, two_o, pad, parts):
     tile = pl.program_id(0)
 
@@ -134,10 +144,9 @@
     first_o[...] = first
     end0 = run0[7:8]
     end1 = run1[7:8]
-    state = jnp.exp(head_columns(0, CH, end1)) * first + two[...]
+    state = jnp.exp(head_spread(end1)) * first + two[...]
     pay_o[:, 0:PIECE, :] = state.astype(BF16).reshape(PARTS, PIECE, STATE)
-    total = head_columns(0, CH, end0 + end1).reshape(PARTS, PIECE, 1)[:, 0 : PAY - PIECE, :]
-    total = jnp.broadcast_to(total, (PARTS, PAY - PIECE, STATE))
+    total = head_spread(end0 + end1).reshape(PARTS, PIECE, STATE)[:, 0 : PAY - PIECE, :]
     high = total.astype(BF16).astype(F32)
     rest = total - high
     middle = rest.astype(BF16).astype(F32)
@@ -214,7 +223,7 @@
     start = incoming[...]
     for step in range(steps):
         if step == SPAN // ROWS:
-            decay = jnp.exp(head_columns(0, CH, run[SPAN - 1 : SPAN]))
+            decay = jnp.exp(head_spread(run[SPAN - 1 : SPAN]))
             start = (decay * incoming[...].astype(F32) + first[...]).astype(BF16)
         rows = slice(step * ROWS, (step + 1) * ROWS)
         carried = dot(cs[rows], start, ((1,), (1,)))
@@ -272,7 +281,8 @@
     down_o[...] = (came_down[...].astype(F32) + part_down[...]).astype(BF16)
 
 
-def finish(own_a, up_a, down_a, own_b, up_b, down_b, scale, out):
+def finish(group, own, up, down, scale, *refs):
+    out = refs[-1]
     row = lax.broadcasted_iota(jnp.int32, (HAD_BLOCK, HAD_BLOCK), 0)
     column = lax.broadcasted_iota(jnp.int32, (HAD_BLOCK, HAD_BLOCK), 1)
     ones = row & column
@@ -280,22 +290,18 @@
     ones = ones ^ (ones >> 2)
     ones = ones ^ (ones >> 1)
     table = (1 - 2 * (ones & 1)).astype(F32).astype(BF16)
-    half = up_a.shape[1]
-    for group, (own, up, down) in enumerate(((own_a, up_a, down_a), (own_b, up_b, down_b))):
-        at = slice(group * half, (group + 1) * half)
-        total = (own[...] + up[...].astype(F32) + down[...].astype(F32)) * scale[:, at]
-        stacked = jnp.concatenate(
-            [total[:, k * HAD_BLOCK : (k + 1) * HAD_BLOCK] for k in range(half // HAD_BLOCK)], 0
-        )
-        high = stacked.astype(BF16)
-        rest = stacked - high.astype(F32)
-        middle = rest.astype(BF16)
-        low = (rest - middle.astype(F32)).astype(BF16)
-        rotated = dot(high, table) + dot(middle, table) + dot(low, table)
-        rotated = (rotated * (1.0 / math.sqrt(HAD_BLOCK))).astype(BF16)
-        for k in range(half // HAD_BLOCK):
-            lanes = slice(group * half + k * HAD_BLOCK, group * half + (k + 1) * HAD_BLOCK)
-            out[:, lanes] = rotated[k * SHARE : (k + 1) * SHARE]
+    half = up.shape[1]
+    at = slice(group * half, (group + 1) * half)
+    total = (own[...] + up[...].astype(F32) + down[...].astype(F32)) * scale[:, at]
+    stacked = jnp.concatenate([total[:, k * HAD_BLOCK : (k + 1) * HAD_BLOCK] for k in range(half // HAD_BLOCK)], 0)
+    high = stacked.astype(BF16)
+    rest = stacked - high.astype(F32)
+    middle = rest.astype(BF16)
+    low = (rest - middle.astype(F32)).astype(BF16)
+    rotated = dot(high, table) + dot(middle, table) + dot(low, table)
+    rotated = (rotated * (1.0 / math.sqrt(HAD_BLOCK))).astype(BF16)
+    for k in range(half // HAD_BLOCK):
+        out[:, k * HAD_BLOCK : (k + 1) * HAD_BLOCK] = rotated[k * SHARE : (k + 1) * SHARE]
 
 
 def whole(shape):
@@ -508,14 +514,21 @@
             up, down = ring(up, 1), ring(down, -1)
             up, down = add(add_far if distance == 3 else add_two, up, down, mine[distance], mine[-distance])
         ends += [mine[0], ring(up, 1), ring(down, -1)]
-    return pl.pallas_call(
-        finish,
-        in_specs=[vmem] * 7,
-        out_specs=vmem,
-        out_shape=shape((SHARE, model), BF16),
-        compiler_params=params(LIMIT["ring"]),
-        name="finish",
-    )(*ends, scale[None, :])
+    result = []
+    for group in (1, 0):
+        result = [
+            pl.pallas_call(
+                functools.partial(finish, group),
+                grid=(1,),
+                in_specs=[vmem] * 4 + [anywhere] * len(result),
+                out_specs=block((SHARE, half), 0, group),
+                out_shape=shape((SHARE, model), BF16),
+                input_output_aliases={4: 0} if result else {},
+                compiler_params=params(LIMIT["ring"]),
+                name="finish",
+            )(*ends[3 * group : 3 * group + 3], scale[None, :], *result)
+        ]
+    return result[0]
 
 
 def solution(mesh):

time: 103 us -> 102 us (level)
  waiting for transfers between devices: 24.2 us -> 23.1 us
    ppermute x16, waiting for transfers between devices: 16.2 us -> 15.1 us  [ring(): lax.ppermute(value, 'tp', [(k, (k + step) % count) for k in range(count)])]
    pallas_call x1 -> x2, Pallas kernels: 1.5 us -> 2.2 us  [local(): pl.pallas_call(functools.partial(finish, group), grid=(1,), in_specs=[vme...]
  transfers between devices with their start and end apart: 19 -> 19, of which waited for: 8 -> 8; matrix products, arithmetic and copies ran while one was open for 1% -> 1% of each run, Pallas kernels for 18% -> 19%
where the time goes in v7:
time: 102 us
  starting transfers between devices  45 us (44%)
  Pallas kernels  32.1 us (31%)
  waiting for transfers between devices  23.1 us (23%)
  local copies, waits for them, and re-layouts  1.38 us (1%)
    ppermute x16, starting transfers between devices, ring(): lax.ppermute(value, 'tp', [(k, (k + step) % count) for k in range(count)])  29.4 us
    ppermute x16, waiting for transfers between devices, ring(): lax.ppermute(value, 'tp', [(k, (k + step) % count) for k in range(count)])  15.1 us
    all_to_all x1, starting transfers between devices, local(): got = lax.all_to_all(pay, 'seq', 0, 0, tiled=True)  8.61 us
    all_to_all x1, waiting for transfers between devices, local(): got = lax.all_to_all(pay, 'seq', 0, 0, tiled=True)  7.97 us
    pallas_call x1, Pallas kernels, local(): pl.pallas_call(inside, grid=(tiles,), in_specs=[tiled((TOK, TILE), 1), wh...  7.76 us
    pallas_call x1, Pallas kernels, local(): pl.pallas_call(norm_project, in_specs=[anywhere] * 2 + [vmem] * 5 + [anyw...  6.77 us
    pallas_call x1, Pallas kernels, local(): pl.pallas_call(scan_in, grid=(CH // SCAN_TILE,), in_specs=[tiled((TOK, SC...  6.07 us
    all_to_all x1, starting transfers between devices, local(): lax.all_to_all(before, 'seq', 0, 0, tiled=True).reshape(CH, STATE)  5.12 us
  transfers between devices with their start and end apart: 19, of which 8 were waited for; matrix products, arithmetic and copies ran while one was open for 1% of the time, Pallas kernels for 19%

profile of v7, /device:TPU:2, one launch (start us, length us, event | category | flops | bytes accessed | tf_op | source)
XLA Modules:
  0.0 101.8 jit_solution(13324269480187179935)
XLA Ops:
  0.0 1.4 %tail_rows.1 = bf16[16,1280]{1,0:T(8,128)(2,1)} custom-call(bf16[512,1024]{1,0:T(8,128)(2,1)} %x.5, bf16[512,128]{1,0:T(8,128)(2,1)} %b.5, bf16[512,128]{1,0:T(8,128)(2,1)} %c.5), custom_call_target="tpu_custom_call" | custom-call | tf_op jit(solution)/shard_map/tail_rows/pallas_call | solution.py:339
  1.4 1.9 %collective-permute-start = (bf16[16,1280]{1,0:T(8,128)(2,1)}, bf16[16,1280]{1,0:T(8,128)(2,1)S(1)}, u32[]{:S(2)}, u32[]{:S(2)}) collective-permute-start(bf16[16,1280]{1,0:T(8,128)(2,1)} %tail_rows.1), channel_id=1, source_target_pairs={{0,8},{8,16},{16,24},{24,32},{32,40},{40,48},{48,56},{56,64},{64,7... | collective-permute-start | bytes 122888 | tf_op jit(solution)/shard_map/ppermute | solution.py:348
  3.3 6.1 %scan_in.1 = (bf16[512,1024]{1,0:T(8,128)(2,1)}, bf16[512,128]{1,0:T(8,128)(2,1)}, bf16[512,128]{1,0:T(8,128)(2,1)}, f32[512,16]{1,0:T(8,128)}, f32[512,16]{1,0:...) custom-call(bf16[512,1024]{1,0:T(8,128)(2,1)} %x.5, bf16[512,128]{1,0:T(8,128)(2,1)} %b.5, bf16[512,128]{1,0:T(8,128)(2,1)} %c.5, ...), custom_call_target="tpu_custom_call" | custom-call | flops 1000000000 | bytes 4000000 | tf_op jit(solution)/shard_map/scan_in/pallas_call | solution.py:349
  10.0 2.8 %scan_edge.1 = (bf16[512,1024]{1,0:T(8,128)(2,1)}, bf16[512,128]{1,0:T(8,128)(2,1)}, bf16[512,128]{1,0:T(8,128)(2,1)}, f32[1024,128]{1,0:T(8,128)}, bf16[32,48,128]{2,1,0:T(8,128)(2,1)}) custom-call(bf16[16,1280]{1,0:T(8,128)(2,1)} %copy-done.4, bf16[512,1024]{1,0:T(8,128)(2,1)} %x.5, ...), custom_call_target="tpu_custom_call", output_to_operand_aliasing={{0}: (12, {}), {1}: (13, {}), {2}: (14, {})} | custom-call | tf_op jit(solution)/shard_map/scan_edge/pallas_call | solution.py:386
  12.8 8.6 %all-to-all-start = ((bf16[32,48,128]{2,1,0:T(8,128)(2,1)}), bf16[32,48,128]{2,1,0:T(8,128)(2,1)S(1)}, u32[]{:S(2)}, u32[]{:S(2)}) async-start(bf16[32,48,128]{2,1,0:T(8,128)(2,1)} %get-tuple-element.63), calls=%async_computation | async-start | bytes 786432 | tf_op jit(solution)/shard_map/all_to_all | solution.py:425
  22.2 8.0 %all-to-all-done.got = bf16[32,48,128]{2,1,0:T(8,128)(2,1)S(1)} async-done(((bf16[32,48,128]{2,1,0:T(8,128)(2,1)}), bf16[32,48,128]{2,1,0:T(8,128)(2,1)S(1)}, u32[]{:S(2)}, u32[]{:S(2)}) %all-to-all-start) | async-done | bytes 393248 | tf_op jit(solution)/shard_map/all_to_all | solution.py:425
  30.9 5.1 %all-to-all-start.1 = ((bf16[32,32,128]{2,1,0:T(8,128)(2,1)}), bf16[32,32,128]{2,1,0:T(8,128)(2,1)S(1)}, u32[]{:S(2)}, u32[]{:S(2)}) async-start(bf16[32,32,128]{2,1,0:T(8,128)(2,1)} %prefix.1), calls=%async_computation.1 | async-start | bytes 524288 | tf_op jit(solution)/shard_map/all_to_all | solution.py:461
  36.1 7.8 %inside.1 = (f32[512,1024]{1,0:T(8,128)}, f32[512,1024]{1,0:T(8,128)}) custom-call(bf16[512,1024]{1,0:T(8,128)(2,1)} %get-tuple-element.57.xs, bf16[512,128]{1,0:T(8,128)(2,1)} %get-tuple-element.58.bs, bf16[512,128]{1,0:T(8,128)(2,1)} %get-tuple-element.59.cs, f32[512,16]{1,0:T(8,128)} %get-tuple-element.51.run0.run1.run, f32[16,512]{1,0:T(8,128)} %bitcast.12, ...), custom_call_target="tpu_custom_call" | custom-call | flops 4000000000 | bytes 6000000 | tf_op jit(solution)/shard_map/inside/pallas_call | solution.py:426
  43.9 6.8 %norm_project.1 = (bf16[512,1024]{1,0:T(8,128)(2,1)S(1)}, bf16[64,1024]{1,0:T(8,128)(2,1)S(1)}, bf16[64,1024]{1,0:T(8,128)(2,1)S(1)}, bf16[64,1024]{1,0:T(8,128)...) custom-call(f32[512,1024]{1,0:T(8,128)} %get-tuple-element.60.y, ...), custom_call_target="tpu_custom_call" | custom-call | flops 1000000000 | bytes 10000000 | tf_op jit(solution)/shard_map/norm_project/pallas_call | solution.py:467
  50.7 5.9 %collective-permute-start.10 = (bf16[64,1024]{1,0:T(8,128)(2,1)S(1)}, bf16[64,1024]{1,0:T(8,128)(2,1)S(1)}, u32[]{:S(2)}, u32[]{:S(2)}) collective-permute-start(bf16[64,1024]{1,0:T(8,128)(2,1)S(1)} %get-tuple-element.82), channel_id=1, source_target_pairs={{0,7},{1,0},{2,1},{3,2},{4,3},{5,4},{6,5},{7,6},{8,15},{9,8},{10,9... | collective-permute-start | bytes 393224 | tf_op jit(solution)/shard_map/ppermute | solution.py:321
  56.6 3.3 %collective-permute-start.2 = (bf16[64,1024]{1,0:T(8,128)(2,1)S(1)}, bf16[64,1024]{1,0:T(8,128)(2,1)S(1)}, u32[]{:S(2)}, u32[]{:S(2)}) collective-permute-start(bf16[64,1024]{1,0:T(8,128)(2,1)S(1)} %get-tuple-element.66), channel_id=1, source_target_pairs={{0,7},{1,0},{2,1},{3,2},{4,3},{5,4},{6,5},{7,6},{8,15},{9,8},{10,9... | collective-permute-start | bytes 393224 | tf_op jit(solution)/shard_map/ppermute | solution.py:321
  59.9 3.8 %project.1 = (f32[64,2048]{1,0:T(8,128)S(1)}, f32[64,2048]{1,0:T(8,128)S(1)}, f32[64,2048]{1,0:T(8,128)S(1)}, f32[64,2048]{1,0:T(8,128)S(1)}, f32[64,2048]{1,0:T...) custom-call(bf16[512,1024]{1,0:T(8,128)(2,1)S(1)} %get-tuple-element.79.normed, bf16[1024,4096]{1,0:T(8,128)(2,1)} %weight.3), custom_call_target="tpu_custom_call" | custom-call | flops 10 | bytes 10 | tf_op jit(solution)/shard_map/project/pallas_call | solution.py:483
  64.4 3.2 %collective-permute-start.12 = (bf16[64,2048]{1,0:T(8,128)(2,1)S(1)}, bf16[64,2048]{1,0:T(8,128)(2,1)S(1)}, u32[]{:S(2)}, u32[]{:S(2)}) collective-permute-start(bf16[64,2048]{1,0:T(8,128)(2,1)S(1)} %get-tuple-element.86), channel_id=1, source_target_pairs={{0,7},{1,0},{2,1},{3,2},{4,3},{5,4},{6,5},{7,6},{8,15},{9,8},{10,9... | collective-permute-start | bytes 786440 | tf_op jit(solution)/shard_map/ppermute | solution.py:321
  67.8 3.2 %collective-permute-start.4 = (bf16[64,2048]{1,0:T(8,128)(2,1)S(1)}, bf16[64,2048]{1,0:T(8,128)(2,1)S(1)}, u32[]{:S(2)}, u32[]{:S(2)}) collective-permute-start(bf16[64,2048]{1,0:T(8,128)(2,1)S(1)} %get-tuple-element.70), channel_id=1, source_target_pairs={{0,7},{1,0},{2,1},{3,2},{4,3},{5,4},{6,5},{7,6},{8,15},{9,8},{10,9... | collective-permute-start | bytes 786440 | tf_op jit(solution)/shard_map/ppermute | solution.py:321
  71.0 3.8 %collective-permute-done.11.came_up = bf16[64,2048]{1,0:T(8,128)(2,1)S(1)} collective-permute-done((bf16[64,2048]{1,0:T(8,128)(2,1)S(1)}, bf16[64,2048]{1,0:T(8,128)(2,1)S(1)}, u32[]{:S(2)}, u32[]{:S(2)}) %collective-permute-start.11) | collective-permute-done | bytes 262176 | tf_op jit(solution)/shard_map/ppermute | solution.py:321
  75.0 3.3 %collective-permute-start.14 = (bf16[64,2048]{1,0:T(8,128)(2,1)S(1)}, bf16[64,2048]{1,0:T(8,128)(2,1)S(1)}, u32[]{:S(2)}, u32[]{:S(2)}) collective-permute-start(bf16[64,2048]{1,0:T(8,128)(2,1)S(1)} %get-tuple-element.90), channel_id=1, source_target_pairs={{0,7},{1,0},{2,1},{3,2},{4,3},{5,4},{6,5},{7,6},{8,15},{9,8},{10,9... | collective-permute-start | bytes 786440 | tf_op jit(solution)/shard_map/ppermute | solution.py:321
  78.3 2.1 %collective-permute-done.3.came_up = bf16[64,2048]{1,0:T(8,128)(2,1)S(1)} collective-permute-done((bf16[64,2048]{1,0:T(8,128)(2,1)S(1)}, bf16[64,2048]{1,0:T(8,128)(2,1)S(1)}, u32[]{:S(2)}, u32[]{:S(2)}) %collective-permute-start.3) | collective-permute-done | bytes 262176 | tf_op jit(solution)/shard_map/ppermute | solution.py:321
  80.6 3.3 %collective-permute-start.6 = (bf16[64,2048]{1,0:T(8,128)(2,1)S(1)}, bf16[64,2048]{1,0:T(8,128)(2,1)S(1)}, u32[]{:S(2)}, u32[]{:S(2)}) collective-permute-start(bf16[64,2048]{1,0:T(8,128)(2,1)S(1)} %get-tuple-element.74), channel_id=1, source_target_pairs={{0,7},{1,0},{2,1},{3,2},{4,3},{5,4},{6,5},{7,6},{8,15},{9,8},{10,9... | collective-permute-start | bytes 786440 | tf_op jit(solution)/shard_map/ppermute | solution.py:321
  83.9 2.1 %collective-permute-done.13.came_up = bf16[64,2048]{1,0:T(8,128)(2,1)S(1)} collective-permute-done((bf16[64,2048]{1,0:T(8,128)(2,1)S(1)}, bf16[64,2048]{1,0:T(8,128)(2,1)S(1)}, u32[]{:S(2)}, u32[]{:S(2)}) %collective-permute-start.13) | collective-permute-done | bytes 262176 | tf_op jit(solution)/shard_map/ppermute | solution.py:321
  86.6 2.9 %collective-permute-start.16 = (bf16[64,2048]{1,0:T(8,128)(2,1)S(1)}, bf16[64,2048]{1,0:T(8,128)(2,1)S(1)}, u32[]{:S(2)}, u32[]{:S(2)}) collective-permute-start(bf16[64,2048]{1,0:T(8,128)(2,1)S(1)} %get-tuple-element.94), channel_id=1, source_target_pairs={{0,7},{1,0},{2,1},{3,2},{4,3},{5,4},{6,5},{7,6},{8,15},{9,8},{10,9... | collective-permute-start | bytes 786440 | tf_op jit(solution)/shard_map/ppermute | solution.py:321
  89.5 2.1 %collective-permute-done.5.came_up = bf16[64,2048]{1,0:T(8,128)(2,1)S(1)} collective-permute-done((bf16[64,2048]{1,0:T(8,128)(2,1)S(1)}, bf16[64,2048]{1,0:T(8,128)(2,1)S(1)}, u32[]{:S(2)}, u32[]{:S(2)}) %collective-permute-start.5) | collective-permute-done | bytes 262176 | tf_op jit(solution)/shard_map/ppermute | solution.py:321
  92.3 2.9 %collective-permute-start.8 = (bf16[64,2048]{1,0:T(8,128)(2,1)S(1)}, bf16[64,2048]{1,0:T(8,128)(2,1)S(1)}, u32[]{:S(2)}, u32[]{:S(2)}) collective-permute-start(bf16[64,2048]{1,0:T(8,128)(2,1)S(1)} %get-tuple-element.78), channel_id=1, source_target_pairs={{0,7},{1,0},{2,1},{3,2},{4,3},{5,4},{6,5},{7,6},{8,15},{9,8},{10,9... | collective-permute-start | bytes 786440 | tf_op jit(solution)/shard_map/ppermute | solution.py:321
  95.2 2.1 %collective-permute-done.15.up = bf16[64,2048]{1,0:T(8,128)(2,1)S(1)} collective-permute-done((bf16[64,2048]{1,0:T(8,128)(2,1)S(1)}, bf16[64,2048]{1,0:T(8,128)(2,1)S(1)}, u32[]{:S(2)}, u32[]{:S(2)}) %collective-permute-start.15) | collective-permute-done | bytes 262176 | tf_op jit(solution)/shard_map/ppermute | solution.py:321
  98.4 2.3 %collective-permute-done.7.up = bf16[64,2048]{1,0:T(8,128)(2,1)S(1)} collective-permute-done((bf16[64,2048]{1,0:T(8,128)(2,1)S(1)}, bf16[64,2048]{1,0:T(8,128)(2,1)S(1)}, u32[]{:S(2)}, u32[]{:S(2)}) %collective-permute-start.7) | collective-permute-done | bytes 262176 | tf_op jit(solution)/shard_map/ppermute | solution.py:321
  (48 shorter events, 6.7 us)
Async XLA Ops:
  1.4 8.0 %collective-permute-start = (bf16[16,1280]{1,0:T(8,128)(2,1)}, bf16[16,1280]{1,0:T(8,128)(2,1)S(1)}, u32[]{:S(2)}, u32[]{:S(2)}) collective-permute-start(bf16[16,1280]{1,0:T(8,128)(2,1)} %tail_rows.1), channel_id=1, source_target_pairs={{0,8},{8,16},{16,24},{24,32},{32,40},{40,48},{48,56},{56,64},{64,7... | collective-permute-start | bytes 122888 | tf_op jit(solution)/shard_map/ppermute | solution.py:348
  10.0 11.4 %copy-start.7 = (f32[16]{0:T(128)S(1)}, f32[16]{0:T(128)}, u32[]{:S(2)}) copy-start(f32[16]{0:T(128)} %param.23) | copy-start | bytes 196
  12.8 17.3 %all-to-all-start = ((bf16[32,48,128]{2,1,0:T(8,128)(2,1)}), bf16[32,48,128]{2,1,0:T(8,128)(2,1)S(1)}, u32[]{:S(2)}, u32[]{:S(2)}) async-start(bf16[32,48,128]{2,1,0:T(8,128)(2,1)} %get-tuple-element.63), calls=%async_computation | async-start | bytes 786432 | tf_op jit(solution)/shard_map/all_to_all | solution.py:425
  30.9 12.9 %all-to-all-start.1 = ((bf16[32,32,128]{2,1,0:T(8,128)(2,1)}), bf16[32,32,128]{2,1,0:T(8,128)(2,1)S(1)}, u32[]{:S(2)}, u32[]{:S(2)}) async-start(bf16[32,32,128]{2,1,0:T(8,128)(2,1)} %prefix.1), calls=%async_computation.1 | async-start | bytes 524288 | tf_op jit(solution)/shard_map/all_to_all | solution.py:461
  36.1 7.8 %copy-start = (f32[512,16]{1,0:T(8,128)S(1)}, f32[512,16]{1,0:T(8,128)}, u32[]{:S(2)}) copy-start(f32[512,16]{1,0:T(8,128)} %get-tuple-element.51.run0.run1.run) | copy-start | bytes 98308
  36.1 7.8 %copy-start.1 = (bf16[512,128]{1,0:T(8,128)(2,1)S(1)}, bf16[512,128]{1,0:T(8,128)(2,1)}, u32[]{:S(2)}) copy-start(bf16[512,128]{1,0:T(8,128)(2,1)} %get-tuple-element.59.cs) | copy-start | bytes 393220
  50.7 13.0 %collective-permute-start.10 = (bf16[64,1024]{1,0:T(8,128)(2,1)S(1)}, bf16[64,1024]{1,0:T(8,128)(2,1)S(1)}, u32[]{:S(2)}, u32[]{:S(2)}) collective-permute-start(bf16[64,1024]{1,0:T(8,128)(2,1)S(1)} %get-tuple-element.82), channel_id=1, source_target_pairs={{0,7},{1,0},{2,1},{3,2},{4,3},{5,4},{6,5},{7,6},{8,15},{9,8},{10,9... | collective-permute-start | bytes 393224 | tf_op jit(solution)/shard_map/ppermute | solution.py:321
  56.6 7.6 %collective-permute-start.9 = (bf16[64,1024]{1,0:T(8,128)(2,1)S(1)}, bf16[64,1024]{1,0:T(8,128)(2,1)S(1)}, u32[]{:S(2)}, u32[]{:S(2)}) collective-permute-start(bf16[64,1024]{1,0:T(8,128)(2,1)S(1)} %get-tuple-element.81), channel_id=1, source_target_pairs={{0,1},{1,2},{2,3},{3,4},{4,5},{5,6},{6,7},{7,0},{8,9},{9,10},{10,1... | collective-permute-start | bytes 393224 | tf_op jit(solution)/shard_map/ppermute | solution.py:321
  56.6 11.0 %collective-permute-start.1 = (bf16[64,1024]{1,0:T(8,128)(2,1)S(1)}, bf16[64,1024]{1,0:T(8,128)(2,1)S(1)}, u32[]{:S(2)}, u32[]{:S(2)}) collective-permute-start(bf16[64,1024]{1,0:T(8,128)(2,1)S(1)} %get-tuple-element.65), channel_id=1, source_target_pairs={{0,1},{1,2},{2,3},{3,4},{4,5},{5,6},{6,7},{7,0},{8,9},{9,10},{10,1... | collective-permute-start | bytes 393224 | tf_op jit(solution)/shard_map/ppermute | solution.py:321
  56.6 11.0 %collective-permute-start.2 = (bf16[64,1024]{1,0:T(8,128)(2,1)S(1)}, bf16[64,1024]{1,0:T(8,128)(2,1)S(1)}, u32[]{:S(2)}, u32[]{:S(2)}) collective-permute-start(bf16[64,1024]{1,0:T(8,128)(2,1)S(1)} %get-tuple-element.66), channel_id=1, source_target_pairs={{0,7},{1,0},{2,1},{3,2},{4,3},{5,4},{6,5},{7,6},{8,15},{9,8},{10,9... | collective-permute-start | bytes 393224 | tf_op jit(solution)/shard_map/ppermute | solution.py:321
  64.3 10.5 %collective-permute-start.11 = (bf16[64,2048]{1,0:T(8,128)(2,1)S(1)}, bf16[64,2048]{1,0:T(8,128)(2,1)S(1)}, u32[]{:S(2)}, u32[]{:S(2)}) collective-permute-start(bf16[64,2048]{1,0:T(8,128)(2,1)S(1)} %get-tuple-element.85), channel_id=1, source_target_pairs={{0,1},{1,2},{2,3},{3,4},{4,5},{5,6},{6,7},{7,0},{8,9},{9,10},{10,1... | collective-permute-start | bytes 786440 | tf_op jit(solution)/shard_map/ppermute | solution.py:321
  64.4 10.4 %collective-permute-start.12 = (bf16[64,2048]{1,0:T(8,128)(2,1)S(1)}, bf16[64,2048]{1,0:T(8,128)(2,1)S(1)}, u32[]{:S(2)}, u32[]{:S(2)}) collective-permute-start(bf16[64,2048]{1,0:T(8,128)(2,1)S(1)} %get-tuple-element.86), channel_id=1, source_target_pairs={{0,7},{1,0},{2,1},{3,2},{4,3},{5,4},{6,5},{7,6},{8,15},{9,8},{10,9... | collective-permute-start | bytes 786440 | tf_op jit(solution)/shard_map/ppermute | solution.py:321
  67.7 12.8 %collective-permute-start.3 = (bf16[64,2048]{1,0:T(8,128)(2,1)S(1)}, bf16[64,2048]{1,0:T(8,128)(2,1)S(1)}, u32[]{:S(2)}, u32[]{:S(2)}) collective-permute-start(bf16[64,2048]{1,0:T(8,128)(2,1)S(1)} %get-tuple-element.69), channel_id=1, source_target_pairs={{0,1},{1,2},{2,3},{3,4},{4,5},{5,6},{6,7},{7,0},{8,9},{9,10},{10,1... | collective-permute-start | bytes 786440 | tf_op jit(solution)/shard_map/ppermute | solution.py:321
  67.8 12.7 %collective-permute-start.4 = (bf16[64,2048]{1,0:T(8,128)(2,1)S(1)}, bf16[64,2048]{1,0:T(8,128)(2,1)S(1)}, u32[]{:S(2)}, u32[]{:S(2)}) collective-permute-start(bf16[64,2048]{1,0:T(8,128)(2,1)S(1)} %get-tuple-element.70), channel_id=1, source_target_pairs={{0,7},{1,0},{2,1},{3,2},{4,3},{5,4},{6,5},{7,6},{8,15},{9,8},{10,9... | collective-permute-start | bytes 786440 | tf_op jit(solution)/shard_map/ppermute | solution.py:321
  74.9 11.1 %collective-permute-start.13 = (bf16[64,2048]{1,0:T(8,128)(2,1)S(1)}, bf16[64,2048]{1,0:T(8,128)(2,1)S(1)}, u32[]{:S(2)}, u32[]{:S(2)}) collective-permute-start(bf16[64,2048]{1,0:T(8,128)(2,1)S(1)} %get-tuple-element.89), channel_id=1, source_target_pairs={{0,1},{1,2},{2,3},{3,4},{4,5},{5,6},{6,7},{7,0},{8,9},{9,10},{10,1... | collective-permute-start | bytes 786440 | tf_op jit(solution)/shard_map/ppermute | solution.py:321
  75.0 11.1 %collective-permute-start.14 = (bf16[64,2048]{1,0:T(8,128)(2,1)S(1)}, bf16[64,2048]{1,0:T(8,128)(2,1)S(1)}, u32[]{:S(2)}, u32[]{:S(2)}) collective-permute-start(bf16[64,2048]{1,0:T(8,128)(2,1)S(1)} %get-tuple-element.90), channel_id=1, source_target_pairs={{0,7},{1,0},{2,1},{3,2},{4,3},{5,4},{6,5},{7,6},{8,15},{9,8},{10,9... | collective-permute-start | bytes 786440 | tf_op jit(solution)/shard_map/ppermute | solution.py:321
  80.4 14.7 %copy-start.5 = (s32[4096]{0:T(1024)S(1)}, s32[4096]{0:T(1024)}, u32[]{:S(2)}) copy-start(s32[4096]{0:T(1024)} %param.27) | copy-start | bytes 49156
  80.4 14.7 %copy-start.6 = (s32[4096]{0:T(1024)S(1)}, s32[4096]{0:T(1024)}, u32[]{:S(2)}) copy-start(s32[4096]{0:T(1024)} %param.26) | copy-start | bytes 49156
  80.5 11.1 %collective-permute-start.5 = (bf16[64,2048]{1,0:T(8,128)(2,1)S(1)}, bf16[64,2048]{1,0:T(8,128)(2,1)S(1)}, u32[]{:S(2)}, u32[]{:S(2)}) collective-permute-start(bf16[64,2048]{1,0:T(8,128)(2,1)S(1)} %get-tuple-element.73), channel_id=1, source_target_pairs={{0,1},{1,2},{2,3},{3,4},{4,5},{5,6},{6,7},{7,0},{8,9},{9,10},{10,1... | collective-permute-start | bytes 786440 | tf_op jit(solution)/shard_map/ppermute | solution.py:321
  80.6 11.0 %collective-permute-start.6 = (bf16[64,2048]{1,0:T(8,128)(2,1)S(1)}, bf16[64,2048]{1,0:T(8,128)(2,1)S(1)}, u32[]{:S(2)}, u32[]{:S(2)}) collective-permute-start(bf16[64,2048]{1,0:T(8,128)(2,1)S(1)} %get-tuple-element.74), channel_id=1, source_target_pairs={{0,7},{1,0},{2,1},{3,2},{4,3},{5,4},{6,5},{7,6},{8,15},{9,8},{10,9... | collective-permute-start | bytes 786440 | tf_op jit(solution)/shard_map/ppermute | solution.py:321
  86.1 11.1 %collective-permute-start.15 = (bf16[64,2048]{1,0:T(8,128)(2,1)S(1)}, bf16[64,2048]{1,0:T(8,128)(2,1)S(1)}, u32[]{:S(2)}, u32[]{:S(2)}) collective-permute-start(bf16[64,2048]{1,0:T(8,128)(2,1)S(1)} %get-tuple-element.93), channel_id=1, source_target_pairs={{0,1},{1,2},{2,3},{3,4},{4,5},{5,6},{6,7},{7,0},{8,9},{9,10},{10,1... | collective-permute-start | bytes 786440 | tf_op jit(solution)/shard_map/ppermute | solution.py:321
  86.6 10.6 %collective-permute-start.16 = (bf16[64,2048]{1,0:T(8,128)(2,1)S(1)}, bf16[64,2048]{1,0:T(8,128)(2,1)S(1)}, u32[]{:S(2)}, u32[]{:S(2)}) collective-permute-start(bf16[64,2048]{1,0:T(8,128)(2,1)S(1)} %get-tuple-element.94), channel_id=1, source_target_pairs={{0,7},{1,0},{2,1},{3,2},{4,3},{5,4},{6,5},{7,6},{8,15},{9,8},{10,9... | collective-permute-start | bytes 786440 | tf_op jit(solution)/shard_map/ppermute | solution.py:321
  91.8 9.0 %collective-permute-start.7 = (bf16[64,2048]{1,0:T(8,128)(2,1)S(1)}, bf16[64,2048]{1,0:T(8,128)(2,1)S(1)}, u32[]{:S(2)}, u32[]{:S(2)}) collective-permute-start(bf16[64,2048]{1,0:T(8,128)(2,1)S(1)} %get-tuple-element.77), channel_id=1, source_target_pairs={{0,1},{1,2},{2,3},{3,4},{4,5},{5,6},{6,7},{7,0},{8,9},{9,10},{10,1... | collective-permute-start | bytes 786440 | tf_op jit(solution)/shard_map/ppermute | solution.py:321
  92.3 8.5 %collective-permute-start.8 = (bf16[64,2048]{1,0:T(8,128)(2,1)S(1)}, bf16[64,2048]{1,0:T(8,128)(2,1)S(1)}, u32[]{:S(2)}, u32[]{:S(2)}) collective-permute-start(bf16[64,2048]{1,0:T(8,128)(2,1)S(1)} %get-tuple-element.78), channel_id=1, source_target_pairs={{0,7},{1,0},{2,1},{3,2},{4,3},{5,4},{6,5},{7,6},{8,15},{9,8},{10,9... | collective-permute-start | bytes 786440 | tf_op jit(solution)/shard_map/ppermute | solution.py:321
  (3 other events, 16.2 us)
